TPU v7x, 32 devices: a whole 2x2x4 slice. The times are simulated.
32 devices in a mesh: replica: 4 (over y, x), shard: 8 (over z, core).
Axes of the slice: x: 2, y: 2, z: 4, core: 2. Of those that a mesh axis runs over, the one named last changes fastest.
Arguments:
- hidden_in: float32 [96, 256, 768], P(('replica', 'shard')), may hold values from -1.7 to 1.7
- condition: float32 [96, 768], P(('replica', 'shard')), may hold values from -1.7 to 1.7
- latent_live: int32 [96], P(('replica', 'shard')), may hold values from 0 to 1, as said below
- out_grad: float32 [96, 256, 768], P(('replica', 'shard')), may hold values from -1.7 to 1.7
- ada_weight: float32 [2, 768, 4608], P(None, 'shard'), may hold values from -0.21875 to 0.21875
- qkv_weight: float32 [2, 768, 2304], P(None, 'shard'), may hold values from -0.21875 to 0.21875
- proj_weight: float32 [2, 768, 768], P(None, 'shard'), may hold values from -0.875 to 0.875
- fc1_weight: float32 [2, 768, 3072], P(None, 'shard'), may hold values from -0.21875 to 0.21875
- fc2_weight: float32 [2, 3072, 768], P(None, 'shard'), may hold values from -0.109375 to 0.109375
- ada_bias: float32 [2, 4608], P(None, 'shard'), may hold values from -0.8 to 0.8
- qv_bias: float32 [2, 1536], P(None, 'shard'), may hold values from -0.8 to 0.8
- proj_bias: float32 [2, 768], P(None, 'shard'), may hold values from -0.8 to 0.8
- fc1_bias: float32 [2, 3072], P(None, 'shard'), may hold values from -0.8 to 0.8
- fc2_bias: float32 [2, 768], P(None, 'shard'), may hold values from -0.8 to 0.8
Outputs:
- out_hidden: float32 [96, 256, 768], P(('replica', 'shard'))
- grad_hidden: float32 [96, 256, 768], P(('replica', 'shard'))
- grad_condition: float32 [96, 768], P(('replica', 'shard'))
- grad_ada_weight: float32 [2, 768, 4608], P(None, 'shard')
- grad_qkv_weight: float32 [2, 768, 2304], P(None, 'shard')
- grad_proj_weight: float32 [2, 768, 768], P(None, 'shard')
- grad_fc1_weight: float32 [2, 768, 3072], P(None, 'shard')
- grad_fc2_weight: float32 [2, 3072, 768], P(None, 'shard')
- grad_ada_bias: float32 [2, 4608], P(None, 'shard')
- grad_qv_bias: float32 [2, 1536], P(None, 'shard')
- grad_proj_bias: float32 [2, 768], P(None, 'shard')
- grad_fc1_bias: float32 [2, 3072], P(None, 'shard')
- grad_fc2_bias: float32 [2, 768], P(None, 'shard')
Inputs may be any that keep to these rules, and one draw needn't show every extreme that they name: `latent_live`: slot i holds a latent whenever i is a multiple of 3; the other slots may be empty.
All inputs are finite; a program needn't handle non-finite values.
Results may differ from a plain program's by a relative error of at most 0.013.
The roundings to bfloat16 on the way count: a program that leaves them out, or rounds other values in their place, can miss the bound.
Values may be sent and summed in bfloat16 or wider, within the bound.
No kernel may reach another device: no remote copies, remote signals or barrier semaphores. Data moves between devices by JAX's collectives and lax.ppermute only.
A program may use at most 256 MiB of HBM per device.

v0:
```python
import jax
import jax.numpy as jnp
from jax import lax
from jax.sharding import PartitionSpec as P

HEADS = 12
HEAD_DIM = 64
LAYERS = 2


norm_eps = 1e-06
highest = lax.Precision.HIGHEST


def norm_mod(hidden, offset, stretch):
    average = jnp.mean(hidden, axis=-1, keepdims=True)
    centred = hidden - average
    spread = jnp.mean(centred * centred, axis=-1, keepdims=True)
    normed = centred * lax.rsqrt(spread + norm_eps)
    return normed * (1.0 + stretch[:, None, :]) + offset[:, None, :]


def gelu_tanh(argument):
    return jax.nn.gelu(argument, approximate=True)


def matmul(left_side, right_side):
    return jnp.dot(left_side, right_side, preferred_element_type=jnp.float32)


def dot_lead(left_side, right_side):
    return lax.dot_general(
        left_side, right_side, (((0,), (0,)), ((), ())), preferred_element_type=jnp.float32
    )


def dot_trail(left_side, right_side):
    return lax.dot_general(
        left_side, right_side, (((1,), (1,)), ((), ())), preferred_element_type=jnp.float32
    )


def exact_lead(left_side, right_side):
    return lax.dot_general(
        left_side,
        right_side,
        (((0,), (0,)), ((), ())),
        precision=highest,
        preferred_element_type=jnp.float32,
    )


def exact_trail(left_side, right_side):
    return lax.dot_general(
        left_side,
        right_side,
        (((1,), (1,)), ((), ())),
        precision=highest,
        preferred_element_type=jnp.float32,
    )


def column_sums(values):
    return jnp.sum(values.astype(jnp.float32), axis=0)


def attention_probs(qkv_low):
    latents_here, seq_len, triple_width = qkv_low.shape
    heads_view = qkv_low.reshape(latents_here, seq_len, 3, HEADS, HEAD_DIM)
    queries = heads_view[:, :, 0]
    key_rows = heads_view[:, :, 1]
    value_rows = heads_view[:, :, 2]
    raw_scores = jnp.einsum(
        "bqhd,bkhd->bhqk", queries, key_rows, preferred_element_type=jnp.float32
    )
    attn_probs = jax.nn.softmax(raw_scores * HEAD_DIM ** (-0.5), axis=-1)
    return (attn_probs, queries, key_rows, value_rows)


def gather_forward(shards, layer_index):
    ada_w, qkv_w, proj_w, up_w, down_w, ada_b, qv_b, proj_b, up_b, down_b = [
        weight_piece[layer_index].astype(jnp.bfloat16) for weight_piece in shards
    ]
    return (
        lax.all_gather(ada_w, "shard", axis=0, tiled=True),
        lax.all_gather(qkv_w, "shard", axis=0, tiled=True),
        lax.all_gather(proj_w, "shard", axis=0, tiled=True),
        lax.all_gather(up_w, "shard", axis=0, tiled=True),
        lax.all_gather(down_w, "shard", axis=0, tiled=True),
        lax.all_gather(ada_b, "shard", axis=0, tiled=True),
        lax.all_gather(qv_b, "shard", axis=0, tiled=True),
        lax.all_gather(proj_b, "shard", axis=0, tiled=True),
        lax.all_gather(up_b, "shard", axis=0, tiled=True),
        lax.all_gather(down_b, "shard", axis=0, tiled=True),
    )


def gather_backward(shards, layer_index):
    ada_w, qkv_w, proj_w, up_w, down_w, ada_b, qv_b, proj_b, up_b, down_b = [
        weight_piece[layer_index].astype(jnp.bfloat16) for weight_piece in shards
    ]
    return (
        lax.all_gather(ada_w, "shard", axis=0, tiled=True),
        lax.all_gather(qkv_w, "shard", axis=0, tiled=True),
        lax.all_gather(proj_w, "shard", axis=0, tiled=True),
        lax.all_gather(up_w, "shard", axis=0, tiled=True),
        lax.all_gather(down_w, "shard", axis=0, tiled=True),
        lax.all_gather(ada_b, "shard", axis=0, tiled=True),
        lax.all_gather(qv_b, "shard", axis=0, tiled=True),
        lax.all_gather(proj_b, "shard", axis=0, tiled=True),
        lax.all_gather(up_b, "shard", axis=0, tiled=True),
        lax.all_gather(down_b, "shard", axis=0, tiled=True),
    )


def scatter_grads(local_grads):
    ga_w, gq_w, gp_w, gu_w, gd_w, ga_b, gq_b, gp_b, gu_b, gd_b = local_grads
    return (
        lax.psum_scatter(ga_w, "shard", scatter_dimension=0, tiled=True),
        lax.psum_scatter(gq_w, "shard", scatter_dimension=0, tiled=True),
        lax.psum_scatter(gp_w, "shard", scatter_dimension=0, tiled=True),
        lax.psum_scatter(gu_w, "shard", scatter_dimension=0, tiled=True),
        lax.psum_scatter(gd_w, "shard", scatter_dimension=0, tiled=True),
        lax.psum_scatter(ga_b, "shard", scatter_dimension=0, tiled=True),
        lax.psum_scatter(gq_b, "shard", scatter_dimension=0, tiled=True),
        lax.psum_scatter(gp_b, "shard", scatter_dimension=0, tiled=True),
        lax.psum_scatter(gu_b, "shard", scatter_dimension=0, tiled=True),
        lax.psum_scatter(gd_b, "shard", scatter_dimension=0, tiled=True),
    )


def sum_replicas(owned_layer):
    ga_w, gq_w, gp_w, gu_w, gd_w, ga_b, gq_b, gp_b, gu_b, gd_b = owned_layer
    return lax.psum((ga_w, gq_w, gp_w, gu_w, gd_w, ga_b, gq_b, gp_b, gu_b, gd_b), "replica")


def forward_layer(hidden, cond_low, weights):
    ada_w, qkv_w, proj_w, up_w, down_w, ada_b, qv_b, proj_b, up_b, down_b = weights
    latents_here, seq_len, model_width = hidden.shape
    row_count = latents_here * seq_len
    modulation = matmul(cond_low, ada_w) + ada_b.astype(jnp.float32)
    offset_one, stretch_one, gate_one, offset_two, stretch_two, gate_two = jnp.split(
        modulation, 6, axis=-1
    )
    normed_one = norm_mod(hidden, offset_one, stretch_one).astype(jnp.bfloat16)
    bias_full = jnp.concatenate(
        [qv_b[:model_width], jnp.zeros((model_width,), jnp.bfloat16), qv_b[model_width:]]
    ).astype(jnp.float32)
    qkv_low = (matmul(normed_one.reshape(row_count, model_width), qkv_w) + bias_full).astype(
        jnp.bfloat16
    )
    attn_probs, queries, key_rows, value_rows = attention_probs(
        qkv_low.reshape(latents_here, seq_len, 3 * model_width)
    )
    mixed_heads = jnp.einsum(
        "bhqk,bkhd->bqhd",
        attn_probs.astype(jnp.bfloat16),
        value_rows,
        preferred_element_type=jnp.float32,
    )
    mixed_low = mixed_heads.reshape(row_count, model_width).astype(jnp.bfloat16)
    branch_one = (matmul(mixed_low, proj_w) + proj_b.astype(jnp.float32)).reshape(
        latents_here, seq_len, model_width
    )
    middle = hidden + gate_one[:, None, :] * branch_one
    normed_two = norm_mod(middle, offset_two, stretch_two).astype(jnp.bfloat16)
    pre_act = matmul(normed_two.reshape(row_count, model_width), up_w) + up_b.astype(jnp.float32)
    act_low = gelu_tanh(pre_act).astype(jnp.bfloat16)
    branch_two = (matmul(act_low, down_w) + down_b.astype(jnp.float32)).reshape(
        latents_here, seq_len, model_width
    )
    result = middle + gate_two[:, None, :] * branch_two
    saved_state = (
        hidden,
        modulation,
        normed_one,
        qkv_low,
        mixed_low,
        branch_one,
        middle,
        normed_two,
        pre_act,
        act_low,
        branch_two,
    )
    return (result, saved_state)


def backward_layer(grad_out, weights, saved_state):
    ada_w, qkv_w, proj_w, up_w, down_w, ada_b, qv_b, proj_b, up_b, down_b = weights
    (
        hidden,
        modulation,
        normed_one,
        qkv_low,
        mixed_low,
        branch_one,
        middle,
        normed_two,
        pre_act,
        act_low,
        branch_two,
    ) = saved_state
    latents_here, seq_len, model_width = hidden.shape
    row_count = latents_here * seq_len
    offset_one, stretch_one, gate_one, offset_two, stretch_two, gate_two = jnp.split(
        modulation, 6, axis=-1
    )
    grad_gate_two = jnp.sum(grad_out * branch_two, axis=1)
    grad_branch_two = (
        (grad_out * gate_two[:, None, :]).reshape(row_count, model_width).astype(jnp.bfloat16)
    )
    grad_down_w = dot_lead(act_low, grad_branch_two)
    grad_down_b = column_sums(grad_branch_two)
    grad_act = dot_trail(grad_branch_two, down_w)
    grad_pre = jax.vjp(gelu_tanh, pre_act)[1](grad_act)[0].astype(jnp.bfloat16)
    grad_up_w = dot_lead(normed_two.reshape(row_count, model_width), grad_pre)
    grad_up_b = column_sums(grad_pre)
    grad_normed_two = dot_trail(grad_pre, up_w).reshape(latents_here, seq_len, model_width)
    grad_middle, grad_offset_two, grad_stretch_two = jax.vjp(
        norm_mod, middle, offset_two, stretch_two
    )[1](grad_normed_two)
    grad_middle = grad_middle + grad_out
    grad_gate_one = jnp.sum(grad_middle * branch_one, axis=1)
    grad_branch_one = (
        (grad_middle * gate_one[:, None, :]).reshape(row_count, model_width).astype(jnp.bfloat16)
    )
    grad_proj_w = dot_lead(mixed_low, grad_branch_one)
    grad_proj_b = column_sums(grad_branch_one)
    grad_mixed = (
        dot_trail(grad_branch_one, proj_w)
        .astype(jnp.bfloat16)
        .reshape(latents_here, seq_len, HEADS, HEAD_DIM)
    )
    attn_probs, queries, key_rows, value_rows = attention_probs(
        qkv_low.reshape(latents_here, seq_len, 3 * model_width)
    )
    grad_values = jnp.einsum(
        "bhqk,bqhd->bkhd",
        attn_probs.astype(jnp.bfloat16),
        grad_mixed,
        preferred_element_type=jnp.float32,
    )
    grad_probs = jnp.einsum(
        "bqhd,bkhd->bhqk", grad_mixed, value_rows, preferred_element_type=jnp.float32
    )
    row_dots = jnp.sum(grad_probs * attn_probs, axis=-1, keepdims=True)
    grad_raw = (attn_probs * (grad_probs - row_dots) * HEAD_DIM ** (-0.5)).astype(jnp.bfloat16)
    grad_queries = jnp.einsum(
        "bhqk,bkhd->bqhd", grad_raw, key_rows, preferred_element_type=jnp.float32
    )
    grad_keys = jnp.einsum("bhqk,bqhd->bkhd", grad_raw, queries, preferred_element_type=jnp.float32)
    grad_qkv = (
        jnp.stack([grad_queries, grad_keys, grad_values], axis=2)
        .reshape(row_count, 3 * model_width)
        .astype(jnp.bfloat16)
    )
    grad_qkv_w = dot_lead(normed_one.reshape(row_count, model_width), grad_qkv)
    qkv_sums = column_sums(grad_qkv)
    grad_qv_b = jnp.concatenate([qkv_sums[:model_width], qkv_sums[2 * model_width :]])
    grad_normed_one = dot_trail(grad_qkv, qkv_w).reshape(latents_here, seq_len, model_width)
    grad_hidden, grad_offset_one, grad_stretch_one = jax.vjp(
        norm_mod, hidden, offset_one, stretch_one
    )[1](grad_normed_one)
    grad_hidden = grad_hidden + grad_middle
    grad_modul = jnp.concatenate(
        [
            grad_offset_one,
            grad_stretch_one,
            grad_gate_one,
            grad_offset_two,
            grad_stretch_two,
            grad_gate_two,
        ],
        axis=-1,
    )
    grad_cond = exact_trail(grad_modul, ada_w.astype(jnp.float32))
    rest_grads = (
        grad_qkv_w,
        grad_proj_w,
        grad_up_w,
        grad_down_w,
        grad_qv_b,
        grad_proj_b,
        grad_up_b,
        grad_down_b,
    )
    return (grad_hidden, grad_cond, grad_modul, rest_grads)


def local(
    hidden_in,
    condition,
    latent_live,
    out_grad,
    ada_weight,
    qkv_weight,
    proj_weight,
    fc1_weight,
    fc2_weight,
    ada_bias,
    qv_bias,
    proj_bias,
    fc1_bias,
    fc2_bias,
):
    shards = (
        ada_weight,
        qkv_weight,
        proj_weight,
        fc1_weight,
        fc2_weight,
        ada_bias,
        qv_bias,
        proj_bias,
        fc1_bias,
        fc2_bias,
    )
    cond_low = jax.nn.silu(condition).astype(jnp.bfloat16)
    cond_wide = cond_low.astype(jnp.float32)
    live_rows = latent_live.astype(jnp.float32)[:, None, None]
    saved_all = []
    current = hidden_in
    for layer_index in range(LAYERS):
        weights = gather_forward(shards, layer_index)
        current, saved_state = forward_layer(current, cond_low, weights)
        saved_all.append(saved_state)
    result = current * live_rows
    grad_now = out_grad * live_rows
    grad_cond = jnp.zeros(condition.shape, jnp.float32)
    owned_grads = [None] * LAYERS
    for layer_index in reversed(range(LAYERS)):
        weights = gather_backward(shards, layer_index)
        grad_now, grad_extra, grad_modul, rest_grads = backward_layer(
            grad_now, weights, saved_all[layer_index]
        )
        grad_cond = grad_cond + grad_extra
        local_grads = (
            exact_lead(cond_wide, grad_modul),
            rest_grads[0],
            rest_grads[1],
            rest_grads[2],
            rest_grads[3],
            column_sums(grad_modul),
            rest_grads[4],
            rest_grads[5],
            rest_grads[6],
            rest_grads[7],
        )
        owned_grads[layer_index] = scatter_grads(local_grads)
        owned_grads[layer_index] = sum_replicas(owned_grads[layer_index])
    grad_condition = jax.vjp(jax.nn.silu, condition)[1](grad_cond)[0]
    stacked = [
        jnp.stack([owned_grads[layer_index][member] for layer_index in range(LAYERS)])
        for member in range(10)
    ]
    return (
        result,
        grad_now,
        grad_condition,
        stacked[0],
        stacked[1],
        stacked[2],
        stacked[3],
        stacked[4],
        stacked[5],
        stacked[6],
        stacked[7],
        stacked[8],
        stacked[9],
    )


def solution(mesh):
    placed = (
        P(("replica", "shard"), None, None),
        P(("replica", "shard"), None),
        P(("replica", "shard")),
        P(("replica", "shard"), None, None),
        P(None, "shard", None),
        P(None, "shard", None),
        P(None, "shard", None),
        P(None, "shard", None),
        P(None, "shard", None),
        P(None, "shard"),
        P(None, "shard"),
        P(None, "shard"),
        P(None, "shard"),
        P(None, "shard"),
    )
    return jax.shard_map(
        local,
        mesh=mesh,
        in_specs=placed,
        out_specs=(
            P(("replica", "shard"), None, None),
            P(("replica", "shard"), None, None),
            P(("replica", "shard"), None),
            P(None, "shard", None),
            P(None, "shard", None),
            P(None, "shard", None),
            P(None, "shard", None),
            P(None, "shard", None),
            P(None, "shard"),
            P(None, "shard"),
            P(None, "shard"),
            P(None, "shard"),
            P(None, "shard"),
        ),
        check_vma=False,
    )
```

profile of v0, /device:TPU:0, one launch (start us, length us, event | category | flops | bytes accessed | tf_op | source)
XLA Modules:
  0.0 1817.7 jit_solution(10864552406709867987)
XLA Ops:
  25.2 32.4 %all-reduce.21 = (bf16[4608]{0:T(1024)(128)(2,1)S(1)}, bf16[1536]{0:T(1024)(128)(2,1)S(1)}, bf16[768]{0:T(1024)(128)(2,1)S(1)}, bf16[768]{0:T(1024)(128)(2,1)S(1...) all-reduce(bf16[4608]{0:T(1024)(128)(2,1)S(1)} %dynamic-update-slic, ...), channel_id=3, replica_groups=mesh['replica'=4,'shard'=8] {'shard'}, use_global_device_ids=true, to_apply=%add | all-reduce | flops 15360 | bytes 61440
  58.9 12.9 all-gather.7
  74.1 13.4 all-gather.17
  95.8 32.7 %all-gather.33.cloned.1.call-done = bf16[1,768,2304]{2,1,0:T(8,128)(2,1)} async-done(((bf16[1,96,2304]{2,1,0:T(8,128)(2,1)}), bf16[1,768,2304]{2,1,0:T(8,128)(2,1)}) %all-gather.33.cloned.1.call-update) | async-done | bytes 3538960 | tf_op jit(solution)/shard_map/all_gather | solution.py:86
  133.8 9.0 reshape.429
  142.7 6.4 fusion.209
  161.2 9.0 fusion.221
  182.3 23.0 %all-gather.37.cloned.1.call-done = bf16[1,768,3072]{2,1,0:T(8,128)(2,1)} async-done(((bf16[1,96,3072]{2,1,0:T(8,128)(2,1)}), bf16[1,768,3072]{2,1,0:T(8,128)(2,1)}) %all-gather.37.cloned.1.call-update) | async-done | bytes 4718608 | tf_op jit(solution)/shard_map/all_gather | solution.py:88
  205.3 8.9 fusion.74
  214.2 43.7 %all-gather.39.cloned.1.call-done = bf16[1,3072,768]{2,1,0:T(8,128)(2,1)} async-done(((bf16[1,384,768]{2,1,0:T(8,128)(2,1)}), bf16[1,3072,768]{2,1,0:T(8,128)(2,1)}) %all-gather.39.cloned.1.call-update) | async-done | bytes 4718608 | tf_op jit(solution)/shard_map/all_gather | solution.py:89
  257.9 9.8 fusion.118
  271.5 58.6 %all-gather.41.cloned.1.call-done = bf16[1,768,4608]{2,1,0:T(8,128)(2,1)} async-done(((bf16[1,96,4608]{2,1,0:T(8,128)(2,1)}), bf16[1,768,4608]{2,1,0:T(8,128)(2,1)}) %all-gather.41.cloned.1.call-update) | async-done | bytes 7077904 | tf_op jit(solution)/shard_map/all_gather | solution.py:85
  336.1 35.7 %all-gather.43.cloned.1.call-done = bf16[1,768,2304]{2,1,0:T(8,128)(2,1)} async-done(((bf16[1,96,2304]{2,1,0:T(8,128)(2,1)}), bf16[1,768,2304]{2,1,0:T(8,128)(2,1)}) %all-gather.43.cloned.1.call-update) | async-done | bytes 3538960 | tf_op jit(solution)/shard_map/all_gather | solution.py:86
  371.9 6.3 add_convert_fusion
  378.2 11.5 reshape.430
  389.7 6.9 fusion.208
  409.7 9.1 fusion.230
  436.4 12.4 all-gather.47.cloned.1.call-done
  448.8 10.4 fusion.66
  459.2 42.2 %all-gather.49.cloned.1.call-done = bf16[1,3072,768]{2,1,0:T(8,128)(2,1)} async-done(((bf16[1,384,768]{2,1,0:T(8,128)(2,1)}), bf16[1,3072,768]{2,1,0:T(8,128)(2,1)}) %all-gather.49.cloned.1.call-update) | async-done | bytes 4718608 | tf_op jit(solution)/shard_map/all_gather | solution.py:89
  501.4 13.6 convert_reduce_fusion
  522.0 5.8 fusion.121
  544.7 6.4 fusion.151
  551.0 16.1 fusion.112
  567.2 16.1 fusion.115
  583.3 6.4 fusion.103
  608.8 12.9 convert_reduce_fusion.1
  655.5 6.9 fusion.169
  662.4 14.8 fusion.106
  677.2 15.4 fusion.109
  710.4 8.7 fusion.244
  720.4 13.2 fusion.203
  735.0 8.6 fusion.243
  744.9 13.1 fusion.204
  769.9 8.9 fusion.202
  779.7 9.0 fusion.201
  792.0 41.7 %reduce-scatter.15.cloned.1.call-done = f32[96,2304]{1,0:T(8,128)} async-done(((f32[768,2304]{1,0:T(8,128)}), f32[96,2304]{1,0:T(8,128)}) %reduce-scatter.15.cloned.1.call-update) | async-done | bytes 884752 | tf_op jit(solution)/shard_map/reduce_scatter | solution.py:120
  833.7 100.0 %reduce-scatter.25.cloned.1.call-done = f32[96,3072]{1,0:T(8,128)} async-done(((f32[768,3072]{1,0:T(8,128)}), f32[96,3072]{1,0:T(8,128)}) %reduce-scatter.25.cloned.1.call-update) | async-done | bytes 1179664 | tf_op jit(solution)/shard_map/reduce_scatter | solution.py:122
  933.7 100.1 %reduce-scatter.27.cloned.1.call-done = f32[384,768]{1,0:T(8,128)} async-done(((f32[3072,768]{1,0:T(8,128)}), f32[384,768]{1,0:T(8,128)}) %reduce-scatter.27.cloned.1.call-update) | async-done | bytes 1179664 | tf_op jit(solution)/shard_map/reduce_scatter | solution.py:123
  1033.8 100.1 %reduce-scatter.23.cloned.1.call-done = f32[96,3072]{1,0:T(8,128)} async-done(((f32[768,3072]{1,0:T(8,128)}), f32[96,3072]{1,0:T(8,128)}) %reduce-scatter.23.cloned.1.call-update) | async-done | bytes 1179664 | tf_op jit(solution)/shard_map/reduce_scatter | solution.py:122
  1133.8 100.1 %reduce-scatter.29.cloned.1.call-done = f32[384,768]{1,0:T(8,128)} async-done(((f32[3072,768]{1,0:T(8,128)}), f32[384,768]{1,0:T(8,128)}) %reduce-scatter.29.cloned.1.call-update) | async-done | bytes 1179664 | tf_op jit(solution)/shard_map/reduce_scatter | solution.py:123
  1233.9 144.7 %reduce-scatter.11.cloned.1.call-done = f32[96,4608]{1,0:T(8,128)} async-done(((f32[768,4608]{1,0:T(8,128)}), f32[96,4608]{1,0:T(8,128)}) %reduce-scatter.11.cloned.1.call-update) | async-done | bytes 1769488 | tf_op jit(solution)/shard_map/reduce_scatter | solution.py:119
  1378.6 144.6 %reduce-scatter.13.cloned.1.call-done = f32[96,4608]{1,0:T(8,128)} async-done(((f32[768,4608]{1,0:T(8,128)}), f32[96,4608]{1,0:T(8,128)}) %reduce-scatter.13.cloned.1.call-update) | async-done | bytes 1769488 | tf_op jit(solution)/shard_map/reduce_scatter | solution.py:119
  1525.9 7.7 fusion.22
  1533.6 8.4 fusion.180
  1542.0 37.1 %all-reduce.25.cloned.1.call-done = (f32[4608]{0:T(1024)}, f32[4608]{0:T(1024)}, f32[1536]{0:T(1024)}, f32[1536]{0:T(1024)}, f32[768]{0:T(1024)}, /*index=5*/f32...) async-done(((f32[4608]{0:T(1024)}, f32[4608]{0:T(1024)}, f32[1536]{0:T(1024)}, f32[1536]{0:T(1024)}, f32[768]{0:T(1024)}, ...) | async-done | bytes 86032
  1586.8 16.4 all-reduce.19
  1606.0 194.4 %all-reduce.27.cloned.1.call-done = (f32[1,96,4608]{2,1,0:T(8,128)}, f32[1,96,4608]{2,1,0:T(8,128)}, f32[1,96,2304]{2,1,0:T(8,128)}, f32[1,96,2304]{2,1,0:T(8,12...) async-done(((f32[1,96,4608]{2,1,0:T(8,128)}, ...) | async-done | bytes 10616848 | tf_op jit(solution)/shard_map/psum | solution.py:134
  (504 shorter events, 231.3 us)
Async XLA Ops:
  7.2 82.2 %all-gather.31.cloned.1.call-start = ((), (), s32[]{:S(2)}) async-start(), calls=%async_computation.20 | async-start | bytes 7962624 | tf_op jit(solution)/shard_map/all_gather | solution.py:85
  10.8 117.7 %all-gather.33.cloned.1.call-start = ((), (), s32[]{:S(2)}) async-start(), calls=%async_computation.21 | async-start | bytes 3981312 | tf_op jit(solution)/shard_map/all_gather | solution.py:86
  12.6 163.7 %all-gather.35.cloned.1.call-start = ((), (), s32[]{:S(2)}) async-start(), calls=%async_computation.22 | async-start | bytes 1327104 | tf_op jit(solution)/shard_map/all_gather | solution.py:87
  13.5 191.8 %all-gather.37.cloned.1.call-start = ((), (), s32[]{:S(2)}) async-start(), calls=%async_computation.23 | async-start | bytes 5308416 | tf_op jit(solution)/shard_map/all_gather | solution.py:88
  14.9 243.0 %all-gather.39.cloned.1.call-start = ((), (), s32[]{:S(2)}) async-start(), calls=%async_computation.24 | async-start | bytes 5308416 | tf_op jit(solution)/shard_map/all_gather | solution.py:89
  16.1 7.3 copy-start.121
  16.1 41.5 %copy-start.2 = (f32[3,256,768]{2,1,0:T(8,128)S(1)}, f32[3,256,768]{2,1,0:T(8,128)}, u32[]{:S(2)}) copy-start(f32[3,256,768]{2,1,0:T(8,128)} %param.14) | copy-start | bytes 7077892
  17.2 312.9 %all-gather.41.cloned.1.call-start = ((), (), s32[]{:S(2)}) async-start(), calls=%async_computation.25 | async-start | bytes 7962624 | tf_op jit(solution)/shard_map/all_gather | solution.py:85
  17.8 354.1 %all-gather.43.cloned.1.call-start = ((), (), s32[]{:S(2)}) async-start(), calls=%async_computation.26 | async-start | bytes 3981312 | tf_op jit(solution)/shard_map/all_gather | solution.py:86
  18.5 407.3 %all-gather.45.cloned.1.call-start = ((), (), s32[]{:S(2)}) async-start(), calls=%async_computation.27 | async-start | bytes 1327104 | tf_op jit(solution)/shard_map/all_gather | solution.py:87
  19.3 429.5 %all-gather.47.cloned.1.call-start = ((), (), s32[]{:S(2)}) async-start(), calls=%async_computation.28 | async-start | bytes 5308416 | tf_op jit(solution)/shard_map/all_gather | solution.py:88
  20.0 481.4 %all-gather.49.cloned.1.call-start = ((), (), s32[]{:S(2)}) async-start(), calls=%async_computation.29 | async-start | bytes 5308416 | tf_op jit(solution)/shard_map/all_gather | solution.py:89
  20.6 771.3 %reduce-scatter.21.cloned.1.call-start = ((), (), s32[]{:S(2)}) async-start(), calls=%async_computation.15 | async-start | bytes 2654208 | tf_op jit(solution)/shard_map/reduce_scatter | solution.py:121
  57.6 16.0 copy-start.130
  57.6 31.8 %copy-start.56 = (f32[3,768]{1,0:T(4,128)S(1)}, f32[3,768]{1,0:T(4,128)}, u32[]{:S(2)}) copy-start(f32[3,768]{1,0:T(4,128)} %param.15) | copy-start | bytes 27652
  57.8 36.2 %copy-start.76 = (f32[3,256]{1,0:T(4,128)}, f32[3,256]{1,0:T(4,128)S(1)}, u32[]{:S(2)}) copy-start(f32[3,256]{1,0:T(4,128)S(1)} %broadcast_multiply_fusion.3) | copy-start | bytes 9220
  58.2 35.8 %copy-start.83 = (f32[3,256]{1,0:T(4,128)}, f32[3,256]{1,0:T(4,128)S(1)}, u32[]{:S(2)}) copy-start(f32[3,256]{1,0:T(4,128)S(1)} %fusion.187) | copy-start | bytes 9220
  94.0 34.5 %copy-start.62 = (f32[3,768]{1,0:T(4,128)}, f32[3,768]{1,0:T(4,128)S(1)}, u32[]{:S(2)}) copy-start(f32[3,768]{1,0:T(4,128)S(1)} %get-tuple-element.124) | copy-start | bytes 27652
  161.2 9.0 copy-start.21
  180.6 87.2 %copy-start = (f32[3,256,768]{2,1,0:T(8,128)}, f32[3,256,768]{2,1,0:T(8,128)S(1)}, u32[]{:S(2)}) copy-start(f32[3,256,768]{2,1,0:T(8,128)S(1)} %get-tuple-element.91) | copy-start | bytes 7077892
  182.3 31.9 %copy-start.26 = (bf16[3,256,768]{2,1,0:T(8,128)(2,1)}, bf16[3,256,768]{2,1,0:T(8,128)(2,1)S(1)}, u32[]{:S(2)}) copy-start(bf16[3,256,768]{2,1,0:T(8,128)(2,1)S(1)} %add_convert_fusion.4) | copy-start | bytes 3538948
  257.9 9.8 copy-start.70
  269.1 61.0 %copy-start.80 = (f32[4608]{0:T(1024)S(1)}, f32[4608]{0:T(1024)}, u32[]{:S(2)}) copy-start(f32[4608]{0:T(1024)} %convert_element_type.390) | copy-start | bytes 55300
  269.1 65.7 %copy-start.78 = (f32[3,256]{1,0:T(4,128)}, f32[3,256]{1,0:T(4,128)S(1)}, u32[]{:S(2)}) copy-start(f32[3,256]{1,0:T(4,128)S(1)} %broadcast_multiply_fusion.1) | copy-start | bytes 9220
  270.9 63.2 %copy-start.105 = (f32[3,256]{1,0:T(4,128)}, f32[3,256]{1,0:T(4,128)S(1)}, u32[]{:S(2)}) copy-start(f32[3,256]{1,0:T(4,128)S(1)} %multiply_reduce_fusion.17) | copy-start | bytes 9220
  271.5 63.8 %copy-start.6 = (f32[3,256,768]{2,1,0:T(8,128)S(1)}, f32[3,256,768]{2,1,0:T(8,128)}, u32[]{:S(2)}) copy-start(f32[3,256,768]{2,1,0:T(8,128)} %copy-done.5) | copy-start | bytes 7077892
  336.1 42.1 %copy-start.37 = (bf16[3,256,768]{2,1,0:T(8,128)(2,1)}, bf16[3,256,768]{2,1,0:T(8,128)(2,1)S(1)}, u32[]{:S(2)}) copy-start(bf16[3,256,768]{2,1,0:T(8,128)(2,1)S(1)} %add_convert_fusion.3) | copy-start | bytes 3538948
  501.4 13.7 copy-start.123
  501.4 20.5 %slice-start.2 = ((s8[9437184]{0:T(1024)(128)(4,1)}), s8[4194304]{0:T(1024)(128)(4,1)S(1)}, s32[]{:S(2)}) async-start(s8[9437184]{0:T(1024)(128)(4,1)} %bitcast.337), calls=%async_computation.34 | async-start | bytes 8388608
  501.4 20.5 %slice-start.3 = ((s8[9437184]{0:T(1024)(128)(4,1)}), s8[4194304]{0:T(1024)(128)(4,1)S(1)}, s32[]{:S(2)}) async-start(s8[9437184]{0:T(1024)(128)(4,1)} %bitcast.337), calls=%async_computation.35 | async-start | bytes 8388608
  567.1 16.1 copy-start.22
  603.6 188.3 %reduce-scatter.19.cloned.1.call-start = ((), (), s32[]{:S(2)}) async-start(), calls=%async_computation.14 | async-start | bytes 2654208 | tf_op jit(solution)/shard_map/reduce_scatter | solution.py:121
  604.3 17.4 slice-start
  608.8 12.9 copy-start.46
  608.8 12.9 slice-start.1
  635.1 156.8 %reduce-scatter.17.cloned.1.call-start = ((), (), s32[]{:S(2)}) async-start(), calls=%async_computation.13 | async-start | bytes 7962624 | tf_op jit(solution)/shard_map/reduce_scatter | solution.py:120
  645.1 188.6 %reduce-scatter.15.cloned.1.call-start = ((), (), s32[]{:S(2)}) async-start(), calls=%async_computation.12 | async-start | bytes 7962624 | tf_op jit(solution)/shard_map/reduce_scatter | solution.py:120
  655.5 6.9 copy-start.40
  662.4 14.8 copy-start.39
  677.1 15.4 copy-start.23
  709.2 224.5 %reduce-scatter.25.cloned.1.call-start = ((), (), s32[]{:S(2)}) async-start(), calls=%async_computation.17 | async-start | bytes 10616832 | tf_op jit(solution)/shard_map/reduce_scatter | solution.py:122
  719.2 314.6 %reduce-scatter.27.cloned.1.call-start = ((), (), s32[]{:S(2)}) async-start(), calls=%async_computation.18 | async-start | bytes 10616832 | tf_op jit(solution)/shard_map/reduce_scatter | solution.py:123
  733.7 400.1 %reduce-scatter.23.cloned.1.call-start = ((), (), s32[]{:S(2)}) async-start(), calls=%async_computation.16 | async-start | bytes 10616832 | tf_op jit(solution)/shard_map/reduce_scatter | solution.py:122
  743.6 490.3 %reduce-scatter.29.cloned.1.call-start = ((), (), s32[]{:S(2)}) async-start(), calls=%async_computation.19 | async-start | bytes 10616832 | tf_op jit(solution)/shard_map/reduce_scatter | solution.py:123
  758.0 620.6 %reduce-scatter.11.cloned.1.call-start = ((), (), s32[]{:S(2)}) async-start(), calls=%async_computation.10 | async-start | bytes 15925248 | tf_op jit(solution)/shard_map/reduce_scatter | solution.py:119
  779.0 744.3 %reduce-scatter.13.cloned.1.call-start = ((), (), s32[]{:S(2)}) async-start(), calls=%async_computation.11 | async-start | bytes 15925248 | tf_op jit(solution)/shard_map/reduce_scatter | solution.py:119
  788.7 790.4 %all-reduce.25.cloned.1.call-start = ((), (), s32[]{:S(2)}) async-start(), calls=%async_computation.30 | async-start | bytes 196608
  791.6 1008.8 %all-reduce.27.cloned.1.call-start = ((), (), s32[]{:S(2)}) async-start(), calls=%async_computation.31 | async-start | bytes 21233664 | tf_op jit(solution)/shard_map/psum | solution.py:134
  (111 other events, 288.9 us)
Sparse Core Ops, SparseCore 0:
  10.9 75.1 all-gather.30
  88.3 40.1 all-gather.32
  130.1 21.5 all-gather.34
  153.8 51.4 all-gather.36
  207.4 50.5 all-gather.38
  260.0 70.0 all-gather.40
  331.7 40.0 all-gather.42
  373.5 21.5 all-gather.44
  397.3 51.4 all-gather.46
  450.9 50.5 all-gather.48
  603.7 35.0 reduce-scatter.20
  641.5 35.5 reduce-scatter.18
  679.4 76.4 reduce-scatter.16
  758.1 75.5 reduce-scatter.14
  835.8 97.8 reduce-scatter.24
  935.9 97.8 reduce-scatter.26
  1035.9 97.8 reduce-scatter.22
  1136.0 97.8 reduce-scatter.28
  1236.2 142.4 reduce-scatter.10
  1380.8 142.4 reduce-scatter.12
  1527.6 51.4 all-reduce.24
  1585.5 214.9 all-reduce.26
where the time goes:
time: 1830 us; the launch traced here: 1820 us
  waiting for transfers between devices  1210 us (66%)
  matrix products  313 us (17%)
  local copies, waits for them, and re-layouts  132 us (7%)
  blocking collectives  75.1 us (4%)
  other arithmetic  60.1 us (3%)
  between operations  20.8 us (1%)
    reduce_scatter x2, waiting for transfers between devices, scatter_grads(): lax.psum_scatter(ga_w, 'shard', scatter_dimension=0, tiled=True)  289 us
    reduce_scatter x2, waiting for transfers between devices, scatter_grads(): lax.psum_scatter(gd_w, 'shard', scatter_dimension=0, tiled=True)  200 us
    reduce_scatter x2, waiting for transfers between devices, scatter_grads(): lax.psum_scatter(gu_w, 'shard', scatter_dimension=0, tiled=True)  200 us
    psum x1, waiting for transfers between devices, sum_replicas(): lax.psum((ga_w, gq_w, gp_w, gu_w, gd_w, ga_b, gq_b, gp_b, gu_b, gd_b), 'r...  194 us
    all_gather x2, waiting for transfers between devices, gather_forward(): lax.all_gather(down_w, 'shard', axis=0, tiled=True)  85.9 us
    all_gather x2, waiting for transfers between devices, gather_forward(): lax.all_gather(qkv_w, 'shard', axis=0, tiled=True)  68.4 us
    unnamed x317, local copies, waits for them, and re-layouts  61.5 us
    dot_general x10, matrix products, matmul(): return jnp.dot(left_side, right_side, preferred_element_type=jnp.float32)  60.2 us
  transfers between devices with their start and end apart: 22, of which 16 were waited for; matrix products, arithmetic and copies ran while one was open for 20% of the time, Pallas kernels for 0%

commit v1 on v0

v1 whole, which is shorter than its diff:
```python
import functools

import jax
import jax.numpy as jnp
from jax import lax
from jax.experimental import pallas as pl
from jax.experimental.pallas import tpu as pltpu
from jax.sharding import PartitionSpec as P

HEADS = 12
HEAD_DIM = 64
LAYERS = 2
SLABS = 4

norm_eps = 1e-06
highest = lax.Precision.HIGHEST
low_type = jnp.bfloat16
wide = jnp.float32


def nn(left, right):
    return lax.dot_general(left, right, (((1,), (0,)), ((), ())), preferred_element_type=wide)


def nt(left, right):
    return lax.dot_general(left, right, (((1,), (1,)), ((), ())), preferred_element_type=wide)


def tn(left, right):
    return lax.dot_general(left, right, (((0,), (0,)), ((), ())), preferred_element_type=wide)


def exact_lead(left_side, right_side):
    return lax.dot_general(
        left_side,
        right_side,
        (((0,), (0,)), ((), ())),
        precision=highest,
        preferred_element_type=wide,
    )


def exact_trail(left_side, right_side):
    return lax.dot_general(
        left_side,
        right_side,
        (((1,), (1,)), ((), ())),
        precision=highest,
        preferred_element_type=wide,
    )


def normalise(rows):
    centred = rows - jnp.mean(rows, axis=-1, keepdims=True)
    spread = jnp.mean(centred * centred, axis=-1, keepdims=True)
    inverse = lax.rsqrt(spread + norm_eps)
    return centred * inverse, inverse


def norm_back(grad, rows, stretch):
    normed, inverse = normalise(rows)
    inner = grad * (1.0 + stretch)
    first = jnp.mean(inner, axis=-1, keepdims=True)
    second = jnp.mean(inner * normed, axis=-1, keepdims=True)
    back = (inner - first - normed * second) * inverse
    return (
        back,
        jnp.sum(grad, axis=0, keepdims=True),
        jnp.sum(grad * normed, axis=0, keepdims=True),
    )


def qkv_kernel(x_ref, mod_ref, w_ref, b_ref, u_ref, qkv_ref):
    latents, seq, _ = x_ref.shape

    @pl.when(pl.program_id(0) == 0)
    def _():
        for i in range(latents):
            normed, _ = normalise(x_ref[i])
            u_ref[i * seq : (i + 1) * seq] = (
                normed * (1.0 + mod_ref[i, 1:2]) + mod_ref[i, 0:1]
            ).astype(low_type)

    for i in range(latents):
        part = slice(i * seq, (i + 1) * seq)
        qkv_ref[0, part] = (nn(u_ref[part], w_ref[0]) + b_ref[0]).astype(low_type)


def mix_kernel(qkv_ref, x_ref, mod_ref, w_ref, b_ref, o_ref, a_ref, x1_ref, u2_ref):
    seq, width = o_ref.shape
    pair = 2 * HEAD_DIM
    lane = lax.broadcasted_iota(jnp.int32, (seq, pair), 1)
    left = lane < HEAD_DIM
    for at in range(0, width, pair):
        query = qkv_ref[0, :, at : at + pair]
        key = qkv_ref[1, :, at : at + pair]
        value = qkv_ref[2, :, at : at + pair]
        mixed = []
        for side in (left, jnp.logical_not(left)):
            raw = nt(jnp.where(side, query, jnp.zeros_like(query)), key) * HEAD_DIM ** (-0.5)
            top = jnp.exp(raw - jnp.max(raw, axis=-1, keepdims=True))
            probs = top * (1.0 / jnp.sum(top, axis=-1, keepdims=True))
            mixed.append(nn(probs.astype(low_type), value))
        o_ref[:, at : at + pair] = jnp.where(left, mixed[0], mixed[1]).astype(low_type)
    branch = nn(o_ref[...], w_ref[0]) + b_ref[...]
    a_ref[...] = branch
    middle = x_ref[0] + mod_ref[0, 2:3] * branch
    x1_ref[...] = middle
    normed, _ = normalise(middle)
    u2_ref[...] = (normed * (1.0 + mod_ref[0, 4:5]) + mod_ref[0, 3:4]).astype(low_type)


GELU_SCALE = 0.7978845608028654
GELU_CUBE = 0.044715


def feed_kernel(
    u2_ref, x1_ref, mod_ref, up_ref, upb_ref, down_ref, downb_ref, g_ref, slope_ref, m_ref, x_ref
):
    latents = mod_ref.shape[0]
    seq = u2_ref.shape[0] // latents
    step = pl.program_id(0)
    for i in range(latents):
        part = slice(i * seq, (i + 1) * seq)
        pre = nn(u2_ref[part], up_ref[0]) + upb_ref[0]
        square = pre * pre
        bent = jnp.tanh(GELU_SCALE * (pre + GELU_CUBE * (square * pre)))
        half = 0.5 * (1.0 + bent)
        act = (pre * half).astype(low_type)
        g_ref[0, part] = act
        slope_ref[0, part] = (
            half
            + (0.5 * GELU_SCALE)
            * pre
            * (1.0 - bent * bent)
            * (1.0 + (3.0 * GELU_CUBE) * square)
        ).astype(low_type)
        part_sum = nn(act, down_ref[0])

        @pl.when(step == 0)
        def _():
            m_ref[part] = part_sum + downb_ref[...]

        @pl.when(step > 0)
        def _():
            m_ref[part] = m_ref[part] + part_sum

        @pl.when(step == pl.num_programs(0) - 1)
        def _():
            x_ref[part] = x1_ref[part] + mod_ref[i, 5:6] * m_ref[part]


def feed_back_kernel(
    dy_ref, m_ref, mod_ref, u2_ref, g_ref, slope_ref, up_ref, down_ref,
    gw_ref, du_ref, dgate_ref, downb_ref, upb_ref, dm_ref, df_ref,
):
    latents = mod_ref.shape[0]
    seq = u2_ref.shape[0] // latents
    step = pl.program_id(0)

    @pl.when(step == 0)
    def _():
        total = jnp.zeros(downb_ref.shape, wide)
        for i in range(latents):
            part = slice(i * seq, (i + 1) * seq)
            grad = dy_ref[part]
            dgate_ref[i] = jnp.sum(grad * m_ref[part], axis=0, keepdims=True)
            lower = (grad * mod_ref[i, 5:6]).astype(low_type)
            dm_ref[part] = lower
            total += jnp.sum(lower.astype(wide), axis=0, keepdims=True)
        downb_ref[...] = total

    sums = jnp.zeros(upb_ref.shape[1:], wide)
    for i in range(latents):
        part = slice(i * seq, (i + 1) * seq)
        lower = (nt(dm_ref[part], down_ref[0]) * slope_ref[0, part].astype(wide)).astype(low_type)
        df_ref[part] = lower
        sums += jnp.sum(lower.astype(wide), axis=0, keepdims=True)
        back = nt(lower, up_ref[0])

        @pl.when(step == 0)
        def _():
            du_ref[part] = back

        @pl.when(step > 0)
        def _():
            du_ref[part] = du_ref[part] + back

    upb_ref[0] = sums
    gw_ref[0, 0] = tn(g_ref[0], dm_ref[...]).astype(low_type)
    gw_ref[1, 0] = tn(u2_ref[...], df_ref[...]).astype(low_type)


def mix_back_kernel(
    du_ref, x1_ref, dy_ref, a_ref, qkv_ref, mod_ref, w_ref,
    dx1_ref, dall_ref, dmod_ref, sums_ref, do_ref,
):
    seq, width = x1_ref.shape
    pair = 2 * HEAD_DIM
    back, dshift, dscale = norm_back(du_ref[...], x1_ref[...], mod_ref[0, 4:5])
    dx1 = back + dy_ref[...]
    dx1_ref[...] = dx1
    dmod_ref[0, 0:1] = dshift
    dmod_ref[0, 1:2] = dscale
    dmod_ref[0, 2:3] = jnp.sum(dx1 * a_ref[...], axis=0, keepdims=True)
    da = (dx1 * mod_ref[0, 2:3]).astype(low_type)
    dall_ref[3] = da
    do_ref[...] = nt(da, w_ref[0]).astype(low_type)
    lane = lax.broadcasted_iota(jnp.int32, (seq, pair), 1)
    left = lane < HEAD_DIM
    for at in range(0, width, pair):
        cols = slice(at, at + pair)
        query = qkv_ref[0, :, cols]
        key = qkv_ref[1, :, cols]
        value = qkv_ref[2, :, cols]
        grad = do_ref[:, cols]
        found = []
        for side in (left, jnp.logical_not(left)):
            none = jnp.zeros_like(query)
            raw = nt(key, jnp.where(side, query, none)) * HEAD_DIM ** (-0.5)
            top = jnp.exp(raw - jnp.max(raw, axis=0, keepdims=True))
            probs = top * (1.0 / jnp.sum(top, axis=0, keepdims=True))
            dvalue = nn(probs.astype(low_type), grad)
            dprobs = nt(value, jnp.where(side, grad, none))
            dots = jnp.sum(dprobs * probs, axis=0, keepdims=True)
            draw = (probs * (dprobs - dots) * HEAD_DIM ** (-0.5)).astype(low_type)
            found.append((tn(draw, key), nn(draw, query), dvalue))
        for which in range(3):
            dall_ref[which, :, cols] = jnp.where(
                left, found[0][which], found[1][which]
            ).astype(low_type)

    @pl.when(pl.program_id(0) == 0)
    def _():
        sums_ref[...] = jnp.zeros_like(sums_ref)

    for which in range(4):
        sums_ref[which : which + 1] += jnp.sum(
            dall_ref[which].astype(wide), axis=0, keepdims=True
        )


def qkv_back_kernel(
    u1_ref, o_ref, dall_ref, w_ref, x_ref, dx1_ref, mod_ref, gw_ref, dx_ref, dmod_ref, acc_ref
):
    latents, seq, _ = x_ref.shape
    step = pl.program_id(0)

    @pl.when(step < 3)
    def _():
        gw_ref[0] = tn(u1_ref[...], dall_ref[0]).astype(low_type)
        for i in range(latents):
            part = slice(i * seq, (i + 1) * seq)
            back = nt(dall_ref[0, part], w_ref[0])

            @pl.when(step == 0)
            def _():
                acc_ref[part] = back

            @pl.when(step > 0)
            def _():
                acc_ref[part] = acc_ref[part] + back

    @pl.when(step == 3)
    def _():
        gw_ref[0] = tn(o_ref[...], dall_ref[0]).astype(low_type)
        for i in range(latents):
            part = slice(i * seq, (i + 1) * seq)
            back, dshift, dscale = norm_back(acc_ref[part], x_ref[i], mod_ref[i, 1:2])
            dx_ref[i] = back + dx1_ref[part]
            dmod_ref[i, 0:1] = dshift
            dmod_ref[i, 1:2] = dscale


def shape_of(dims, kind):
    return jax.ShapeDtypeStruct(tuple(dims), kind)


def full(dims):
    return pl.BlockSpec(tuple(dims), lambda step: (0,) * len(dims))


def along(dims, where):
    return pl.BlockSpec(
        tuple(dims), lambda step: tuple(step if i == where else 0 for i in range(len(dims)))
    )


def call(kernel, grid, in_specs, out_specs, out_shape, scratch, flops, moved):
    return pl.pallas_call(
        kernel,
        grid=(grid,),
        in_specs=in_specs,
        out_specs=out_specs,
        out_shape=out_shape,
        scratch_shapes=scratch,
        compiler_params=pltpu.CompilerParams(vmem_limit_bytes=56 * 2**20),
        cost_estimate=pl.CostEstimate(flops=flops, bytes_accessed=moved, transcendentals=0),
        name=kernel.__name__,
    )


def forward_layer(hidden, mod, weights):
    attn_w, up_w, down_w, qkv_b, proj_b, up_b, down_b = weights
    latents, seq, width = hidden.shape
    rows = latents * seq
    unit = 2 * rows * width * width
    size = rows * width
    u1, qkv = call(
        qkv_kernel,
        3,
        [
            full(hidden.shape),
            full(mod.shape),
            along((1, width, width), 0),
            along((1, 1, width), 0),
        ],
        [full((rows, width)), along((1, rows, width), 0)],
        [shape_of((rows, width), low_type), shape_of((3, rows, width), low_type)],
        [],
        3 * unit,
        18 * size,
    )(hidden, mod, attn_w, qkv_b)
    token = along((seq, width), 0)
    mixed, branch, middle, u2 = call(
        mix_kernel,
        latents,
        [
            along((3, seq, width), 1),
            along((1, seq, width), 0),
            along((1, 6, width), 0),
            pl.BlockSpec((1, width, width), lambda step: (3, 0, 0)),
            full((1, width)),
        ],
        [token, token, token, token],
        [
            shape_of((rows, width), low_type),
            shape_of((rows, width), wide),
            shape_of((rows, width), wide),
            shape_of((rows, width), low_type),
        ],
        [],
        5 * unit,
        24 * size,
    )(qkv, hidden, mod, attn_w, proj_b)
    act, slope, branch_two, result = call(
        feed_kernel,
        SLABS,
        [
            full((rows, width)),
            full((rows, width)),
            full(mod.shape),
            along((1, width, width), 0),
            along((1, 1, width), 0),
            along((1, width, width), 0),
            full((1, width)),
        ],
        [
            along((1, rows, width), 0),
            along((1, rows, width), 0),
            full((rows, width)),
            full((rows, width)),
        ],
        [
            shape_of((SLABS, rows, width), low_type),
            shape_of((SLABS, rows, width), low_type),
            shape_of((rows, width), wide),
            shape_of((rows, width), wide),
        ],
        [],
        12 * unit,
        40 * size,
    )(u2, middle, mod, up_w, up_b, down_w, down_b)
    saved = (hidden, mod, u1, qkv, mixed, branch, middle, u2, act, slope, branch_two)
    return result.reshape(hidden.shape), saved


def backward_layer(grad_out, weights, saved):
    attn_w, up_w, down_w = weights[:3]
    hidden, mod, u1, qkv, mixed, branch, middle, u2, act, slope, branch_two = saved
    latents, seq, width = hidden.shape
    rows = latents * seq
    unit = 2 * rows * width * width
    size = rows * width
    grad_out = grad_out.reshape(rows, width)
    block = along((1, rows, width), 0)
    square = along((1, width, width), 0)
    flat = full((rows, width))
    ff_grads, du2, dgate_two, down_sums, up_sums = call(
        feed_back_kernel,
        SLABS,
        [flat, flat, full(mod.shape), flat, block, block, square, square],
        [
            along((2, 1, width, width), 1),
            flat,
            full((latents, 1, width)),
            full((1, width)),
            along((1, 1, width), 0),
        ],
        [
            shape_of((2, SLABS, width, width), low_type),
            shape_of((rows, width), wide),
            shape_of((latents, 1, width), wide),
            shape_of((1, width), wide),
            shape_of((SLABS, 1, width), wide),
        ],
        [pltpu.VMEM((rows, width), low_type), pltpu.VMEM((rows, width), low_type)],
        16 * unit,
        50 * size,
    )(grad_out, branch_two, mod, u2, act, slope, up_w, down_w)
    token = along((seq, width), 0)
    dx1, dall, dmod_mid, sums = call(
        mix_back_kernel,
        latents,
        [
            token,
            token,
            token,
            token,
            along((3, seq, width), 1),
            along((1, 6, width), 0),
            pl.BlockSpec((1, width, width), lambda step: (3, 0, 0)),
        ],
        [
            token,
            along((4, seq, width), 1),
            along((1, 3, width), 0),
            full((4, width)),
        ],
        [
            shape_of((rows, width), wide),
            shape_of((4, rows, width), low_type),
            shape_of((latents, 3, width), wide),
            shape_of((4, width), wide),
        ],
        [pltpu.VMEM((seq, width), low_type)],
        10 * unit,
        40 * size,
    )(du2, middle, grad_out, branch, qkv, mod, attn_w)
    at_grads, dx, dmod_low = call(
        qkv_back_kernel,
        4,
        [
            flat,
            flat,
            block,
            square,
            full(hidden.shape),
            flat,
            full(mod.shape),
        ],
        [square, full(hidden.shape), full((latents, 2, width))],
        [
            shape_of((4, width, width), low_type),
            shape_of(hidden.shape, wide),
            shape_of((latents, 2, width), wide),
        ],
        [pltpu.VMEM((rows, width), wide)],
        7 * unit,
        36 * size,
    )(u1, mixed, dall, attn_w, hidden, dx1, mod)
    dmod = jnp.concatenate(
        [dmod_low, dmod_mid[:, 2:3], dmod_mid[:, 0:2], dgate_two], axis=1
    ).reshape(latents, 6 * width)
    return dx, dmod, ff_grads, at_grads, (sums, up_sums, down_sums)


class Net:
    def __init__(self, mesh):
        self.replicas = mesh.shape["replica"]
        self.shards = mesh.shape["shard"]

    def swap(self, values, axis, step):
        count = self.replicas if axis == "replica" else self.shards
        return lax.ppermute(values, axis, [(i, i ^ step) for i in range(count)])

    def bits(self, axis):
        count = self.replicas if axis == "replica" else self.shards
        found = []
        step = 1
        while step < count:
            found.append(step)
            step *= 2
        return found

    def gather_rel(self, values, axes):
        stack = values[None]
        for axis in axes:
            for step in self.bits(axis):
                stack = jnp.concatenate([stack, self.swap(stack, axis, step)])
        return stack

    def scatter_rel(self, stack):
        for step in self.bits("shard"):
            pairs = stack.reshape((stack.shape[0] // 2, 2) + stack.shape[1:])
            stack = pairs[:, 0] + self.swap(pairs[:, 1], "shard", 1 * step)
        return stack[0]


def order_kernel(places, pieces_per_slab, here_ref, near_ref, keep_ref, send_ref):
    shard_low = here_ref[0] % 2
    replica = here_ref[1]
    for place in range(places):
        piece = jnp.bitwise_xor(replica, place)
        slab = piece // pieces_per_slab
        part = piece % pieces_per_slab
        keep_ref[0, place] = near_ref[slab, shard_low, part].astype(keep_ref.dtype)
        send_ref[0, place] = near_ref[slab, 1 - shard_low, part].astype(send_ref.dtype)


def order_grads(net, here, grads):
    slabs, shards, rows, width = grads.shape
    per_slab = net.replicas // SLABS if net.replicas > SLABS else 1
    places = net.replicas
    if net.replicas < SLABS:
        raise ValueError("replicas")
    piece_rows = rows * SLABS // places
    groups = slabs // SLABS
    view = grads.reshape(groups, SLABS, shards, per_slab, piece_rows, width)
    out = jax.ShapeDtypeStruct((groups, shards // 2, places, piece_rows, width), low_type)
    spec = pl.BlockSpec(
        (None, 1, places, piece_rows, width), lambda g, j, here_ref: (g, j, 0, 0, 0)
    )
    return pl.pallas_call(
        functools.partial(order_kernel, places, per_slab),
        grid_spec=pltpu.PrefetchScalarGridSpec(
            num_scalar_prefetch=1,
            grid=(groups, shards // 2),
            in_specs=[
                pl.BlockSpec(
                    (None, SLABS, 2, per_slab, piece_rows, width),
                    lambda g, j, here_ref: (
                        g,
                        0,
                        jnp.bitwise_xor(here_ref[0] // 2, j),
                        0,
                        0,
                        0,
                    ),
                )
            ],
            out_specs=[spec, spec],
        ),
        out_shape=[out, out],
        name="order_grads",
    )(here, view)


def add_low(left, right):
    return (left.astype(wide) + right.astype(wide)).astype(low_type)


def halve(stack, dim, where):
    size = stack.shape[dim]
    shape = stack.shape[:dim] + (size // (2 * where), 2, where) + stack.shape[dim + 1 :]
    view = stack.reshape(shape)
    rest = stack.shape[:dim] + (size // 2,) + stack.shape[dim + 1 :]
    return (
        lax.index_in_dim(view, 0, dim + 1, keepdims=False).reshape(rest),
        lax.index_in_dim(view, 1, dim + 1, keepdims=False).reshape(rest),
    )


def reduce_grads(net, here, grads):
    keep, give = order_grads(net, here, grads)
    total = add_low(keep, net.swap(give, "shard", 1))
    groups, near, places, rows, width = total.shape
    done = []
    for part, order in ((0, 1), (1, -1)):
        piece = total[:, :, :, part * (rows // 2) : (part + 1) * (rows // 2)]
        left = list(range(places))
        for step in net.bits("replica")[::order]:
            where = sum(1 for q in left if q < step)
            keep, give = halve(piece, 2, where)
            left = [q for q in left if not q & step]
            piece = add_low(keep, net.swap(give, "replica", step))
        done.append(piece[:, :, 0])
    total = jnp.concatenate(done, axis=2)
    for step in net.bits("shard")[1:]:
        keep, give = halve(total, 1, 1)
        total = add_low(keep, net.swap(give, "shard", step))
    mine = total[:, 0]
    every = [mine] + [net.swap(mine, "replica", step) for step in range(1, places)]
    stack = jnp.stack(every)
    own = jnp.arange(places, dtype=jnp.int32)
    return jnp.take(stack, jnp.bitwise_xor(own, here[1]), axis=0).astype(wide)


def local(
    net,
    hidden_in,
    condition,
    latent_live,
    out_grad,
    ada_weight,
    qkv_weight,
    proj_weight,
    fc1_weight,
    fc2_weight,
    ada_bias,
    qv_bias,
    proj_bias,
    fc1_bias,
    fc2_bias,
):
    shard = lax.axis_index("shard")
    replica = lax.axis_index("replica")
    here = jnp.stack([shard, replica]).astype(jnp.int32)
    shards, replicas = net.shards, net.replicas
    latents_here, model_width = condition.shape
    rows = proj_weight.shape[1]
    piece_rows = rows * SLABS // replicas
    mod_width = ada_weight.shape[2]

    def pack(layer):
        qkv = qkv_weight[layer].astype(low_type)
        up = fc1_weight[layer].astype(low_type)
        up = up.reshape(rows, shards, SLABS, rows).transpose(2, 0, 1, 3)
        down = fc2_weight[layer].astype(low_type)
        blocks = [qkv[:, b * model_width : (b + 1) * model_width] for b in range(3)]
        blocks += [proj_weight[layer].astype(low_type)]
        blocks += [up[b].reshape(rows, model_width) for b in range(SLABS)]
        blocks += [down[b * rows : (b + 1) * rows] for b in range(SLABS)]
        packed = jnp.stack(blocks).reshape(3, replicas, piece_rows, model_width)
        return lax.dynamic_index_in_dim(packed, replica, 1, keepdims=False)

    gathered = []
    for layer in range(LAYERS):
        whole = lax.all_gather(pack(layer), ("replica", "shard"), axis=0, tiled=False)
        whole = whole.reshape(
            SLABS, replicas // SLABS, shards, 3, piece_rows, model_width
        ).transpose(3, 0, 2, 1, 4, 5)
        gathered.append(whole.reshape(3, SLABS, shards, rows, model_width))

    cond_low = jax.nn.silu(condition).astype(low_type)
    bias_rows = jnp.concatenate([qv_bias, proj_bias, fc1_bias, fc2_bias], axis=1).astype(low_type)
    bias_width = bias_rows.shape[1]
    cond_rel = net.gather_rel(cond_low, ["shard"])
    bias_all = lax.all_gather(bias_rows, "shard", axis=0, tiled=False)
    cond_all_rel = net.gather_rel(cond_rel, ["replica"])
    group = shards * latents_here
    cond_rows = lax.dynamic_slice_in_dim(
        cond_rel.reshape(group, model_width), shard * rows, rows, axis=1
    )
    cond_every = lax.dynamic_slice_in_dim(
        cond_all_rel.reshape(replicas * group, model_width), shard * rows, rows, axis=1
    ).astype(wide)
    ada_low = ada_weight.astype(low_type)
    partial = jnp.stack([nn(cond_rows, ada_low[layer]) for layer in range(LAYERS)], axis=1)
    ada_part = ada_bias.shape[1]
    bias_here = lax.dynamic_update_slice_in_dim(
        jnp.zeros((LAYERS, mod_width), wide),
        ada_bias.astype(low_type).astype(wide),
        shard * ada_part,
        axis=1,
    )
    partial = (partial + bias_here[None]).reshape(shards, latents_here, LAYERS, mod_width)
    modulations = net.scatter_rel(partial)

    widths = (qv_bias.shape[1], proj_bias.shape[1], fc1_bias.shape[1], fc2_bias.shape[1])
    starts = (0, widths[0], widths[0] + widths[1], widths[0] + widths[1] + widths[2])

    def weights_of(layer):
        slabs = gathered[layer].reshape(3, SLABS, model_width, model_width)
        qv, proj, up, down = [
            bias_all[:, layer, start : start + width].reshape(-1).astype(wide)
            for start, width in zip(starts, widths)
        ]
        qkv_b = jnp.stack([qv[:model_width], jnp.zeros((model_width,), wide), qv[model_width:]])
        up_b = up.reshape(shards, SLABS, rows).transpose(1, 0, 2).reshape(SLABS, 1, model_width)
        return (
            slabs[0],
            slabs[1],
            slabs[2],
            qkv_b[:, None],
            proj[None],
            up_b,
            down[None],
        )

    live_rows = latent_live.astype(wide)[:, None, None]
    saved_all = []
    current = hidden_in
    weights_all = [weights_of(layer) for layer in range(LAYERS)]
    for layer in range(LAYERS):
        current, saved_state = forward_layer(
            current, modulations[:, layer].reshape(latents_here, 6, model_width), weights_all[layer]
        )
        saved_all.append(saved_state)
    result = current * live_rows
    grad_now = out_grad * live_rows

    def send(grads):
        slabs = grads.reshape(-1, shards, rows, model_width)
        return reduce_grads(net, here, slabs)

    ada_wide = ada_low.astype(wide)
    grad_cond = jnp.zeros((group, rows), wide)
    owned = [None] * LAYERS
    ada_grads = [None] * LAYERS
    ada_bias_grads = [None] * LAYERS
    bias_sums = [None] * LAYERS
    for layer in reversed(range(LAYERS)):
        grad_now, grad_modul, ff_grads, at_grads, (sums, up_sums, down_sums) = backward_layer(
            grad_now, weights_all[layer], saved_all[layer]
        )
        ff_owned = send(ff_grads)
        at_owned = send(at_grads)
        bias_grads = (
            jnp.concatenate([sums[0], sums[2]]),
            sums[3],
            up_sums.reshape(SLABS, shards, rows).transpose(1, 0, 2).reshape(-1),
            down_sums[0],
        )
        modul_rel = net.gather_rel(net.gather_rel(grad_modul, ["shard"]), ["replica"])
        modul_rel = modul_rel.reshape(replicas, group, mod_width)
        grad_cond = grad_cond + exact_trail(modul_rel[0], ada_wide[layer])
        modul_every = modul_rel.reshape(replicas * group, mod_width)
        ada_grads[layer] = exact_lead(cond_every, modul_every)
        ada_bias_grads[layer] = jnp.sum(
            lax.dynamic_slice_in_dim(modul_every, shard * ada_part, ada_part, axis=1), axis=0
        )
        at_rows = at_owned.transpose(1, 0, 2, 3).reshape(SLABS, rows, model_width)
        ff_rows = ff_owned.transpose(1, 0, 2, 3).reshape(2, SLABS, rows, model_width)
        wide_of = lambda w: w.transpose(1, 0, 2).reshape(rows, -1)
        owned[layer] = (
            wide_of(at_rows[:3]),
            at_rows[3],
            ff_rows[1]
            .reshape(SLABS, rows, shards, rows)
            .transpose(1, 2, 0, 3)
            .reshape(rows, SLABS * model_width),
            ff_rows[0].reshape(SLABS * rows, model_width),
        )
        bias_sums[layer] = jnp.concatenate(
            [grad.reshape(shards, -1) for grad in bias_grads], axis=1
        )
    bias_total = lax.psum(jnp.stack(bias_sums), ("replica", "shard"))
    bias_mine = lax.dynamic_index_in_dim(bias_total, shard, 1, keepdims=False)
    bias_out = [bias_mine[:, start : start + width] for start, width in zip(starts, widths)]

    parts = grad_cond.reshape(shards, latents_here, rows)
    back = [parts[0]] + [net.swap(parts[step], "shard", step) for step in range(1, shards)]
    back = jnp.take(
        jnp.stack(back), jnp.bitwise_xor(jnp.arange(shards, dtype=jnp.int32), here[0]), axis=0
    )
    cond_back = back.transpose(1, 0, 2).reshape(latents_here, model_width)
    grad_condition = jax.vjp(jax.nn.silu, condition)[1](cond_back)[0]
    return (
        result,
        grad_now,
        grad_condition,
        jnp.stack(ada_grads),
        jnp.stack([owned[layer][0] for layer in range(LAYERS)]),
        jnp.stack([owned[layer][1] for layer in range(LAYERS)]),
        jnp.stack([owned[layer][2] for layer in range(LAYERS)]),
        jnp.stack([owned[layer][3] for layer in range(LAYERS)]),
        jnp.stack(ada_bias_grads),
        *bias_out,
    )


def solution(mesh):
    tokens = P(("replica", "shard"), None, None)
    weight = P(None, "shard", None)
    bias = P(None, "shard")
    rows = P(("replica", "shard"), None)
    return jax.shard_map(
        functools.partial(local, Net(mesh)),
        mesh=mesh,
        in_specs=(tokens, rows, P(("replica", "shard")), tokens) + (weight,) * 5 + (bias,) * 5,
        out_specs=(tokens, tokens, rows) + (weight,) * 5 + (bias,) * 5,
        check_vma=False,
    )
```

time: 1830 us -> 904 us (0.49)
  waiting for transfers between devices: 1210 us -> 340 us
  matrix products: 313 us -> 5.86 us
  Pallas kernels: 0 us -> 249 us
  starting transfers between devices: 1.57 us -> 73.3 us
  local copies, waits for them, and re-layouts: 132 us -> 104 us
  blocking collectives: 75.1 us -> 54.2 us
    reduce_scatter x10 -> x0, waiting for transfers between devices: 731 us -> none  [the longest x2 289 us: scatter_grads(): lax.psum_scatter(ga_w, 'shard', scatter_dimension=0, tiled=True)]
    dot_general x36 -> x2, matrix products: 261 us -> 0.48 us  [nn(): lax.dot_general(left, right, (((1,), (0,)), ((), ())), preferred_element_...]
    pallas_call x0 -> x16, Pallas kernels: none -> 249 us  [the longest x2 55.3 us: backward_layer(): call(feed_back_kernel, SLABS, [flat, flat, full(mod.shape), flat, block,...]
    ppermute x0 -> x65, waiting for transfers between devices: none -> 201 us  [swap(): return lax.ppermute(values, axis, [(i, i ^ step) for i in range(count)])]
    psum x1 -> x0, waiting for transfers between devices: 194 us -> none  [sum_replicas(): lax.psum((ga_w, gq_w, gp_w, gu_w, gd_w, ga_b, gq_b, gp_b, gu_b, gd_b), 'r...]
    all_gather x10 -> x2, waiting for transfers between devices: 248 us -> 139 us  [local(): lax.all_gather(pack(layer), ('replica', 'shard'), axis=0, tiled=False)]
    ppermute x0 -> x65, starting transfers between devices: none -> 73.3 us  [swap(): return lax.ppermute(values, axis, [(i, i ^ step) for i in range(count)])]
    unnamed x317 -> x127, local copies, waits for them, and re-layouts: 61.5 us -> 18.6 us
  transfers between devices with their start and end apart: 22 -> 67, of which waited for: 16 -> 41; matrix products, arithmetic and copies ran while one was open for 20% -> 11% of each run, Pallas kernels for 0% -> 4%
where the time goes in v1:
time: 904 us; the launch traced here: 897 us
  waiting for transfers between devices  340 us (38%)
  Pallas kernels  249 us (28%)
  local copies, waits for them, and re-layouts  104 us (12%)
  starting transfers between devices  73.3 us (8%)
  other arithmetic  55.1 us (6%)
  blocking collectives  54.2 us (6%)
  between operations  15.9 us (2%)
    ppermute x65, waiting for transfers between devices, swap(): return lax.ppermute(values, axis, [(i, i ^ step) for i in range(count)])  201 us
    all_gather x2, waiting for transfers between devices, local(): lax.all_gather(pack(layer), ('replica', 'shard'), axis=0, tiled=False)  139 us
    ppermute x65, starting transfers between devices, swap(): return lax.ppermute(values, axis, [(i, i ^ step) for i in range(count)])  73.3 us
    pallas_call x2, Pallas kernels, backward_layer(): call(feed_back_kernel, SLABS, [flat, flat, full(mod.shape), flat, block,...  55.3 us
    pallas_call x2, Pallas kernels, backward_layer(): call(mix_back_kernel, latents, [token, token, token, token, along((3, seq...  48.1 us
    pallas_call x2, Pallas kernels, forward_layer(): call(feed_kernel, SLABS, [full((rows, width)), full((rows, width)), full(...  42 us
    psum x1, blocking collectives, local(): bias_total = lax.psum(jnp.stack(bias_sums), ('replica', 'shard'))  39 us
    pallas_call x2, Pallas kernels, backward_layer(): call(qkv_back_kernel, 4, [flat, flat, block, square, full(hidden.shape),...  32.9 us
  transfers between devices with their start and end apart: 67, of which 41 were waited for; matrix products, arithmetic and copies ran while one was open for 11% of the time, Pallas kernels for 4%

profile of v1, /device:TPU:0, one launch (start us, length us, event | category | flops | bytes accessed | tf_op | source)
XLA Modules:
  0.0 897.0 jit_solution(9644390980275419118)
XLA Ops:
  36.0 15.2 %all_gather.18 = bf16[8,2,768]{2,1,0:T(2,128)(2,1)S(1)} all-gather(bf16[1,2,768]{2,1,0:T(2,128)(2,1)S(1)} %pad_maximum_fusion.29), channel_id=1, replica_groups=mesh['replica'=4,'shard'=8] {'shard'}, dimensions={0}, use_global_device_ids=true | all-gather | bytes 27648 | tf_op jit(solution)/shard_map/all_gather | solution.py:639
  75.3 13.5 %collective-permute-done.4 = f32[2,3,2,4608]{3,1,2,0:T(4,128)S(1)} collective-permute-done((f32[2,3,2,4608]{3,1,2,0:T(4,128)S(1)}, f32[2,3,2,4608]{3,1,2,0:T(4,128)S(1)}, u32[]{:S(2)}, u32[]{:S(2)}) %collective-permute-start.4) | collective-permute-done | bytes 221216 | tf_op jit(solution)/shard_map/ppermute | solution.py:475
  89.5 10.1 %collective-permute-done.5 = f32[1,3,2,4608]{3,1,2,0:T(4,128)S(1)} collective-permute-done((f32[1,3,2,4608]{3,1,2,0:T(4,128)S(1)}, f32[1,3,2,4608]{3,1,2,0:T(4,128)S(1)}, u32[]{:S(2)}, u32[]{:S(2)}) %collective-permute-start.5) | collective-permute-done | bytes 110624 | tf_op jit(solution)/shard_map/ppermute | solution.py:475
  101.1 44.8 %all-gather.5.cloned.1.call-done = bf16[96,1,96,768]{3,2,1,0:T(8,128)(2,1)} async-done(((bf16[3,1,96,768]{3,2,1,0:T(8,128)(2,1)}), bf16[96,1,96,768]{3,2,1,0:T(8,128)(2,1)}) %all-gather.5.cloned.1.call-update) | async-done | bytes 14155792 | tf_op jit(solution)/shard_map/all_gather | solution.py:629
  145.9 11.1 %fusion.89 = (bf16[1,4,8,1,96,768]{5,4,0,2,1,3:T(8,128)(2,1)}, bf16[1,4,8,1,96,768]{5,4,0,2,1,3:T(8,128)(2,1)}, bf16[1,4,8,1,96,768]{5,4,0,2,1,3:T(8,128)(2,1)}) fusion(bf16[3,4,8,1,96,768]{5,4,0,2,1,3:T(8,128)(2,1)} %bitcast.515), kind=kLoop, calls=%fused_computation.322 | loop fusion | bytes 28311552 | tf_op jit(solution)/shard_map/slice | solution.py:674
  157.0 93.9 %all-gather.7.cloned.1.call-done = bf16[96,1,96,768]{3,2,1,0:T(8,128)(2,1)} async-done(((bf16[3,1,96,768]{3,2,1,0:T(8,128)(2,1)}), bf16[96,1,96,768]{3,2,1,0:T(8,128)(2,1)}) %all-gather.7.cloned.1.call-update) | async-done | bytes 14155792 | tf_op jit(solution)/shard_map/all_gather | solution.py:629
  250.9 11.1 %fusion.88 = (bf16[1,4,8,1,96,768]{5,4,0,2,1,3:T(8,128)(2,1)}, bf16[1,4,8,1,96,768]{5,4,0,2,1,3:T(8,128)(2,1)}, bf16[1,4,8,1,96,768]{5,4,0,2,1,3:T(8,128)(2,1)}) fusion(bf16[3,4,8,1,96,768]{5,4,0,2,1,3:T(8,128)(2,1)} %bitcast.516), kind=kLoop, calls=%fused_computation.321 | loop fusion | bytes 28311552 | tf_op jit(solution)/shard_map/slice | solution.py:674
  262.0 7.7 qkv_kernel.2
  269.8 11.1 %mix_kernel.2 = (bf16[768,768]{1,0:T(8,128)(2,1)}, f32[768,768]{1,0:T(8,128)}, f32[768,768]{1,0:T(8,128)}, bf16[768,768]{1,0:T(8,128)(2,1)}) custom-call(bf16[3,768,768]{2,1,0:T(8,128)(2,1)} %get-tuple-element.67.qkv_ref, f32[3,256,768]{2,1,0:T(8,128)} %x_ref.5, f32[3,6,768]{2,1,0:T(8,128)} %reshape_squeeze.128.mod_ref, bf16[4,768,768]{2,1,0:T(8,128)(2,1)} %bitcast.532, ...), custom_call_target="tpu_custom_call" | custom-call | flops 4529848320 | bytes 14155776 | tf_op jit(solution)/shard_map/mix_kernel/pallas_call | solution.py:325
  280.9 21.0 %feed_kernel.2 = (bf16[4,768,768]{2,1,0:T(8,128)(2,1)}, bf16[4,768,768]{2,1,0:T(8,128)(2,1)}, f32[768,768]{1,0:T(8,128)}, f32[768,768]{1,0:T(8,128)}) custom-call(bf16[768,768]{1,0:T(8,128)(2,1)} %get-tuple-element.68.u2_ref, f32[768,768]{1,0:T(8,128)} %get-tuple-element.69.x1_ref, f32[3,6,768]{2,1,0:T(8,128)} %reshape_squeeze.128.mod_ref, ...), custom_call_target="tpu_custom_call" | custom-call | flops 10871635968 | bytes 23592960 | tf_op jit(solution)/shard_map/feed_kernel/pallas_call | solution.py:346
  301.8 8.3 qkv_kernel.3
  310.1 11.2 %mix_kernel.3 = (bf16[768,768]{1,0:T(8,128)(2,1)}, f32[768,768]{1,0:T(8,128)}, f32[768,768]{1,0:T(8,128)}, bf16[768,768]{1,0:T(8,128)(2,1)}) custom-call(bf16[3,768,768]{2,1,0:T(8,128)(2,1)} %get-tuple-element.71.qkv_ref, f32[3,256,768]{2,1,0:T(8,128)} %bitcast.605, f32[3,6,768]{2,1,0:T(8,128)} %reshape_squeeze.129.mod_ref, bf16[4,768,768]{2,1,0:T(8,128)(2,1)} %bitcast.540, ...), custom_call_target="tpu_custom_call" | custom-call | flops 4529848320 | bytes 14155776 | tf_op jit(solution)/shard_map/mix_kernel/pallas_call | solution.py:325
  321.3 21.0 %feed_kernel.3 = (bf16[4,768,768]{2,1,0:T(8,128)(2,1)}, bf16[4,768,768]{2,1,0:T(8,128)(2,1)}, f32[768,768]{1,0:T(8,128)}, f32[768,768]{1,0:T(8,128)}) custom-call(bf16[768,768]{1,0:T(8,128)(2,1)} %get-tuple-element.72.u2_ref, f32[768,768]{1,0:T(8,128)} %get-tuple-element.73.x1_ref, f32[3,6,768]{2,1,0:T(8,128)} %reshape_squeeze.129.mod_ref, ...), custom_call_target="tpu_custom_call" | custom-call | flops 10871635968 | bytes 23592960 | tf_op jit(solution)/shard_map/feed_kernel/pallas_call | solution.py:346
  342.3 4.4 broadcast_multiply_fusion
  346.7 27.7 %feed_back_kernel.2 = (bf16[2,4,768,768]{3,2,1,0:T(8,128)(2,1)}, f32[768,768]{1,0:T(8,128)}, f32[3,1,768]{2,1,0:T(1,128)}, f32[1,768]{1,0:T(1,128)}, f32[4,1,768]{2,1,0:T(1,128)}) custom-call(f32[768,768]{1,0:T(8,128)} %bitcast.573, f32[768,768]{1,0:T(8,128)} %get-tuple-element.79.m_ref, f32[3,6,768]{2,1,0:T(8,128)} %reshape_squeeze.129.mod_ref, ...), custom_call_target="tpu_custom_call" | custom-call | flops 14495514624 | bytes 29491200 | tf_op jit(solution)/shard_map/feed_back_kernel/pallas_call | solution.py:389
  374.4 23.9 %mix_back_kernel.2 = (f32[768,768]{1,0:T(8,128)}, bf16[4,768,768]{2,1,0:T(8,128)(2,1)}, f32[3,3,768]{2,1,0:T(4,128)}, f32[4,768]{1,0:T(4,128)}) custom-call(f32[768,768]{1,0:T(8,128)} %get-tuple-element.82.du_ref, f32[768,768]{1,0:T(8,128)} %get-tuple-element.73.x1_ref, f32[768,768]{1,0:T(8,128)} %bitcast.574, f32[768,768]{1,0:T(8,128)} %get-tuple-element.83.a_ref, ...), custom_call_target="tpu_custom_call" | custom-call | flops 9059696640 | bytes 23592960 | tf_op jit(solution)/shard_map/mix_back_kernel/pallas_call | solution.py:412
  398.3 16.5 %qkv_back_kernel.2 = (bf16[4,768,768]{2,1,0:T(8,128)(2,1)}, f32[3,256,768]{2,1,0:T(8,128)}, f32[3,2,768]{2,1,0:T(2,128)}) custom-call(bf16[768,768]{1,0:T(8,128)(2,1)} %get-tuple-element.77.u1_ref, bf16[768,768]{1,0:T(8,128)(2,1)} %get-tuple-element.78.o_ref, bf16[4,768,768]{2,1,0:T(8,128)(2,1)} %get-tuple-element.84.dall_ref, ...), custom_call_target="tpu_custom_call" | custom-call | flops 6341787648 | bytes 21233664 | tf_op jit(solution)/shard_map/qkv_back_kernel/pallas_call | solution.py:440
  414.8 27.6 %feed_back_kernel.3 = (bf16[2,4,768,768]{3,2,1,0:T(8,128)(2,1)}, f32[768,768]{1,0:T(8,128)}, f32[3,1,768]{2,1,0:T(1,128)}, f32[1,768]{1,0:T(1,128)}, f32[4,1,768]{2,1,0:T(1,128)}) custom-call(f32[768,768]{1,0:T(8,128)} %bitcast.607, f32[768,768]{1,0:T(8,128)} %get-tuple-element.87.m_ref, f32[3,6,768]{2,1,0:T(8,128)} %reshape_squeeze.128.mod_ref, ...), custom_call_target="tpu_custom_call" | custom-call | flops 14495514624 | bytes 29491200 | tf_op jit(solution)/shard_map/feed_back_kernel/pallas_call | solution.py:389
  442.4 24.3 %mix_back_kernel.3 = (f32[768,768]{1,0:T(8,128)}, bf16[4,768,768]{2,1,0:T(8,128)(2,1)}, f32[3,3,768]{2,1,0:T(4,128)}, f32[4,768]{1,0:T(4,128)}) custom-call(f32[768,768]{1,0:T(8,128)} %get-tuple-element.90.du_ref, f32[768,768]{1,0:T(8,128)} %get-tuple-element.69.x1_ref, f32[768,768]{1,0:T(8,128)} %bitcast.608, f32[768,768]{1,0:T(8,128)} %get-tuple-element.91.a_ref, ...), custom_call_target="tpu_custom_call" | custom-call | flops 9059696640 | bytes 23592960 | tf_op jit(solution)/shard_map/mix_back_kernel/pallas_call | solution.py:412
  468.4 16.4 %qkv_back_kernel.3 = (bf16[4,768,768]{2,1,0:T(8,128)(2,1)}, f32[3,256,768]{2,1,0:T(8,128)}, f32[3,2,768]{2,1,0:T(2,128)}) custom-call(bf16[768,768]{1,0:T(8,128)(2,1)} %get-tuple-element.75.u1_ref, bf16[768,768]{1,0:T(8,128)(2,1)} %get-tuple-element.76.o_ref, bf16[4,768,768]{2,1,0:T(8,128)(2,1)} %get-tuple-element.92.dall_ref, ...), custom_call_target="tpu_custom_call" | custom-call | flops 6341787648 | bytes 21233664 | tf_op jit(solution)/shard_map/qkv_back_kernel/pallas_call | solution.py:440
  487.6 39.0 %psum.7 = f32[2,8,768]{2,1,0:T(8,128)S(1)} all-reduce(f32[2,8,768]{2,1,0:T(8,128)S(1)} %pad_maximum_fusion.24), channel_id=1, replica_groups=mesh['replica'=4,'shard'=8] {'replica','shard'}, use_global_device_ids=true, to_apply=%region_2.5 | all-reduce | flops 12288 | bytes 98304 | tf_op jit(solution)/shard_map/psum | solution.py:738
  528.5 5.7 order_grads.4
  534.3 5.7 order_grads.5
  540.5 10.3 %order_grads.6 = (bf16[2,4,4,96,768]{4,3,2,1,0:T(8,128)(2,1)}, bf16[2,4,4,96,768]{4,3,2,1,0:T(8,128)(2,1)}) custom-call(s32[2]{0:T(128)} %pad_add_fusion.here_ref, bf16[2,4,8,1,96,768]{5,4,3,2,1,0:T(8,128)(2,1)} %bitcast.518), custom_call_target="tpu_custom_call" | custom-call | tf_op jit(solution)/shard_map/order_grads/pallas_call | solution.py:524
  550.8 10.4 %order_grads.7 = (bf16[2,4,4,96,768]{4,3,2,1,0:T(8,128)(2,1)}, bf16[2,4,4,96,768]{4,3,2,1,0:T(8,128)(2,1)}) custom-call(s32[2]{0:T(128)} %pad_add_fusion.here_ref, bf16[2,4,8,1,96,768]{5,4,3,2,1,0:T(8,128)(2,1)} %bitcast.517), custom_call_target="tpu_custom_call" | custom-call | tf_op jit(solution)/shard_map/order_grads/pallas_call | solution.py:524
  563.4 4.5 collective-permute-done.10
  573.0 17.8 %collective-permute-done.11 = f32[4,3,4608]{2,1,0:T(4,128)S(1)} collective-permute-done((f32[4,3,4608]{2,1,0:T(4,128)S(1)}, f32[4,3,4608]{2,1,0:T(4,128)S(1)}, u32[]{:S(2)}, u32[]{:S(2)}) %collective-permute-start.11) | collective-permute-done | bytes 221216 | tf_op jit(solution)/shard_map/ppermute | solution.py:475
  591.8 4.4 collective-permute-done.8
  616.5 8.7 collective-permute-done.23
  629.1 3.5 collective-permute-done.21
  636.9 12.9 %collective-permute-done.24 = f32[2,8,3,4608]{3,1,2,0:T(8,128)S(1)} collective-permute-done((f32[2,8,3,4608]{3,1,2,0:T(8,128)}, f32[2,8,3,4608]{3,1,2,0:T(8,128)S(1)}, u32[]{:S(2)}, u32[]{:S(2)}) %collective-permute-start.24) | collective-permute-done | bytes 884768 | tf_op jit(solution)/shard_map/ppermute | solution.py:475
  650.0 13.6 %collective-permute-done.22 = f32[2,8,3,4608]{3,1,2,0:T(8,128)} collective-permute-done((f32[2,8,3,4608]{3,1,2,0:T(8,128)}, f32[2,8,3,4608]{3,1,2,0:T(8,128)}, u32[]{:S(2)}, u32[]{:S(2)}) %collective-permute-start.22) | collective-permute-done | bytes 884768 | tf_op jit(solution)/shard_map/ppermute | solution.py:475
  690.8 9.9 %collective-permute-done.28 = bf16[1,4,2,48,768]{4,3,2,1,0:T(8,128)(2,1)S(1)} collective-permute-done((bf16[1,4,2,48,768]{4,3,2,1,0:T(8,128)(2,1)S(1)}, bf16[1,4,2,48,768]{4,3,2,1,0:T(8,128)(2,1)S(1)}, u32[]{:S(2)}, u32[]{:S(2)}) %collective-permute-start.28) | collective-permute-done | bytes 589856 | tf_op jit(solution)/shard_map/ppermute | solution.py:475
  703.6 7.0 collective-permute-done.38
  726.2 3.7 collective-permute-start.31
  729.8 3.7 collective-permute-done.40
  734.2 3.3 collective-permute-start.34
  748.8 3.9 collective-permute-done.42
  753.6 5.5 add_convert_fusion.1
  762.9 4.1 add_convert_fusion
  772.1 18.1 %collective-permute-done.46 = bf16[2,4,2,48,768]{4,3,1,0,2:T(8,128)(2,1)} collective-permute-done((bf16[2,4,2,48,768]{4,3,1,0,2:T(8,128)(2,1)}, bf16[2,4,2,48,768]{4,3,1,0,2:T(8,128)(2,1)}, u32[]{:S(2)}, u32[]{:S(2)}) %collective-permute-start.46) | collective-permute-done | bytes 1179680 | tf_op jit(solution)/shard_map/ppermute | solution.py:475
  793.8 19.2 %collective-permute-done.56 = bf16[2,4,2,48,768]{4,3,1,0,2:T(8,128)(2,1)S(1)} collective-permute-done((bf16[2,4,2,48,768]{4,3,1,0,2:T(8,128)(2,1)S(1)}, bf16[2,4,2,48,768]{4,3,1,0,2:T(8,128)(2,1)S(1)}, u32[]{:S(2)}, u32[]{:S(2)}) %collective-permute-start.56) | collective-permute-done | bytes 1179680 | tf_op jit(solution)/shard_map/ppermute | solution.py:475
  815.1 3.9 collective-permute-done.47
  822.1 3.3 collective-permute-done.57
  840.1 4.7 collective-permute-done.60
  846.4 3.4 collective-permute-done.51
  849.9 4.7 collective-permute-start.54
  863.4 3.9 collective-permute-done.64
  (479 shorter events, 221.7 us)
Async XLA Ops:
  7.2 138.7 %all-gather.5.cloned.1.call-start = ((), (), s32[]{:S(2)}) async-start(), calls=%async_computation | async-start | bytes 14598144 | tf_op jit(solution)/shard_map/all_gather | solution.py:629
  33.4 217.5 %all-gather.7.cloned.1.call-start = ((), (), s32[]{:S(2)}) async-start(), calls=%async_computation.1 | async-start | bytes 14598144 | tf_op jit(solution)/shard_map/all_gather | solution.py:629
  35.3 16.2 %collective-permute-start = (bf16[1,3,768]{2,1,0:T(4,128)(2,1)S(1)}, bf16[1,3,768]{2,1,0:T(4,128)(2,1)S(1)}, u32[]{:S(2)}, u32[]{:S(2)}) collective-permute-start(bf16[1,3,768]{2,1,0:T(4,128)(2,1)S(1)} %fusion.74), channel_id=1, source_target_pairs={{0,1},{1,0},{2,3},{3,2},{4,5},{5,4},{6,7},{7,6},{8,9},{9,8},{10,11... | collective-permute-start | bytes 13832 | tf_op jit(solution)/shard_map/ppermute | solution.py:475
  62.6 11.0 %collective-permute-start.19 = (bf16[1,8,3,768]{3,2,1,0:T(4,128)(2,1)S(1)}, bf16[1,8,3,768]{3,2,1,0:T(4,128)(2,1)S(1)}, u32[]{:S(2)}, u32[]{:S(2)}) collective-permute-start(bf16[1,8,3,768]{3,2,1,0:T(4,128)(2,1)S(1)} %fusion.111), channel_id=1, source_target_pairs={{0,8},{8,0},{16,24},{24,16},{1,9},{9,1},{17,25},{25,17},{2,10},{10... | collective-permute-start | bytes 110600 | tf_op jit(solution)/shard_map/ppermute | solution.py:475
  65.1 23.7 %collective-permute-start.4 = (f32[2,3,2,4608]{3,1,2,0:T(4,128)S(1)}, f32[2,3,2,4608]{3,1,2,0:T(4,128)S(1)}, u32[]{:S(2)}, u32[]{:S(2)}) collective-permute-start(f32[2,3,2,4608]{3,1,2,0:T(4,128)S(1)} %bitcast.590), channel_id=1, source_target_pairs={{0,2},{1,3},{2,0},{3,1},{4,6},{5,7},{6,4},{7,5},{8,10},{9,11},{10,... | collective-permute-start | bytes 663560 | tf_op jit(solution)/shard_map/ppermute | solution.py:475
  73.7 15.5 %collective-permute-start.20 = (bf16[2,8,3,768]{3,2,1,0:T(4,128)(2,1)S(1)}, bf16[2,8,3,768]{3,2,1,0:T(4,128)(2,1)S(1)}, u32[]{:S(2)}, u32[]{:S(2)}) collective-permute-start(bf16[2,8,3,768]{3,2,1,0:T(4,128)(2,1)S(1)} %pad_maximum_fusion.20), channel_id=1, source_target_pairs={{0,16},{8,24},{16,0},{24,8},{1,17},{9,25},{17,1},{25,9},{2,18},{10... | collective-permute-start | bytes 221192 | tf_op jit(solution)/shard_map/ppermute | solution.py:475
  89.0 10.7 %collective-permute-start.5 = (f32[1,3,2,4608]{3,1,2,0:T(4,128)S(1)}, f32[1,3,2,4608]{3,1,2,0:T(4,128)S(1)}, u32[]{:S(2)}, u32[]{:S(2)}) collective-permute-start(f32[1,3,2,4608]{3,1,2,0:T(4,128)S(1)} %slice_bitcast_fusion.46), channel_id=1, source_target_pairs={{0,4},{1,5},{2,6},{3,7},{4,0},{5,1},{6,2},{7,3},{8,12},{9,13},{10,... | collective-permute-start | bytes 331784 | tf_op jit(solution)/shard_map/ppermute | solution.py:475
  485.6 75.6 %collective-permute-start.9 = (f32[1,3,4608]{2,1,0:T(4,128)S(1)}, f32[1,3,4608]{2,1,0:T(4,128)S(1)}, u32[]{:S(2)}, u32[]{:S(2)}) collective-permute-start(f32[1,3,4608]{2,1,0:T(4,128)S(1)} %broadcast_in_dim_reshape.7), channel_id=1, source_target_pairs={{0,1},{1,0},{2,3},{3,2},{4,5},{5,4},{6,7},{7,6},{8,9},{9,8},{10,11... | collective-permute-start | bytes 165896 | tf_op jit(solution)/shard_map/ppermute | solution.py:475
  486.0 76.5 %collective-permute-start.6 = (f32[1,3,4608]{2,1,0:T(4,128)S(1)}, f32[1,3,4608]{2,1,0:T(4,128)S(1)}, u32[]{:S(2)}, u32[]{:S(2)}) collective-permute-start(f32[1,3,4608]{2,1,0:T(4,128)S(1)} %broadcast_in_dim_reshape.6), channel_id=1, source_target_pairs={{0,1},{1,0},{2,3},{3,2},{4,5},{5,4},{6,7},{7,6},{8,9},{9,8},{10,11... | collective-permute-start | bytes 165896 | tf_op jit(solution)/shard_map/ppermute | solution.py:475
  534.3 146.8 %collective-permute-start.25 = (bf16[1,4,4,96,768]{4,3,2,1,0:T(8,128)(2,1)}, bf16[1,4,4,96,768]{4,3,2,1,0:T(8,128)(2,1)}, u32[]{:S(2)}, u32[]{:S(2)}) collective-permute-start(bf16[1,4,4,96,768]{4,3,2,1,0:T(8,128)(2,1)} %get-tuple-element.103), channel_id=1, source_target_pairs={{0,1},{1,0},{2,3},{3,2},{4,5},{5,4},{6,7},{7,6},{8,9},{9,8},{10,11... | collective-permute-start | bytes 7077896 | tf_op jit(solution)/shard_map/ppermute | solution.py:475
  540.0 147.6 %collective-permute-start.35 = (bf16[1,4,4,96,768]{4,3,2,1,0:T(8,128)(2,1)}, bf16[1,4,4,96,768]{4,3,2,1,0:T(8,128)(2,1)}, u32[]{:S(2)}, u32[]{:S(2)}) collective-permute-start(bf16[1,4,4,96,768]{4,3,2,1,0:T(8,128)(2,1)} %get-tuple-element.106), channel_id=1, source_target_pairs={{0,1},{1,0},{2,3},{3,2},{4,5},{5,4},{6,7},{7,6},{8,9},{9,8},{10,11... | collective-permute-start | bytes 7077896 | tf_op jit(solution)/shard_map/ppermute | solution.py:475
  550.8 202.8 %collective-permute-start.45 = (bf16[2,4,4,96,768]{4,3,2,1,0:T(8,128)(2,1)}, bf16[2,4,4,96,768]{4,3,2,1,0:T(8,128)(2,1)}, u32[]{:S(2)}, u32[]{:S(2)}) collective-permute-start(bf16[2,4,4,96,768]{4,3,2,1,0:T(8,128)(2,1)} %get-tuple-element.109), channel_id=1, source_target_pairs={{0,1},{1,0},{2,3},{3,2},{4,5},{5,4},{6,7},{7,6},{8,9},{9,8},{10,11... | collective-permute-start | bytes 14155784 | tf_op jit(solution)/shard_map/ppermute | solution.py:475
  562.6 8.0 collective-permute-start.7
  568.0 22.8 %collective-permute-start.11 = (f32[4,3,4608]{2,1,0:T(4,128)S(1)}, f32[4,3,4608]{2,1,0:T(4,128)S(1)}, u32[]{:S(2)}, u32[]{:S(2)}) collective-permute-start(f32[4,3,4608]{2,1,0:T(4,128)S(1)} %pad_maximum_fusion.16), channel_id=1, source_target_pairs={{0,4},{1,5},{2,6},{3,7},{4,0},{5,1},{6,2},{7,3},{8,12},{9,13},{10,... | collective-permute-start | bytes 663560 | tf_op jit(solution)/shard_map/ppermute | solution.py:475
  571.4 24.8 %collective-permute-start.8 = (f32[4,3,4608]{2,1,0:T(4,128)}, f32[4,3,4608]{2,1,0:T(4,128)}, u32[]{:S(2)}, u32[]{:S(2)}) collective-permute-start(f32[4,3,4608]{2,1,0:T(4,128)} %pad_maximum_fusion.15), channel_id=1, source_target_pairs={{0,4},{1,5},{2,6},{3,7},{4,0},{5,1},{6,2},{7,3},{8,12},{9,13},{10,... | collective-permute-start | bytes 663560 | tf_op jit(solution)/shard_map/ppermute | solution.py:475
  612.0 13.3 %collective-permute-start.23 = (f32[1,8,3,4608]{3,1,2,0:T(8,128)S(1)}, f32[1,8,3,4608]{3,1,2,0:T(8,128)S(1)}, u32[]{:S(2)}, u32[]{:S(2)}) collective-permute-start(f32[1,8,3,4608]{3,1,2,0:T(8,128)S(1)} %copy.158), channel_id=1, source_target_pairs={{0,8},{8,0},{16,24},{24,16},{1,9},{9,1},{17,25},{25,17},{2,10},{10... | collective-permute-start | bytes 1327112 | tf_op jit(solution)/shard_map/ppermute | solution.py:475
  614.2 18.4 %collective-permute-start.21 = (f32[1,8,3,4608]{3,1,2,0:T(8,128)S(1)}, f32[1,8,3,4608]{3,1,2,0:T(8,128)S(1)}, u32[]{:S(2)}, u32[]{:S(2)}) collective-permute-start(f32[1,8,3,4608]{3,1,2,0:T(8,128)S(1)} %copy.153), channel_id=1, source_target_pairs={{0,8},{8,0},{16,24},{24,16},{1,9},{9,1},{17,25},{25,17},{2,10},{10... | collective-permute-start | bytes 1327112 | tf_op jit(solution)/shard_map/ppermute | solution.py:475
  627.0 22.9 %collective-permute-start.24 = (f32[2,8,3,4608]{3,1,2,0:T(8,128)}, f32[2,8,3,4608]{3,1,2,0:T(8,128)S(1)}, u32[]{:S(2)}, u32[]{:S(2)}) collective-permute-start(f32[2,8,3,4608]{3,1,2,0:T(8,128)} %copy.157), channel_id=1, source_target_pairs={{0,16},{8,24},{16,0},{24,8},{1,17},{9,25},{17,1},{25,9},{2,18},{10... | collective-permute-start | bytes 2654216 | tf_op jit(solution)/shard_map/ppermute | solution.py:475
  634.3 29.3 %collective-permute-start.22 = (f32[2,8,3,4608]{3,1,2,0:T(8,128)}, f32[2,8,3,4608]{3,1,2,0:T(8,128)}, u32[]{:S(2)}, u32[]{:S(2)}) collective-permute-start(f32[2,8,3,4608]{3,1,2,0:T(8,128)} %copy.152), channel_id=1, source_target_pairs={{0,16},{8,24},{16,0},{24,8},{1,17},{9,25},{17,1},{25,9},{2,18},{10... | collective-permute-start | bytes 2654216 | tf_op jit(solution)/shard_map/ppermute | solution.py:475
  649.9 113.1 %collective-permute-start.55 = (bf16[2,4,4,96,768]{4,3,2,1,0:T(8,128)(2,1)}, bf16[2,4,4,96,768]{4,3,2,1,0:T(8,128)(2,1)}, u32[]{:S(2)}, u32[]{:S(2)}) collective-permute-start(bf16[2,4,4,96,768]{4,3,2,1,0:T(8,128)(2,1)} %get-tuple-element.112), channel_id=1, source_target_pairs={{0,1},{1,0},{2,3},{3,2},{4,5},{5,4},{6,7},{7,6},{8,9},{9,8},{10,11... | collective-permute-start | bytes 14155784 | tf_op jit(solution)/shard_map/ppermute | solution.py:475
  684.4 16.3 %collective-permute-start.28 = (bf16[1,4,2,48,768]{4,3,2,1,0:T(8,128)(2,1)S(1)}, bf16[1,4,2,48,768]{4,3,2,1,0:T(8,128)(2,1)S(1)}, u32[]{:S(2)}, u32[]{:S(2)}) collective-permute-start(bf16[1,4,2,48,768]{4,3,2,1,0:T(8,128)(2,1)S(1)} %slice_bitcast_fusion.14), channel_id=1, source_target_pairs={{0,16},{8,24},{16,0},{24,8},{1,17},{9,25},{17,1},{25,9},{2,18},{10... | collective-permute-start | bytes 1769480 | tf_op jit(solution)/shard_map/ppermute | solution.py:475
  686.0 15.9 %collective-permute-start.26 = (bf16[1,4,2,48,768]{4,3,2,1,0:T(8,128)(2,1)S(1)}, bf16[1,4,2,48,768]{4,3,2,1,0:T(8,128)(2,1)S(1)}, u32[]{:S(2)}, u32[]{:S(2)}) collective-permute-start(bf16[1,4,2,48,768]{4,3,2,1,0:T(8,128)(2,1)S(1)} %slice_bitcast_fusion.16), channel_id=1, source_target_pairs={{0,8},{8,0},{16,24},{24,16},{1,9},{9,1},{17,25},{25,17},{2,10},{10... | collective-permute-start | bytes 1769480 | tf_op jit(solution)/shard_map/ppermute | solution.py:475
  690.2 20.4 %collective-permute-start.38 = (bf16[1,4,2,48,768]{4,3,2,1,0:T(8,128)(2,1)S(1)}, bf16[1,4,2,48,768]{4,3,2,1,0:T(8,128)(2,1)S(1)}, u32[]{:S(2)}, u32[]{:S(2)}) collective-permute-start(bf16[1,4,2,48,768]{4,3,2,1,0:T(8,128)(2,1)S(1)} %slice_bitcast_fusion.10), channel_id=1, source_target_pairs={{0,16},{8,24},{16,0},{24,8},{1,17},{9,25},{17,1},{25,9},{2,18},{10... | collective-permute-start | bytes 1769480 | tf_op jit(solution)/shard_map/ppermute | solution.py:475
  700.7 14.2 %collective-permute-start.36 = (bf16[1,4,2,48,768]{4,3,2,1,0:T(8,128)(2,1)S(1)}, bf16[1,4,2,48,768]{4,3,2,1,0:T(8,128)(2,1)S(1)}, u32[]{:S(2)}, u32[]{:S(2)}) collective-permute-start(bf16[1,4,2,48,768]{4,3,2,1,0:T(8,128)(2,1)S(1)} %slice_bitcast_fusion.12), channel_id=1, source_target_pairs={{0,8},{8,0},{16,24},{24,16},{1,9},{9,1},{17,25},{25,17},{2,10},{10... | collective-permute-start | bytes 1769480 | tf_op jit(solution)/shard_map/ppermute | solution.py:475
  701.9 16.2 %collective-permute-start.29 = (bf16[1,4,1,48,768]{4,3,1,2,0:T(8,128)(2,1)S(1)}, bf16[1,4,1,48,768]{4,3,1,2,0:T(8,128)(2,1)S(1)}, u32[]{:S(2)}, u32[]{:S(2)}) collective-permute-start(bf16[1,4,1,48,768]{4,3,1,2,0:T(8,128)(2,1)S(1)} %slice_bitcast_fusion.32), channel_id=1, source_target_pairs={{0,8},{8,0},{16,24},{24,16},{1,9},{9,1},{17,25},{25,17},{2,10},{10... | collective-permute-start | bytes 884744 | tf_op jit(solution)/shard_map/ppermute | solution.py:475
  710.6 8.1 collective-permute-start.27
  718.8 7.3 collective-permute-start.30
  724.9 8.6 collective-permute-start.40
  726.2 8.0 collective-permute-start.31
  733.6 7.1 collective-permute-start.41
  734.2 6.8 collective-permute-start.34
  745.9 6.7 collective-permute-start.42
  761.0 29.2 %collective-permute-start.46 = (bf16[2,4,2,48,768]{4,3,1,0,2:T(8,128)(2,1)}, bf16[2,4,2,48,768]{4,3,1,0,2:T(8,128)(2,1)}, u32[]{:S(2)}, u32[]{:S(2)}) collective-permute-start(bf16[2,4,2,48,768]{4,3,1,0,2:T(8,128)(2,1)} %bitcast.504), channel_id=1, source_target_pairs={{0,8},{8,0},{16,24},{24,16},{1,9},{9,1},{17,25},{25,17},{2,10},{10... | collective-permute-start | bytes 3538952 | tf_op jit(solution)/shard_map/ppermute | solution.py:475
  762.4 29.5 %collective-permute-start.48 = (bf16[2,4,2,48,768]{4,3,1,0,2:T(8,128)(2,1)}, bf16[2,4,2,48,768]{4,3,1,0,2:T(8,128)(2,1)S(1)}, u32[]{:S(2)}, u32[]{:S(2)}) collective-permute-start(bf16[2,4,2,48,768]{4,3,1,0,2:T(8,128)(2,1)} %bitcast.503), channel_id=1, source_target_pairs={{0,16},{8,24},{16,0},{24,8},{1,17},{9,25},{17,1},{25,9},{2,18},{10... | collective-permute-start | bytes 3538952 | tf_op jit(solution)/shard_map/ppermute | solution.py:475
  768.3 44.7 %collective-permute-start.56 = (bf16[2,4,2,48,768]{4,3,1,0,2:T(8,128)(2,1)S(1)}, bf16[2,4,2,48,768]{4,3,1,0,2:T(8,128)(2,1)S(1)}, u32[]{:S(2)}, u32[]{:S(2)}) collective-permute-start(bf16[2,4,2,48,768]{4,3,1,0,2:T(8,128)(2,1)S(1)} %bitcast.577), channel_id=1, source_target_pairs={{0,8},{8,0},{16,24},{24,16},{1,9},{9,1},{17,25},{25,17},{2,10},{10... | collective-permute-start | bytes 3538952 | tf_op jit(solution)/shard_map/ppermute | solution.py:475
  770.0 44.1 %collective-permute-start.58 = (bf16[2,4,2,48,768]{4,3,1,0,2:T(8,128)(2,1)S(1)}, bf16[2,4,2,48,768]{4,3,1,0,2:T(8,128)(2,1)S(1)}, u32[]{:S(2)}, u32[]{:S(2)}) collective-permute-start(bf16[2,4,2,48,768]{4,3,1,0,2:T(8,128)(2,1)S(1)} %bitcast.576), channel_id=1, source_target_pairs={{0,16},{8,24},{16,0},{24,8},{1,17},{9,25},{17,1},{25,9},{2,18},{10... | collective-permute-start | bytes 3538952 | tf_op jit(solution)/shard_map/ppermute | solution.py:475
  791.8 27.2 %collective-permute-start.47 = (bf16[2,4,1,48,768]{4,3,1,0,2:T(8,128)(2,1)S(1)}, bf16[2,4,1,48,768]{4,3,1,0,2:T(8,128)(2,1)S(1)}, u32[]{:S(2)}, u32[]{:S(2)}) collective-permute-start(bf16[2,4,1,48,768]{4,3,1,0,2:T(8,128)(2,1)S(1)} %slice_bitcast_fusion.8), channel_id=1, source_target_pairs={{0,16},{8,24},{16,0},{24,8},{1,17},{9,25},{17,1},{25,9},{2,18},{10... | collective-permute-start | bytes 1769480 | tf_op jit(solution)/shard_map/ppermute | solution.py:475
  792.3 27.1 %collective-permute-start.49 = (bf16[2,4,1,48,768]{4,3,1,0,2:T(8,128)(2,1)S(1)}, bf16[2,4,1,48,768]{4,3,1,0,2:T(8,128)(2,1)S(1)}, u32[]{:S(2)}, u32[]{:S(2)}) collective-permute-start(bf16[2,4,1,48,768]{4,3,1,0,2:T(8,128)(2,1)S(1)} %slice_bitcast_fusion.6), channel_id=1, source_target_pairs={{0,8},{8,0},{16,24},{24,16},{1,9},{9,1},{17,25},{25,17},{2,10},{10... | collective-permute-start | bytes 1769480 | tf_op jit(solution)/shard_map/ppermute | solution.py:475
  813.4 12.0 %collective-permute-start.57 = (bf16[2,4,1,48,768]{4,3,1,0,2:T(8,128)(2,1)S(1)}, bf16[2,4,1,48,768]{4,3,1,0,2:T(8,128)(2,1)S(1)}, u32[]{:S(2)}, u32[]{:S(2)}) collective-permute-start(bf16[2,4,1,48,768]{4,3,1,0,2:T(8,128)(2,1)S(1)} %slice_bitcast_fusion.4), channel_id=1, source_target_pairs={{0,16},{8,24},{16,0},{24,8},{1,17},{9,25},{17,1},{25,9},{2,18},{10... | collective-permute-start | bytes 1769480 | tf_op jit(solution)/shard_map/ppermute | solution.py:475
  814.4 11.2 %collective-permute-start.59 = (bf16[2,4,1,48,768]{4,3,1,0,2:T(8,128)(2,1)S(1)}, bf16[2,4,1,48,768]{4,3,1,0,2:T(8,128)(2,1)S(1)}, u32[]{:S(2)}, u32[]{:S(2)}) collective-permute-start(bf16[2,4,1,48,768]{4,3,1,0,2:T(8,128)(2,1)S(1)} %slice_bitcast_fusion.2), channel_id=1, source_target_pairs={{0,8},{8,0},{16,24},{24,16},{1,9},{9,1},{17,25},{25,17},{2,10},{10... | collective-permute-start | bytes 1769480 | tf_op jit(solution)/shard_map/ppermute | solution.py:475
  821.2 16.3 %collective-permute-start.50 = (bf16[2,2,96,768]{3,2,0,1:T(8,128)(2,1)}, bf16[2,2,96,768]{3,2,0,1:T(8,128)(2,1)}, u32[]{:S(2)}, u32[]{:S(2)}) collective-permute-start(bf16[2,2,96,768]{3,2,0,1:T(8,128)(2,1)} %bitcast.508), channel_id=1, source_target_pairs={{0,2},{1,3},{2,0},{3,1},{4,6},{5,7},{6,4},{7,5},{8,10},{9,11},{10,... | collective-permute-start | bytes 1769480 | tf_op jit(solution)/shard_map/ppermute | solution.py:475
  827.6 17.2 %collective-permute-start.60 = (bf16[2,2,96,768]{3,2,0,1:T(8,128)(2,1)}, bf16[2,2,96,768]{3,2,0,1:T(8,128)(2,1)}, u32[]{:S(2)}, u32[]{:S(2)}) collective-permute-start(bf16[2,2,96,768]{3,2,0,1:T(8,128)(2,1)} %bitcast.507), channel_id=1, source_target_pairs={{0,2},{1,3},{2,0},{3,1},{4,6},{5,7},{6,4},{7,5},{8,10},{9,11},{10,... | collective-permute-start | bytes 1769480 | tf_op jit(solution)/shard_map/ppermute | solution.py:475
  839.0 10.8 %collective-permute-start.51 = (bf16[2,1,96,768]{3,2,0,1:T(8,128)(2,1)S(1)}, bf16[2,1,96,768]{3,2,0,1:T(8,128)(2,1)S(1)}, u32[]{:S(2)}, u32[]{:S(2)}) collective-permute-start(bf16[2,1,96,768]{3,2,0,1:T(8,128)(2,1)S(1)} %slice_bitcast_fusion.24), channel_id=1, source_target_pairs={{0,4},{1,5},{2,6},{3,7},{4,0},{5,1},{6,2},{7,3},{8,12},{9,13},{10,... | collective-permute-start | bytes 884744 | tf_op jit(solution)/shard_map/ppermute | solution.py:475
  846.2 10.4 %collective-permute-start.61 = (bf16[2,1,96,768]{3,2,0,1:T(8,128)(2,1)S(1)}, bf16[2,1,96,768]{3,2,0,1:T(8,128)(2,1)S(1)}, u32[]{:S(2)}, u32[]{:S(2)}) collective-permute-start(bf16[2,1,96,768]{3,2,0,1:T(8,128)(2,1)S(1)} %slice_bitcast_fusion.22), channel_id=1, source_target_pairs={{0,4},{1,5},{2,6},{3,7},{4,0},{5,1},{6,2},{7,3},{8,12},{9,13},{10,... | collective-permute-start | bytes 884744 | tf_op jit(solution)/shard_map/ppermute | solution.py:475
  849.9 10.3 %collective-permute-start.54 = (bf16[2,96,768]{2,1,0:T(8,128)(2,1)S(1)}, bf16[2,96,768]{2,1,0:T(8,128)(2,1)S(1)}, u32[]{:S(2)}, u32[]{:S(2)}) collective-permute-start(bf16[2,96,768]{2,1,0:T(8,128)(2,1)S(1)} %get-tuple-element.176), channel_id=1, source_target_pairs={{0,24},{8,16},{16,8},{24,0},{1,25},{9,17},{17,9},{25,1},{2,26},{10... | collective-permute-start | bytes 884744 | tf_op jit(solution)/shard_map/ppermute | solution.py:475
  857.4 10.0 %collective-permute-start.64 = (bf16[2,96,768]{2,1,0:T(8,128)(2,1)S(1)}, bf16[2,96,768]{2,1,0:T(8,128)(2,1)S(1)}, u32[]{:S(2)}, u32[]{:S(2)}) collective-permute-start(bf16[2,96,768]{2,1,0:T(8,128)(2,1)S(1)} %get-tuple-element.178), channel_id=1, source_target_pairs={{0,24},{8,16},{16,8},{24,0},{1,25},{9,17},{17,9},{25,1},{2,26},{10... | collective-permute-start | bytes 884744 | tf_op jit(solution)/shard_map/ppermute | solution.py:475
  860.2 9.9 %collective-permute-start.63 = (bf16[2,96,768]{2,1,0:T(8,128)(2,1)S(1)}, bf16[2,96,768]{2,1,0:T(8,128)(2,1)S(1)}, u32[]{:S(2)}, u32[]{:S(2)}) collective-permute-start(bf16[2,96,768]{2,1,0:T(8,128)(2,1)S(1)} %get-tuple-element.178), channel_id=1, source_target_pairs={{0,16},{8,24},{16,0},{24,8},{1,17},{9,25},{17,1},{25,9},{2,18},{10... | collective-permute-start | bytes 884744 | tf_op jit(solution)/shard_map/ppermute | solution.py:475
  860.2 9.9 %collective-permute-start.62 = (bf16[2,96,768]{2,1,0:T(8,128)(2,1)S(1)}, bf16[2,96,768]{2,1,0:T(8,128)(2,1)S(1)}, u32[]{:S(2)}, u32[]{:S(2)}) collective-permute-start(bf16[2,96,768]{2,1,0:T(8,128)(2,1)S(1)} %get-tuple-element.178), channel_id=1, source_target_pairs={{0,8},{8,0},{16,24},{24,16},{1,9},{9,1},{17,25},{25,17},{2,10},{10... | collective-permute-start | bytes 884744 | tf_op jit(solution)/shard_map/ppermute | solution.py:475
  (63 other events, 463.9 us)
Sparse Core Ops, SparseCore 0:
  33.5 112.3 all-gather.4
  149.5 101.4 all-gather.6

commit v2 on v1

--- a/solution.py
+++ b/solution.py
@@ -70,6 +70,18 @@
     )
 
 
+def slab(ref):
+    return ref[0].reshape(ref.shape[3], ref.shape[3])
+
+
+def tall(ref):
+    if ref.shape[0] == 1:
+        return slab(ref)
+    return jnp.concatenate(
+        [ref[r, s] for s in range(ref.shape[1]) for r in range(ref.shape[0])], axis=0
+    )
+
+
 def qkv_kernel(x_ref, mod_ref, w_ref, b_ref, u_ref, qkv_ref):
     latents, seq, _ = x_ref.shape
 
@@ -83,7 +95,7 @@
 
     for i in range(latents):
         part = slice(i * seq, (i + 1) * seq)
-        qkv_ref[0, part] = (nn(u_ref[part], w_ref[0]) + b_ref[0]).astype(low_type)
+        qkv_ref[0, part] = (nn(u_ref[part], slab(w_ref)) + b_ref[0]).astype(low_type)
 
 
 def mix_kernel(qkv_ref, x_ref, mod_ref, w_ref, b_ref, o_ref, a_ref, x1_ref, u2_ref):
@@ -102,7 +114,7 @@
             probs = top * (1.0 / jnp.sum(top, axis=-1, keepdims=True))
             mixed.append(nn(probs.astype(low_type), value))
         o_ref[:, at : at + pair] = jnp.where(left, mixed[0], mixed[1]).astype(low_type)
-    branch = nn(o_ref[...], w_ref[0]) + b_ref[...]
+    branch = nn(o_ref[...], slab(w_ref)) + b_ref[...]
     a_ref[...] = branch
     middle = x_ref[0] + mod_ref[0, 2:3] * branch
     x1_ref[...] = middle
@@ -120,9 +132,10 @@
     latents = mod_ref.shape[0]
     seq = u2_ref.shape[0] // latents
     step = pl.program_id(0)
+    down = tall(down_ref)
     for i in range(latents):
         part = slice(i * seq, (i + 1) * seq)
-        pre = nn(u2_ref[part], up_ref[0]) + upb_ref[0]
+        pre = nn(u2_ref[part], slab(up_ref)) + upb_ref[0]
         square = pre * pre
         bent = jnp.tanh(GELU_SCALE * (pre + GELU_CUBE * (square * pre)))
         half = 0.5 * (1.0 + bent)
@@ -135,7 +148,7 @@
             * (1.0 - bent * bent)
             * (1.0 + (3.0 * GELU_CUBE) * square)
         ).astype(low_type)
-        part_sum = nn(act, down_ref[0])
+        part_sum = nn(act, down)
 
         @pl.when(step == 0)
         def _():
@@ -150,10 +163,23 @@
             x_ref[part] = x1_ref[part] + mod_ref[i, 5:6] * m_ref[part]
 
 
+def store_slab(here_ref, product, kept_ref, sent_ref, hold_ref):
+    hold_ref[...] = product.astype(low_type).reshape(hold_ref.shape)
+    for near in range(kept_ref.shape[0]):
+        owner = jnp.bitwise_xor(here_ref[0], 2 * near)
+        kept_ref[near, 0] = hold_ref[owner]
+        sent_ref[near, 0] = hold_ref[jnp.bitwise_xor(owner, 1)]
+
+
 def feed_back_kernel(
-    dy_ref, m_ref, mod_ref, u2_ref, g_ref, slope_ref, up_ref, down_ref,
-    gw_ref, du_ref, dgate_ref, downb_ref, upb_ref, dm_ref, df_ref,
+    fused, here_ref, dy_ref, m_ref, mod_ref, u2_ref, g_ref, slope_ref, up_ref, down_ref,
+    *refs,
 ):
+    if fused:
+        up_grads, down_grads, refs = refs[:2], refs[2:4], refs[4:]
+    else:
+        up_grad, down_grad, refs = refs[0], refs[1], refs[2:]
+    du_ref, dgate_ref, downb_ref, upb_ref, dm_ref, df_ref, hold_ref = refs
     latents = mod_ref.shape[0]
     seq = u2_ref.shape[0] // latents
     step = pl.program_id(0)
@@ -171,12 +197,13 @@
         downb_ref[...] = total
 
     sums = jnp.zeros(upb_ref.shape[1:], wide)
+    down = tall(down_ref)
     for i in range(latents):
         part = slice(i * seq, (i + 1) * seq)
-        lower = (nt(dm_ref[part], down_ref[0]) * slope_ref[0, part].astype(wide)).astype(low_type)
+        lower = (nt(dm_ref[part], down) * slope_ref[0, part].astype(wide)).astype(low_type)
         df_ref[part] = lower
         sums += jnp.sum(lower.astype(wide), axis=0, keepdims=True)
-        back = nt(lower, up_ref[0])
+        back = nt(lower, slab(up_ref))
 
         @pl.when(step == 0)
         def _():
@@ -187,8 +214,20 @@
             du_ref[part] = du_ref[part] + back
 
     upb_ref[0] = sums
-    gw_ref[0, 0] = tn(g_ref[0], dm_ref[...]).astype(low_type)
-    gw_ref[1, 0] = tn(u2_ref[...], df_ref[...]).astype(low_type)
+    down_part = tn(g_ref[0], dm_ref[...])
+    up_part = tn(u2_ref[...], df_ref[...])
+    if not fused:
+        down_grad[0] = down_part.astype(low_type)
+        up_grad[0] = up_part.astype(low_type)
+        return
+    store_slab(here_ref, up_part, up_grads[0], up_grads[1], hold_ref)
+    hold_ref[...] = down_part.astype(low_type).reshape(hold_ref.shape)
+    places = down_grads[0].shape[1]
+    low = here_ref[0] % 2
+    for place in range(places):
+        piece = jnp.bitwise_xor(here_ref[1], place)
+        down_grads[0][0, place] = hold_ref[low * places + piece]
+        down_grads[1][0, place] = hold_ref[(1 - low) * places + piece]
 
 
 def mix_back_kernel(
@@ -205,7 +244,7 @@
     dmod_ref[0, 2:3] = jnp.sum(dx1 * a_ref[...], axis=0, keepdims=True)
     da = (dx1 * mod_ref[0, 2:3]).astype(low_type)
     dall_ref[3] = da
-    do_ref[...] = nt(da, w_ref[0]).astype(low_type)
+    do_ref[...] = nt(da, slab(w_ref)).astype(low_type)
     lane = lax.broadcasted_iota(jnp.int32, (seq, pair), 1)
     left = lane < HEAD_DIM
     for at in range(0, width, pair):
@@ -241,17 +280,26 @@
 
 
 def qkv_back_kernel(
-    u1_ref, o_ref, dall_ref, w_ref, x_ref, dx1_ref, mod_ref, gw_ref, dx_ref, dmod_ref, acc_ref
+    fused, here_ref, u1_ref, o_ref, dall_ref, w_ref, x_ref, dx1_ref, mod_ref, *refs
 ):
+    grads = refs[:2] if fused else refs[:1]
+    dx_ref, dmod_ref, acc_ref, hold_ref = refs[len(grads) :]
+
+    def store(product):
+        if fused:
+            store_slab(here_ref, product, grads[0], grads[1], hold_ref)
+        else:
+            grads[0][0] = product.astype(low_type)
+
     latents, seq, _ = x_ref.shape
     step = pl.program_id(0)
 
     @pl.when(step < 3)
     def _():
-        gw_ref[0] = tn(u1_ref[...], dall_ref[0]).astype(low_type)
+        store(tn(u1_ref[...], dall_ref[0]))
         for i in range(latents):
             part = slice(i * seq, (i + 1) * seq)
-            back = nt(dall_ref[0, part], w_ref[0])
+            back = nt(dall_ref[0, part], slab(w_ref))
 
             @pl.when(step == 0)
             def _():
@@ -263,7 +311,7 @@
 
     @pl.when(step == 3)
     def _():
-        gw_ref[0] = tn(o_ref[...], dall_ref[0]).astype(low_type)
+        store(tn(o_ref[...], dall_ref[0]))
         for i in range(latents):
             part = slice(i * seq, (i + 1) * seq)
             back, dshift, dscale = norm_back(acc_ref[part], x_ref[i], mod_ref[i, 1:2])
@@ -277,42 +325,76 @@
 
 
 def full(dims):
-    return pl.BlockSpec(tuple(dims), lambda step: (0,) * len(dims))
+    return pl.BlockSpec(tuple(dims), lambda step, here_ref: (0,) * len(dims))
 
 
 def along(dims, where):
     return pl.BlockSpec(
-        tuple(dims), lambda step: tuple(step if i == where else 0 for i in range(len(dims)))
-    )
-
-
-def call(kernel, grid, in_specs, out_specs, out_shape, scratch, flops, moved):
-    return pl.pallas_call(
-        kernel,
-        grid=(grid,),
-        in_specs=in_specs,
-        out_specs=out_specs,
+        tuple(dims),
+        lambda step, here_ref: tuple(step if i == where else 0 for i in range(len(dims))),
+    )
+
+
+def slab_spec(weight, fixed=None):
+    array, kind = weight
+    _, shards, _, rows, width = array.shape
+    return pl.BlockSpec(
+        (1, shards, None, rows, width),
+        lambda step, here_ref: (step if fixed is None else fixed, 0, kind, 0, 0),
+    )
+
+
+def tall_spec(weight):
+    array, kind = weight
+    slabs, shards, _, rows, width = array.shape
+    if shards == 1:
+        return slab_spec(weight)
+    return pl.BlockSpec(
+        (slabs, shards // slabs, None, rows, width), lambda step, here_ref: (0, step, kind, 0, 0)
+    )
+
+
+def call(
+    kernel, here, grid, in_specs, out_specs, out_shape, scratch, flops, moved, after=(), fused=None
+):
+    count = len(in_specs)
+
+    def body(here_ref, *refs):
+        lead = () if fused is None else (fused, here_ref)
+        kernel(*lead, *refs[:count], *refs[count + len(after) :])
+
+    run = pl.pallas_call(
+        body,
+        grid_spec=pltpu.PrefetchScalarGridSpec(
+            num_scalar_prefetch=1,
+            grid=(grid,),
+            in_specs=list(in_specs) + [pl.BlockSpec(memory_space=pl.ANY)] * len(after),
+            out_specs=out_specs,
+            scratch_shapes=scratch,
+        ),
         out_shape=out_shape,
-        scratch_shapes=scratch,
-        compiler_params=pltpu.CompilerParams(vmem_limit_bytes=56 * 2**20),
+        compiler_params=pltpu.CompilerParams(vmem_limit_bytes=58 * 2**20),
         cost_estimate=pl.CostEstimate(flops=flops, bytes_accessed=moved, transcendentals=0),
         name=kernel.__name__,
     )
-
-
-def forward_layer(hidden, mod, weights):
-    attn_w, up_w, down_w, qkv_b, proj_b, up_b, down_b = weights
+    return lambda *arrays: run(here, *arrays, *after)
+
+
+def forward_layer(here, hidden, mod, attn, feed, biases, slots):
+    qkv_b, proj_b, up_b, down_b = biases
+    attn_w, after = attn()
     latents, seq, width = hidden.shape
     rows = latents * seq
     unit = 2 * rows * width * width
     size = rows * width
     u1, qkv = call(
         qkv_kernel,
+        here,
         3,
         [
             full(hidden.shape),
             full(mod.shape),
-            along((1, width, width), 0),
+            slab_spec(attn_w),
             along((1, 1, width), 0),
         ],
         [full((rows, width)), along((1, rows, width), 0)],
@@ -320,16 +402,18 @@
         [],
         3 * unit,
         18 * size,
-    )(hidden, mod, attn_w, qkv_b)
+        after,
+    )(hidden, mod, attn_w[0], qkv_b)
     token = along((seq, width), 0)
     mixed, branch, middle, u2 = call(
         mix_kernel,
+        here,
         latents,
         [
             along((3, seq, width), 1),
             along((1, seq, width), 0),
             along((1, 6, width), 0),
-            pl.BlockSpec((1, width, width), lambda step: (3, 0, 0)),
+            slab_spec(attn_w, 3),
             full((1, width)),
         ],
         [token, token, token, token],
@@ -342,17 +426,20 @@
         [],
         5 * unit,
         24 * size,
-    )(qkv, hidden, mod, attn_w, proj_b)
+        slots(),
+    )(qkv, hidden, mod, attn_w[0], proj_b)
+    up_w, down_w, after = feed()
     act, slope, branch_two, result = call(
         feed_kernel,
+        here,
         SLABS,
         [
             full((rows, width)),
             full((rows, width)),
             full(mod.shape),
-            along((1, width, width), 0),
+            slab_spec(up_w),
             along((1, 1, width), 0),
-            along((1, width, width), 0),
+            tall_spec(down_w),
             full((1, width)),
         ],
         [
@@ -370,13 +457,14 @@
         [],
         12 * unit,
         40 * size,
-    )(u2, middle, mod, up_w, up_b, down_w, down_b)
+        after,
+    )(u2, middle, mod, up_w[0], up_b, down_w[0], down_b)
     saved = (hidden, mod, u1, qkv, mixed, branch, middle, u2, act, slope, branch_two)
-    return result.reshape(hidden.shape), saved
-
-
-def backward_layer(grad_out, weights, saved):
-    attn_w, up_w, down_w = weights[:3]
+    return result.reshape(hidden.shape), saved, (attn_w, up_w, down_w)
+
+
+def backward_layer(here, fused, grad_out, weights, saved, before, middle_slot, late_slot):
+    attn_w, up_w, down_w = weights
     hidden, mod, u1, qkv, mixed, branch, middle, u2, act, slope, branch_two = saved
     latents, seq, width = hidden.shape
     rows = latents * seq
@@ -384,33 +472,45 @@
     size = rows * width
     grad_out = grad_out.reshape(rows, width)
     block = along((1, rows, width), 0)
+    flat = full((rows, width))
     square = along((1, width, width), 0)
-    flat = full((rows, width))
-    ff_grads, du2, dgate_two, down_sums, up_sums = call(
+    _, shards, _, own, _ = attn_w[0].shape
+    near = shards // 2
+    by_place = pl.BlockSpec(
+        (near, 1, own, width),
+        lambda step, here_ref: (0, jnp.bitwise_xor(here_ref[1], step), 0, 0),
+    )
+    by_near = pl.BlockSpec(
+        (1, SLABS, own, width),
+        lambda step, here_ref: (jnp.bitwise_xor(here_ref[0] // 2, step), 0, 0, 0),
+    )
+    half = shape_of((near, SLABS, own, width), low_type)
+    natural = shape_of((SLABS, width, width), low_type)
+    hold = pltpu.VMEM((shards, own, width), low_type)
+    *ff_grads, du2, dgate_two, down_sums, up_sums = call(
         feed_back_kernel,
+        here,
         SLABS,
-        [flat, flat, full(mod.shape), flat, block, block, square, square],
-        [
-            along((2, 1, width, width), 1),
-            flat,
-            full((latents, 1, width)),
-            full((1, width)),
-            along((1, 1, width), 0),
-        ],
-        [
-            shape_of((2, SLABS, width, width), low_type),
+        [flat, flat, full(mod.shape), flat, block, block, slab_spec(up_w), tall_spec(down_w)],
+        ([by_place, by_place, by_near, by_near] if fused else [square, square])
+        + [flat, full((latents, 1, width)), full((1, width)), along((1, 1, width), 0)],
+        ([half] * 4 if fused else [natural] * 2)
+        + [
             shape_of((rows, width), wide),
             shape_of((latents, 1, width), wide),
             shape_of((1, width), wide),
             shape_of((SLABS, 1, width), wide),
         ],
-        [pltpu.VMEM((rows, width), low_type), pltpu.VMEM((rows, width), low_type)],
+        [pltpu.VMEM((rows, width), low_type), pltpu.VMEM((rows, width), low_type), hold],
         16 * unit,
         50 * size,
-    )(grad_out, branch_two, mod, u2, act, slope, up_w, down_w)
+        before,
+        fused,
+    )(grad_out, branch_two, mod, u2, act, slope, up_w[0], down_w[0])
     token = along((seq, width), 0)
     dx1, dall, dmod_mid, sums = call(
         mix_back_kernel,
+        here,
         latents,
         [
             token,
@@ -419,7 +519,7 @@
             token,
             along((3, seq, width), 1),
             along((1, 6, width), 0),
-            pl.BlockSpec((1, width, width), lambda step: (3, 0, 0)),
+            slab_spec(attn_w, 3),
         ],
         [
             token,
@@ -436,33 +536,27 @@
         [pltpu.VMEM((seq, width), low_type)],
         10 * unit,
         40 * size,
-    )(du2, middle, grad_out, branch, qkv, mod, attn_w)
-    at_grads, dx, dmod_low = call(
+        middle_slot(ff_grads),
+    )(du2, middle, grad_out, branch, qkv, mod, attn_w[0])
+    *at_grads, dx, dmod_low = call(
         qkv_back_kernel,
+        here,
         4,
-        [
-            flat,
-            flat,
-            block,
-            square,
-            full(hidden.shape),
-            flat,
-            full(mod.shape),
-        ],
-        [square, full(hidden.shape), full((latents, 2, width))],
-        [
-            shape_of((4, width, width), low_type),
-            shape_of(hidden.shape, wide),
-            shape_of((latents, 2, width), wide),
-        ],
-        [pltpu.VMEM((rows, width), wide)],
+        [flat, flat, block, slab_spec(attn_w), full(hidden.shape), flat, full(mod.shape)],
+        ([by_place, by_place] if fused else [square])
+        + [full(hidden.shape), full((latents, 2, width))],
+        ([half] * 2 if fused else [natural])
+        + [shape_of(hidden.shape, wide), shape_of((latents, 2, width), wide)],
+        [pltpu.VMEM((rows, width), wide), hold],
         7 * unit,
         36 * size,
-    )(u1, mixed, dall, attn_w, hidden, dx1, mod)
+        late_slot(sums, up_sums, down_sums),
+        fused,
+    )(u1, mixed, dall, attn_w[0], hidden, dx1, mod)
     dmod = jnp.concatenate(
         [dmod_low, dmod_mid[:, 2:3], dmod_mid[:, 0:2], dgate_two], axis=1
     ).reshape(latents, 6 * width)
-    return dx, dmod, ff_grads, at_grads, (sums, up_sums, down_sums)
+    return dx, dmod, at_grads
 
 
 class Net:
@@ -486,14 +580,36 @@
     def gather_rel(self, values, axes):
         stack = values[None]
         for axis in axes:
-            for step in self.bits(axis):
+            for step in self.bits(axis)[::-1]:
                 stack = jnp.concatenate([stack, self.swap(stack, axis, step)])
         return stack
 
+    def gather_steps(self, values, axis):
+        stack = values[None]
+        for step in self.bits(axis)[::-1]:
+            got = self.swap(stack, axis, step)
+            yield [stack]
+            stack = jnp.concatenate([stack, got])
+        return stack
+
+    def total_steps(self, values):
+        for axis in ("shard", "replica"):
+            for step in self.bits(axis):
+                got = self.swap(values, axis, step)
+                yield [values]
+                values = values + got
+        return values
+
+    def order(self, axis):
+        found = [0]
+        for step in self.bits(axis)[::-1]:
+            found = found + [place ^ step for place in found]
+        return found
+
     def scatter_rel(self, stack):
         for step in self.bits("shard"):
-            pairs = stack.reshape((stack.shape[0] // 2, 2) + stack.shape[1:])
-            stack = pairs[:, 0] + self.swap(pairs[:, 1], "shard", 1 * step)
+            half = stack.shape[0] // 2
+            stack = stack[:half] + self.swap(stack[half:], "shard", step)
         return stack[0]
 
 
@@ -561,29 +677,364 @@
     )
 
 
-def reduce_grads(net, here, grads):
-    keep, give = order_grads(net, here, grads)
-    total = add_low(keep, net.swap(give, "shard", 1))
-    groups, near, places, rows, width = total.shape
-    done = []
-    for part, order in ((0, 1), (1, -1)):
-        piece = total[:, :, :, part * (rows // 2) : (part + 1) * (rows // 2)]
-        left = list(range(places))
-        for step in net.bits("replica")[::order]:
-            where = sum(1 for q in left if q < step)
-            keep, give = halve(piece, 2, where)
-            left = [q for q in left if not q & step]
-            piece = add_low(keep, net.swap(give, "replica", step))
-        done.append(piece[:, :, 0])
-    total = jnp.concatenate(done, axis=2)
-    for step in net.bits("shard")[1:]:
-        keep, give = halve(total, 1, 1)
-        total = add_low(keep, net.swap(give, "shard", step))
-    mine = total[:, 0]
+def reduce_steps(net, here, pairs):
+    gots = [net.swap(give, "shard", 1) for _, give in pairs]
+    yield [give for _, give in pairs]
+    near, places, rows, width = pairs[0][0].shape
+    single = len(pairs) == 1
+    if single:
+        cuts = [slice(0, near // 2), slice(near // 2, near)]
+        parts = [add_low(pairs[0][0][cut], gots[0][cut]) for cut in cuts]
+    else:
+        parts = [add_low(keep, got) for (keep, _), got in zip(pairs, gots)]
+    lefts = [list(range(places))] * 2
+    for steps in zip(net.bits("replica"), net.bits("replica")[::-1]):
+        splits = []
+        for i, step in enumerate(steps):
+            where = sum(1 for q in lefts[i] if q < step)
+            splits.append(halve(parts[i], 1, where))
+            lefts[i] = [q for q in lefts[i] if not q & step]
+        gots = [net.swap(give, "replica", step) for (_, give), step in zip(splits, steps)]
+        yield [give for _, give in splits]
+        parts = [add_low(keep, got) for (keep, _), got in zip(splits, gots)]
+    parts = [part[:, 0] for part in parts]
+    steps = net.bits("shard")[1:]
+    for step in steps[:-1] if single else steps:
+        splits = [halve(part, 0, 1) for part in parts]
+        gots = [net.swap(give, "shard", step) for _, give in splits]
+        yield [give for _, give in splits]
+        parts = [add_low(keep, got) for (keep, _), got in zip(splits, gots)]
+    if single:
+        got = net.swap(parts[1], "shard", steps[-1])
+        yield [parts[1]]
+        mine = add_low(parts[0], got)
+    else:
+        mine = jnp.concatenate(parts)
     every = [mine] + [net.swap(mine, "replica", step) for step in range(1, places)]
-    stack = jnp.stack(every)
-    own = jnp.arange(places, dtype=jnp.int32)
-    return jnp.take(stack, jnp.bitwise_xor(own, here[1]), axis=0).astype(wide)
+    yield [mine]
+    return every
+
+
+class Part:
+    def __init__(self, keep, labels, route):
+        self.keep = keep
+        self.got = None
+        self.labels = labels
+        self.route = route
+
+
+class Fold:
+    def __init__(self, net, pairs):
+        self.net = net
+        near, places, rows, width = pairs[0][0].shape
+        ahead = [("replica", step) for step in net.bits("replica")]
+        behind = ahead[::-1]
+        shard_route = [("shard", step) for step in net.bits("shard")[1:]]
+        flat = (near * places, rows, width)
+        keeps = [keep.reshape(flat) for keep, _ in pairs]
+        gives = [give.reshape(flat) for _, give in pairs]
+        self.gots = [net.swap(give, "shard", 1) for give in gives]
+        self.sent = gives
+        labels = [(2 * t, q) for t in range(near) for q in range(places)]
+        self.single = len(pairs) == 1
+        if self.single:
+            half = len(labels) // 2
+            self.parts = [
+                Part((keeps[0], 0), labels[:half], ahead + shard_route[:-1]),
+                Part((keeps[0], half), labels[half:], behind + shard_route[:-1]),
+            ]
+            self.last = shard_route[-1]
+            for part, start in zip(self.parts, (0, half)):
+                part.got = (self.gots[0], start)
+        else:
+            self.parts = [
+                Part((keeps[0], 0), labels, ahead + shard_route),
+                Part((keeps[1], 0), labels, behind + shard_route),
+            ]
+            for part, got in zip(self.parts, self.gots):
+                part.got = (got, 0)
+        self.every = None
+        self.merge = False
+
+    def jobs(self):
+        if self.every is not None:
+            return [], []
+        first = self.parts[0]
+        rows, width = first.keep[0].shape[1:]
+        if self.merge or not first.route:
+            if self.single and not self.merge:
+                a, b = self.parts
+                return [(a, [0], 0), (b, [0], 1)], [(1, rows, width)] * 2
+            parts = self.parts[:1] if self.single else self.parts
+            jobs = [(part, [0], 0) for part in parts]
+            return jobs, [(len(parts), rows, width)]
+        jobs, outs = [], []
+        for part in self.parts:
+            axis, step = part.route[0]
+            which = 0 if axis == "shard" else 1
+            stay = [i for i, label in enumerate(part.labels) if not label[which] & step]
+            leave = [i for i, label in enumerate(part.labels) if label[which] & step]
+            for blocks in (stay, leave):
+                jobs.append((part, blocks, len(outs)))
+                outs.append((len(blocks), rows, width))
+        return jobs, outs
+
+    def take(self, outs):
+        if self.every is not None:
+            return []
+        net = self.net
+        if self.merge or not self.parts[0].route:
+            if self.single and not self.merge:
+                self.merge = True
+                axis, step = self.last
+                self.parts[0].keep = (outs[0], 0)
+                self.parts[0].got = (net.swap(outs[1], axis, step), 0)
+                return [outs[1]]
+            mine = outs[0]
+            self.every = [mine]
+            self.every += [net.swap(mine, "replica", step) for step in range(1, net.replicas)]
+            return [mine]
+        sent = []
+        for part, (keep, give) in zip(self.parts, zip(outs[::2], outs[1::2])):
+            (axis, step), part.route = part.route[0], part.route[1:]
+            which = 0 if axis == "shard" else 1
+            part.labels = [label for label in part.labels if not label[which] & step]
+            part.keep = (keep, 0)
+            part.got = (net.swap(give, axis, step), 0)
+            sent.append(give)
+        return sent
+
+
+def round_kernel(jobs, *refs):
+    place = [0] * 64
+    for keep, got, blocks, keep_at, got_at, out in jobs:
+        for block in blocks:
+            refs[out][place[out]] = (
+                refs[keep][keep_at + block].astype(wide) + refs[got][got_at + block].astype(wide)
+            ).astype(low_type)
+            place[out] += 1
+
+
+def run_round(folds, after=()):
+    arrays, jobs, shapes, counts = [], [], [], []
+
+    def slot(array):
+        for i, known in enumerate(arrays):
+            if known is array:
+                return i
+        arrays.append(array)
+        return len(arrays) - 1
+
+    listed = []
+    for fold in folds:
+        fold_jobs, outs = fold.jobs()
+        for part, blocks, out in fold_jobs:
+            keep, keep_at = part.keep
+            got, got_at = part.got
+            listed.append((slot(keep), slot(got), blocks, keep_at, got_at, len(shapes) + out))
+        shapes += outs
+        counts.append(len(outs))
+    if not shapes:
+        return []
+    first_out = len(arrays) + len(after)
+    jobs = [job[:5] + (first_out + job[5],) for job in listed]
+    outs = pl.pallas_call(
+        functools.partial(round_kernel, jobs),
+        in_specs=[pl.BlockSpec(memory_space=pltpu.VMEM)] * len(arrays)
+        + [pl.BlockSpec(memory_space=pl.ANY)] * len(after),
+        out_specs=[pl.BlockSpec(memory_space=pltpu.VMEM)] * len(shapes),
+        out_shape=[shape_of(dims, low_type) for dims in shapes],
+        compiler_params=pltpu.CompilerParams(vmem_limit_bytes=58 * 2**20),
+        name="round",
+    )(*arrays, *after)
+    sent = []
+    for fold, count in zip(folds, counts):
+        sent += fold.take(outs[:count])
+        outs = outs[count:]
+    return sent
+
+
+def finish_kernel(here_ref, *refs):
+    ins, (qkv_ref, proj_ref, up_ref, down_ref, at_ref, ff_ref) = refs[:-6], refs[-6:]
+    rows, width = proj_ref.shape[1:]
+    for layer in range(LAYERS):
+        at, ff = ins[:SLABS], ins[SLABS : 2 * SLABS]
+        ins = ins[2 * SLABS :]
+        for step in range(SLABS):
+            place = jnp.bitwise_xor(here_ref[1], step)
+            at_ref[place] = at[step][0]
+            ff_ref[place] = ff[step][...]
+        for place in range(SLABS):
+            cols = slice(place * width, (place + 1) * width)
+            if place < 3:
+                qkv_ref[layer, :, cols] = at_ref[place].astype(wide)
+            else:
+                proj_ref[layer] = at_ref[place].astype(wide)
+            up_ref[layer, :, cols] = ff_ref[place, 0].astype(wide)
+            down_ref[layer, place * rows : (place + 1) * rows] = ff_ref[place, 1].astype(wide)
+
+
+def finish(here, owned):
+    arrays = [part for at, ff in owned for part in (*at, *ff)]
+    rows, width = owned[0][0][0].shape[1:]
+    outs = [
+        shape_of((LAYERS, rows, 3 * width), wide),
+        shape_of((LAYERS, rows, width), wide),
+        shape_of((LAYERS, rows, SLABS * width), wide),
+        shape_of((LAYERS, SLABS * rows, width), wide),
+    ]
+    return pl.pallas_call(
+        finish_kernel,
+        grid_spec=pltpu.PrefetchScalarGridSpec(
+            num_scalar_prefetch=1,
+            grid=(1,),
+            in_specs=[full(part.shape) for part in arrays],
+            out_specs=[full(out.shape) for out in outs],
+            scratch_shapes=[
+                pltpu.VMEM((SLABS, rows, width), low_type),
+                pltpu.VMEM((SLABS, 2, rows, width), low_type),
+            ],
+        ),
+        out_shape=outs,
+        compiler_params=pltpu.CompilerParams(vmem_limit_bytes=58 * 2**20),
+        name="finish",
+    )(here, *arrays)
+
+
+def finish_plain(here, owned, places):
+    found = [[], [], [], []]
+    order = jnp.bitwise_xor(jnp.arange(places, dtype=jnp.int32), here[1])
+    for at, ff in owned:
+        at = jnp.take(jnp.stack(at), order, axis=0)[:, 0].astype(wide)
+        ff = jnp.take(jnp.stack(ff), order, axis=0).transpose(1, 0, 2, 3).astype(wide)
+        width = at.shape[-1]
+        at = at.reshape(SLABS, -1, width)
+        ff = ff.reshape(2, SLABS, -1, width)
+        rows = at.shape[1]
+        found[0].append(at[:3].transpose(1, 0, 2).reshape(rows, 3 * width))
+        found[1].append(at[3])
+        found[2].append(ff[0].transpose(1, 0, 2).reshape(rows, SLABS * width))
+        found[3].append(ff[1].reshape(SLABS * rows, width))
+    return [jnp.stack(each) for each in found]
+
+
+def place_kernel(here_ref, own_ref, own_far_ref, *refs):
+    near, far, out_ref = refs[:4], refs[4:8], refs[8]
+    replica = here_ref[1]
+    pair = pl.program_id(0) // 2
+    odd = pl.program_id(0) % 2
+    half = out_ref.shape[3] // 2
+    for parity, own, parts in ((0, own_ref, near), (1, own_far_ref, far)):
+
+        @pl.when(jnp.logical_and(pair == 0, odd == parity))
+        def _():
+            for place in range(SLABS):
+                out_ref[place, 0] = own[place]
+
+        @pl.when(jnp.logical_and(pair > 0, odd == parity))
+        def _():
+            for part, steps, low in zip(parts, ((0, 1), (2, 3), (0, 2), (1, 3)), (0, 0, half, half)):
+                for i, step in enumerate(steps):
+                    place = jnp.bitwise_xor(replica, step)
+                    for k in range(out_ref.shape[2]):
+                        out_ref[place, 0, k, low : low + half] = part[i, 0, k]
+
+
+def place_weights(net, here, own, own_far, near, far):
+    places, kinds, rows, width = own.shape
+    half = rows // 2
+    whole = pl.BlockSpec(own.shape, lambda g, here_ref: (0, 0, 0, 0))
+    part = pl.BlockSpec(
+        (2, 1, kinds, half, width),
+        lambda g, here_ref: (0, jnp.maximum(g // 2 - 1, 0), 0, 0, 0),
+    )
+
+    def target(g, here_ref):
+        pair = g // 2
+        step = (pair % 2) * 4 + (pair // 2) * 2 + g % 2
+        return (0, jnp.bitwise_xor(here_ref[0], step), 0, 0, 0)
+
+    return pl.pallas_call(
+        place_kernel,
+        grid_spec=pltpu.PrefetchScalarGridSpec(
+            num_scalar_prefetch=1,
+            grid=(net.shards,),
+            in_specs=[whole, whole] + [part] * 8,
+            out_specs=pl.BlockSpec((places, 1, kinds, rows, width), target),
+        ),
+        out_shape=shape_of((places, net.shards, kinds, rows, width), low_type),
+        compiler_params=pltpu.CompilerParams(vmem_limit_bytes=56 * 2**20),
+        name="place_weights",
+    )(here, own, own_far, *near, *far)
+
+
+def gather_steps(net, here, packed):
+    own_far = net.swap(packed, "shard", 1)
+    mine = lax.dynamic_index_in_dim(packed, here[1], 0, keepdims=True)
+    got = net.swap(mine, "shard", 4)
+    yield [mine]
+    both = jnp.concatenate([mine, got])
+    more = net.swap(both, "shard", 2)
+    yield [both]
+    half = packed.shape[2] // 2
+    halves = []
+    for cut in (slice(0, half), slice(half, None)):
+        halves.append(jnp.concatenate([got[:, :, cut], more[:, :, cut]])[None])
+    gots = [net.swap(part, "replica", step) for part, step in zip(halves, (1, 2))]
+    yield halves
+    firsts = [jnp.concatenate([part, came]) for part, came in zip(halves, gots)]
+    seconds = [net.swap(part, "replica", step) for part, step in zip(firsts, (2, 1))]
+    firsts_far = [net.swap(part, "shard", 1) for part in firsts]
+    yield firsts
+    seconds_far = [net.swap(part, "shard", 1) for part in seconds]
+    yield seconds
+    near = [firsts[0], seconds[0], firsts[1], seconds[1]]
+    far = [firsts_far[0], seconds_far[0], firsts_far[1], seconds_far[1]]
+    return place_weights(net, here, packed, own_far, near, far)
+
+
+def gather_whole(net, here, packed):
+    mine = lax.dynamic_index_in_dim(packed, here[1], 0, keepdims=False)
+    flat = mine.reshape(-1, mine.shape[-1])
+    whole = lax.all_gather(flat, ("replica", "shard"), axis=0, tiled=True)
+    return whole.reshape((net.replicas, net.shards) + mine.shape)
+
+
+def plain_slabs(net, whole, tall_kind):
+    places, shards, kinds, part, width = whole.shape
+    split = whole.reshape(SLABS, places // SLABS, shards, kinds, part, width)
+    split = split.transpose(3, 0, 2, 1, 4, 5).reshape(kinds, SLABS, shards, -1, width)
+    made = []
+    for kind in range(kinds):
+        each = split[kind]
+        if kind == tall_kind:
+            each = each.transpose(1, 0, 2, 3)
+        made.append(each.reshape(SLABS, 1, width, width))
+    return jnp.stack(made, axis=2)
+
+
+class Steps:
+    def __init__(self, steps):
+        self.steps = steps
+        self.result = None
+        self.over = False
+
+    def go(self, count=1):
+        sent = []
+        for _ in range(count):
+            if not self.over:
+                try:
+                    sent = next(self.steps)
+                except StopIteration as end:
+                    self.over = True
+                    self.result = end.value
+                    sent = []
+        return list(sent)
+
+    def end(self):
+        while not self.over:
+            self.go()
+        return self.result
 
 
 def local(
@@ -612,39 +1063,43 @@
     piece_rows = rows * SLABS // replicas
     mod_width = ada_weight.shape[2]
 
+    fused = replicas == SLABS and shards == 2 * SLABS and rows % 16 == 0
+
     def pack(layer):
         qkv = qkv_weight[layer].astype(low_type)
         up = fc1_weight[layer].astype(low_type)
-        up = up.reshape(rows, shards, SLABS, rows).transpose(2, 0, 1, 3)
         down = fc2_weight[layer].astype(low_type)
-        blocks = [qkv[:, b * model_width : (b + 1) * model_width] for b in range(3)]
-        blocks += [proj_weight[layer].astype(low_type)]
-        blocks += [up[b].reshape(rows, model_width) for b in range(SLABS)]
-        blocks += [down[b * rows : (b + 1) * rows] for b in range(SLABS)]
-        packed = jnp.stack(blocks).reshape(3, replicas, piece_rows, model_width)
-        return lax.dynamic_index_in_dim(packed, replica, 1, keepdims=False)
-
-    gathered = []
-    for layer in range(LAYERS):
-        whole = lax.all_gather(pack(layer), ("replica", "shard"), axis=0, tiled=False)
-        whole = whole.reshape(
-            SLABS, replicas // SLABS, shards, 3, piece_rows, model_width
-        ).transpose(3, 0, 2, 1, 4, 5)
-        gathered.append(whole.reshape(3, SLABS, shards, rows, model_width))
+        columns = lambda w, b: w[:, b * model_width : (b + 1) * model_width]
+        attn = [columns(qkv, b) for b in range(3)] + [proj_weight[layer].astype(low_type)]
+        kinds = [jnp.stack(attn), jnp.stack([columns(up, b) for b in range(SLABS)]), down]
+        return [kind.reshape(replicas, 1, piece_rows, model_width) for kind in kinds]
+
+    packs = [pack(layer) for layer in range(LAYERS)]
+    if fused:
+        a0 = Steps(gather_steps(net, here, packs[0][0]))
+        f0 = Steps(gather_steps(net, here, jnp.concatenate(packs[0][1:], axis=1)))
+        later = gather_whole(net, here, jnp.concatenate(packs[1], axis=1))
+    else:
+        wholes = [
+            plain_slabs(net, gather_whole(net, here, jnp.concatenate(kinds, axis=1)), 2)
+            for kinds in packs
+        ]
 
     cond_low = jax.nn.silu(condition).astype(low_type)
     bias_rows = jnp.concatenate([qv_bias, proj_bias, fc1_bias, fc2_bias], axis=1).astype(low_type)
     bias_width = bias_rows.shape[1]
-    cond_rel = net.gather_rel(cond_low, ["shard"])
-    bias_all = lax.all_gather(bias_rows, "shard", axis=0, tiled=False)
-    cond_all_rel = net.gather_rel(cond_rel, ["replica"])
+    bias_rows = jnp.pad(bias_rows, ((0, 0), (0, model_width - bias_width)))
+    both_rel = net.gather_rel(jnp.concatenate([cond_low, bias_rows]), ["shard"])
+    cond_rel = both_rel[:, :latents_here]
+    found = net.order("shard")
+    spots = jnp.array([found.index(step) for step in range(shards)], jnp.int32)
+    order = jnp.take(spots, jnp.bitwise_xor(jnp.arange(shards, dtype=jnp.int32), here[0]))
+    bias_all = jnp.take(both_rel[:, latents_here:], order, axis=0)
+    cond_steps = Steps(net.gather_steps(cond_rel, "replica"))
     group = shards * latents_here
     cond_rows = lax.dynamic_slice_in_dim(
         cond_rel.reshape(group, model_width), shard * rows, rows, axis=1
     )
-    cond_every = lax.dynamic_slice_in_dim(
-        cond_all_rel.reshape(replicas * group, model_width), shard * rows, rows, axis=1
-    ).astype(wide)
     ada_low = ada_weight.astype(low_type)
     partial = jnp.stack([nn(cond_rows, ada_low[layer]) for layer in range(LAYERS)], axis=1)
     ada_part = ada_bias.shape[1]
@@ -660,90 +1115,162 @@
     widths = (qv_bias.shape[1], proj_bias.shape[1], fc1_bias.shape[1], fc2_bias.shape[1])
     starts = (0, widths[0], widths[0] + widths[1], widths[0] + widths[1] + widths[2])
 
-    def weights_of(layer):
-        slabs = gathered[layer].reshape(3, SLABS, model_width, model_width)
+    def biases_of(layer):
         qv, proj, up, down = [
             bias_all[:, layer, start : start + width].reshape(-1).astype(wide)
             for start, width in zip(starts, widths)
         ]
         qkv_b = jnp.stack([qv[:model_width], jnp.zeros((model_width,), wide), qv[model_width:]])
-        up_b = up.reshape(shards, SLABS, rows).transpose(1, 0, 2).reshape(SLABS, 1, model_width)
-        return (
-            slabs[0],
-            slabs[1],
-            slabs[2],
-            qkv_b[:, None],
-            proj[None],
-            up_b,
-            down[None],
-        )
+        up_b = up.reshape(SLABS, 1, model_width)
+        return (qkv_b[:, None], proj[None], up_b, down[None])
+
+    def attn_first():
+        a0.go(2)
+        a0.go(), f0.go()
+        a0.go(), f0.go()
+        a0.go()
+        after = f0.go()
+        return (a0.end(), 0), after
+
+    def feed_first():
+        both = f0.end()
+        return (both, 0), (both, 1), cond_steps.go()
+
+    if fused:
+        attn_calls = (attn_first, lambda: ((later, 0), []))
+        feed_calls = (feed_first, lambda: ((later, 1), (later, 2), cond_steps.go()))
+        slot_calls = (lambda: f0.go(), lambda: [])
+    else:
+        attn_calls = [lambda w=w: ((w, 0), []) for w in wholes]
+        feed_calls = [lambda w=w: ((w, 1), (w, 2), []) for w in wholes]
+        slot_calls = [lambda: []] * LAYERS
 
     live_rows = latent_live.astype(wide)[:, None, None]
     saved_all = []
     current = hidden_in
-    weights_all = [weights_of(layer) for layer in range(LAYERS)]
+    weights_all = []
     for layer in range(LAYERS):
-        current, saved_state = forward_layer(
-            current, modulations[:, layer].reshape(latents_here, 6, model_width), weights_all[layer]
+        current, saved_state, layer_weights = forward_layer(
+            here,
+            current,
+            modulations[:, layer].reshape(latents_here, 6, model_width),
+            attn_calls[layer],
+            feed_calls[layer],
+            biases_of(layer),
+            slot_calls[layer],
         )
         saved_all.append(saved_state)
+        weights_all.append(layer_weights)
     result = current * live_rows
     grad_now = out_grad * live_rows
 
     def send(grads):
-        slabs = grads.reshape(-1, shards, rows, model_width)
-        return reduce_grads(net, here, slabs)
+        if fused:
+            return Fold(net, list(zip(grads[::2], grads[1::2])))
+        slabs = [grads[0].reshape(SLABS, shards, rows, model_width)]
+        if len(grads) > 1:
+            down = grads[1].reshape(shards, SLABS, rows, model_width)
+            slabs.append(down.transpose(1, 0, 2, 3))
+        pairs = [[half[0] for half in order_grads(net, here, each)] for each in slabs]
+        return Steps(reduce_steps(net, here, pairs))
+
+    sends = {}
+    bias_steps = [None]
+
+    def bias_row(layer, sums, up_sums, down_sums):
+        grads = (
+            jnp.concatenate([sums[0], sums[2]]),
+            sums[3],
+            up_sums.reshape(-1),
+            down_sums[0],
+        )
+        bias_sums[layer] = jnp.concatenate([grad.reshape(shards, -1) for grad in grads], axis=1)
+        if layer == 0:
+            bias_steps[0] = Steps(net.total_steps(jnp.stack(bias_sums)))
+
+    def middle_slot(layer):
+        def slot(ff_grads):
+            fold = sends["ff", layer] = send(ff_grads)
+            if not fused:
+                return []
+            return fold.sent + (run_round([sends["ff", 1], sends["at", 1]]) if layer == 0 else [])
+
+        return slot
+
+    def late_slot(layer):
+        def slot(sums, up_sums, down_sums):
+            bias_row(layer, sums, up_sums, down_sums)
+            if not fused:
+                return []
+            if layer == 1:
+                return run_round([sends["ff", 1]])
+            sent = bias_steps[0].go()
+            return sent + run_round([sends["ff", 1], sends["at", 1], sends["ff", 0]])
+
+        return slot
 
     ada_wide = ada_low.astype(wide)
     grad_cond = jnp.zeros((group, rows), wide)
-    owned = [None] * LAYERS
     ada_grads = [None] * LAYERS
-    ada_bias_grads = [None] * LAYERS
+    modul_grads = [None] * LAYERS
     bias_sums = [None] * LAYERS
     for layer in reversed(range(LAYERS)):
-        grad_now, grad_modul, ff_grads, at_grads, (sums, up_sums, down_sums) = backward_layer(
-            grad_now, weights_all[layer], saved_all[layer]
+        before = sends["at", 1].sent if layer == 0 and fused else []
+        grad_now, grad_modul, at_grads = backward_layer(
+            here,
+            fused,
+            grad_now,
+            weights_all[layer],
+            saved_all[layer],
+            before,
+            middle_slot(layer),
+            late_slot(layer),
         )
-        ff_owned = send(ff_grads)
-        at_owned = send(at_grads)
-        bias_grads = (
-            jnp.concatenate([sums[0], sums[2]]),
-            sums[3],
-            up_sums.reshape(SLABS, shards, rows).transpose(1, 0, 2).reshape(-1),
-            down_sums[0],
-        )
-        modul_rel = net.gather_rel(net.gather_rel(grad_modul, ["shard"]), ["replica"])
-        modul_rel = modul_rel.reshape(replicas, group, mod_width)
-        grad_cond = grad_cond + exact_trail(modul_rel[0], ada_wide[layer])
-        modul_every = modul_rel.reshape(replicas * group, mod_width)
-        ada_grads[layer] = exact_lead(cond_every, modul_every)
-        ada_bias_grads[layer] = jnp.sum(
-            lax.dynamic_slice_in_dim(modul_every, shard * ada_part, ada_part, axis=1), axis=0
-        )
-        at_rows = at_owned.transpose(1, 0, 2, 3).reshape(SLABS, rows, model_width)
-        ff_rows = ff_owned.transpose(1, 0, 2, 3).reshape(2, SLABS, rows, model_width)
-        wide_of = lambda w: w.transpose(1, 0, 2).reshape(rows, -1)
-        owned[layer] = (
-            wide_of(at_rows[:3]),
-            at_rows[3],
-            ff_rows[1]
-            .reshape(SLABS, rows, shards, rows)
-            .transpose(1, 2, 0, 3)
-            .reshape(rows, SLABS * model_width),
-            ff_rows[0].reshape(SLABS * rows, model_width),
-        )
-        bias_sums[layer] = jnp.concatenate(
-            [grad.reshape(shards, -1) for grad in bias_grads], axis=1
-        )
-    bias_total = lax.psum(jnp.stack(bias_sums), ("replica", "shard"))
+        sends["at", layer] = send(at_grads)
+        modul_grads[layer] = grad_modul
+    modul_steps = Steps(net.gather_steps(jnp.concatenate(modul_grads), "shard"))
+    bias_steps = bias_steps[0]
+    ring = [sends["ff", 1], sends["at", 1], sends["ff", 0], sends["at", 0]]
+    every_steps = None
+    for turn in range(8):
+        after = modul_steps.go() + bias_steps.go()
+        if modul_steps.over and every_steps is None:
+            modul_low = modul_steps.result.astype(low_type)
+            every_steps = Steps(net.gather_steps(modul_low, "replica"))
+        if every_steps is not None:
+            after += every_steps.go()
+        if fused:
+            run_round(ring, after)
+    modul = modul_steps.end()
+    modul_low = every_steps.end()
+    cond_every = lax.dynamic_slice_in_dim(
+        cond_steps.end().reshape(replicas * group, model_width), shard * rows, rows, axis=1
+    )
+    per_layer = lambda w, layer: w[..., layer * latents_here : (layer + 1) * latents_here, :]
+    for layer in range(LAYERS):
+        mine = per_layer(modul, layer).reshape(group, mod_width)
+        grad_cond = grad_cond + exact_trail(mine, ada_wide[layer])
+        every = per_layer(modul_low, layer).reshape(replicas * group, mod_width)
+        ada_grads[layer] = tn(cond_every, every)
+    own_mod = lax.dynamic_slice_in_dim(modul_low, shard * ada_part, ada_part, axis=3).astype(wide)
+    own_mod = own_mod.reshape(replicas * shards, LAYERS, latents_here, ada_part)
+    ada_bias_out = jnp.sum(own_mod, axis=(0, 2))
+    bias_total = bias_steps.end()
     bias_mine = lax.dynamic_index_in_dim(bias_total, shard, 1, keepdims=False)
     bias_out = [bias_mine[:, start : start + width] for start, width in zip(starts, widths)]
 
+    if fused:
+        owned = [(sends["at", layer].every, sends["ff", layer].every) for layer in range(LAYERS)]
+        weight_outs = finish(here, owned)
+    else:
+        owned = [
+            (sends["at", layer].end(), sends["ff", layer].end()) for layer in range(LAYERS)
+        ]
+        weight_outs = finish_plain(here, owned, replicas)
     parts = grad_cond.reshape(shards, latents_here, rows)
-    back = [parts[0]] + [net.swap(parts[step], "shard", step) for step in range(1, shards)]
-    back = jnp.take(
-        jnp.stack(back), jnp.bitwise_xor(jnp.arange(shards, dtype=jnp.int32), here[0]), axis=0
-    )
+    back = [parts[0]]
+    back += [net.swap(parts[i], "shard", found[i]) for i in range(1, shards)]
+    back = jnp.take(jnp.stack(back), order, axis=0)
     cond_back = back.transpose(1, 0, 2).reshape(latents_here, model_width)
     grad_condition = jax.vjp(jax.nn.silu, condition)[1](cond_back)[0]
     return (
@@ -751,11 +1278,8 @@
         grad_now,
         grad_condition,
         jnp.stack(ada_grads),
-        jnp.stack([owned[layer][0] for layer in range(LAYERS)]),
-        jnp.stack([owned[layer][1] for layer in range(LAYERS)]),
-        jnp.stack([owned[layer][2] for layer in range(LAYERS)]),
-        jnp.stack([owned[layer][3] for layer in range(LAYERS)]),
-        jnp.stack(ada_bias_grads),
+        *weight_outs,
+        ada_bias_out,
         *bias_out,
     )
 

time: 904 us -> 720 us (0.80)
  waiting for transfers between devices: 340 us -> 238 us
  local copies, waits for them, and re-layouts: 104 us -> 42.8 us
  blocking collectives: 54.2 us -> 0 us
  Pallas kernels: 249 us -> 292 us
  other arithmetic: 55.1 us -> 32.8 us
  starting transfers between devices: 73.3 us -> 88.3 us
    all_gather x2 -> x1, waiting for transfers between devices: 139 us -> 0.02 us  [gather_whole(): whole = lax.all_gather(flat, ('replica', 'shard'), axis=0, tiled=True)]
    pallas_call x16 -> x23, Pallas kernels: 249 us -> 292 us  [the longest x12 228 us: call(): return lambda *arrays: run(here, *arrays, *after)]
    psum x1 -> x0, blocking collectives: 39 us -> none  [local(): bias_total = lax.psum(jnp.stack(bias_sums), ('replica', 'shard'))]
    ppermute x65 -> x95, waiting for transfers between devices: 201 us -> 238 us  [swap(): return lax.ppermute(values, axis, [(i, i ^ step) for i in range(count)])]
    another operation x49 -> x14, local copies, waits for them, and re-layouts: 21.2 us -> 2.03 us  [the longest x5 0.92 us: biases_of(): jnp.stack([qv[:model_width], jnp.zeros((model_width,), wide), qv[model_wi...]
    slice x21 -> x22, local copies, waits for them, and re-layouts: 28.4 us -> 10 us  [the longest x6 3.49 us: local(): w[..., layer * latents_here:(layer + 1) * latents_here, :]]
    all_gather x1 -> x0, blocking collectives: 15.2 us -> none  [local(): bias_all = lax.all_gather(bias_rows, 'shard', axis=0, tiled=False)]
    ppermute x65 -> x95, starting transfers between devices: 73.3 us -> 88.3 us  [swap(): return lax.ppermute(values, axis, [(i, i ^ step) for i in range(count)])]
  transfers between devices with their start and end apart: 67 -> 96, of which waited for: 41 -> 44; matrix products, arithmetic and copies ran while one was open for 11% -> 9% of each run, Pallas kernels for 4% -> 23%
where the time goes in v2:
time: 720 us; the launch traced here: 716 us
  Pallas kernels  292 us (41%)
  waiting for transfers between devices  238 us (33%)
  starting transfers between devices  88.3 us (12%)
  local copies, waits for them, and re-layouts  42.8 us (6%)
  other arithmetic  32.8 us (5%)
  between operations  15.9 us (2%)
    ppermute x95, waiting for transfers between devices, swap(): return lax.ppermute(values, axis, [(i, i ^ step) for i in range(count)])  238 us
    pallas_call x12, Pallas kernels, call(): return lambda *arrays: run(here, *arrays, *after)  228 us
    ppermute x95, starting transfers between devices, swap(): return lax.ppermute(values, axis, [(i, i ^ step) for i in range(count)])  88.3 us
    pallas_call x8, Pallas kernels, run_round(): pl.pallas_call(functools.partial(round_kernel, jobs), in_specs=[pl.BlockS...  38.6 us
    pallas_call x2, Pallas kernels, place_weights(): pl.pallas_call(place_kernel, grid_spec=pltpu.PrefetchScalarGridSpec(num_s...  19.1 us
  transfers between devices with their start and end apart: 96, of which 44 were waited for; matrix products, arithmetic and copies ran while one was open for 9% of the time, Pallas kernels for 23%

profile of v2, /device:TPU:0, one launch (start us, length us, event | category | flops | bytes accessed | tf_op | source)
XLA Modules:
  0.0 715.7 jit_solution(9950906111215570623)
XLA Ops:
  15.5 4.0 collective-permute-start
  27.7 6.6 collective-permute-done.1
  48.3 4.0 collective-permute-done.7
  57.5 16.0 %collective-permute-done.8 = bf16[2,1,96,768]{3,2,0,1:T(8,128)(2,1)S(1)} collective-permute-done((bf16[2,1,96,768]{3,2,0,1:T(8,128)(2,1)S(1)}, bf16[2,1,96,768]{3,2,0,1:T(8,128)(2,1)S(1)}, u32[]{:S(2)}, u32[]{:S(2)}) %collective-permute-start.8) | collective-permute-done | bytes 294944 | tf_op jit(solution)/shard_map/ppermute | solution.py:569
  81.9 13.0 %collective-permute-done.18 = bf16[2,2,96,768]{3,2,1,0:T(8,128)(2,1)S(1)} collective-permute-done((bf16[2,2,96,768]{3,2,1,0:T(8,128)(2,1)S(1)}, bf16[2,2,96,768]{3,2,1,0:T(8,128)(2,1)S(1)}, u32[]{:S(2)}, u32[]{:S(2)}) %collective-permute-start.18) | collective-permute-done | bytes 589856 | tf_op jit(solution)/shard_map/ppermute | solution.py:569
  99.2 4.2 collective-permute-done.19
  105.9 10.8 %collective-permute-done.20 = bf16[1,3,2,48,768]{4,3,2,1,0:T(8,128)(2,1)S(1)} collective-permute-done((bf16[1,3,2,48,768]{4,3,2,1,0:T(8,128)(2,1)S(1)}, bf16[1,3,2,48,768]{4,3,2,1,0:T(8,128)(2,1)S(1)}, u32[]{:S(2)}, u32[]{:S(2)}) %collective-permute-start.20) | collective-permute-done | bytes 442400 | tf_op jit(solution)/shard_map/ppermute | solution.py:569
  122.1 6.2 collective-permute-done.5
  130.1 5.0 collective-permute-done.10
  135.1 7.0 collective-permute-done.12.refs_3_
  146.8 11.6 %collective-permute-done.23.refs_3_ = bf16[2,3,2,48,768]{4,3,2,1,0:T(8,128)(2,1)} collective-permute-done((bf16[2,3,2,48,768]{4,3,2,1,0:T(8,128)(2,1)}, bf16[2,3,2,48,768]{4,3,2,1,0:T(8,128)(2,1)}, u32[]{:S(2)}, u32[]{:S(2)}) %collective-permute-start.23) | collective-permute-done | bytes 884768 | tf_op jit(solution)/shard_map/ppermute | solution.py:569
  163.1 8.2 %place_weights.2.refs_2_.refs_3_.refs_6_ = bf16[4,8,1,96,768]{4,3,2,1,0:T(8,128)(2,1)} custom-call(s32[2]{0:T(128)} %pad_add_fusion.here_ref, bf16[4,1,96,768]{3,2,1,0:T(8,128)(2,1)} %get-tuple-element.293.own_ref, bf16[4,1,96,768]{3,2,1,0:T(8,128)(2,1)} %bitcast.16.own_far_ref, bf16[2,3,1,48,768]{4,3,2,1,0:T(8,128)(2,1)} %get-tuple-element.298.refs_0_, ...), custom_call_target="tpu_custom_call" | custom-call | tf_op jit(solution)/shard_map/place_weights/pallas_call | solution.py:957
  171.3 8.6 %qkv_kernel.2 = (bf16[768,768]{1,0:T(8,128)(2,1)}, bf16[3,768,768]{2,1,0:T(8,128)(2,1)}) custom-call(s32[2]{0:T(128)} %pad_add_fusion.here_ref, f32[3,256,768]{2,1,0:T(8,128)} %refs_4_.1, f32[3,6,768]{2,1,0:T(8,128)} %reshape_squeeze.12.refs_1_.refs_2_.refs_5_.refs_6_, bf16[4,8,1,96,768]{4,3,2,1,0:T(8,128)(2,1)} %place_weights.2.refs_2_.refs_3_.refs_6_, ...), custom_call_target="tpu_custom_call" | custom-call | flops 2717908992 | bytes 10616832 | tf_op jit(solution)/shard_map/qkv_kernel/pallas_call | solution.py:380
  179.9 11.8 %mix_kernel.2 = (bf16[768,768]{1,0:T(8,128)(2,1)}, f32[768,768]{1,0:T(8,128)}, f32[768,768]{1,0:T(8,128)}, bf16[768,768]{1,0:T(8,128)(2,1)}) custom-call(s32[2]{0:T(128)} %pad_add_fusion.here_ref, bf16[3,768,768]{2,1,0:T(8,128)(2,1)} %get-tuple-element.132.refs_0_.refs_4_, f32[3,256,768]{2,1,0:T(8,128)} %refs_4_.1, ...), custom_call_target="tpu_custom_call" | custom-call | flops 4529848320 | bytes 14155776 | tf_op jit(solution)/shard_map/mix_kernel/pallas_call | solution.py:380
  191.7 10.9 %place_weights.3.refs_3_.refs_5_.refs_6_.refs_7_ = bf16[4,8,2,96,768]{4,3,2,1,0:T(8,128)(2,1)} custom-call(s32[2]{0:T(128)} %pad_add_fusion.here_ref, bf16[4,2,96,768]{3,2,1,0:T(8,128)(2,1)} %copy-done.4, bf16[4,2,96,768]{3,2,1,0:T(8,128)(2,1)} %collective-permute-done.21.own_far_ref, bf16[2,3,2,48,768]{4,3,2,1,0:T(8,128)(2,1)} %pad_maximum_fusion.3.refs_5_.refs_0_, ...), custom_call_target="tpu_custom_call" | custom-call | tf_op jit(solution)/shard_map/place_weights/pallas_call | solution.py:957
  202.6 21.8 %feed_kernel.2 = (bf16[4,768,768]{2,1,0:T(8,128)(2,1)}, bf16[4,768,768]{2,1,0:T(8,128)(2,1)}, f32[768,768]{1,0:T(8,128)}, f32[768,768]{1,0:T(8,128)}) custom-call(s32[2]{0:T(128)} %pad_add_fusion.here_ref, bf16[768,768]{1,0:T(8,128)(2,1)} %get-tuple-element.133.refs_0_.refs_3_, f32[768,768]{1,0:T(8,128)} %get-tuple-element.134.refs_1_, ...), custom_call_target="tpu_custom_call" | custom-call | flops 10871635968 | bytes 23592960 | tf_op jit(solution)/shard_map/feed_kernel/pallas_call | solution.py:380
  224.4 8.4 %qkv_kernel.3 = (bf16[768,768]{1,0:T(8,128)(2,1)}, bf16[3,768,768]{2,1,0:T(8,128)(2,1)}) custom-call(s32[2]{0:T(128)} %pad_add_fusion.here_ref, f32[3,256,768]{2,1,0:T(8,128)} %bitcast.180, f32[3,6,768]{2,1,0:T(8,128)} %reshape_squeeze.13.refs_1_.refs_2_.refs_5_.refs_6_, bf16[4,8,3,96,768]{4,3,2,1,0:T(8,128)(2,1)} %bitcast.172, ...), custom_call_target="tpu_custom_call" | custom-call | flops 2717908992 | bytes 10616832 | tf_op jit(solution)/shard_map/qkv_kernel/pallas_call | solution.py:380
  232.8 11.8 %mix_kernel.3 = (bf16[768,768]{1,0:T(8,128)(2,1)}, f32[768,768]{1,0:T(8,128)}, f32[768,768]{1,0:T(8,128)}, bf16[768,768]{1,0:T(8,128)(2,1)}) custom-call(s32[2]{0:T(128)} %pad_add_fusion.here_ref, bf16[3,768,768]{2,1,0:T(8,128)(2,1)} %get-tuple-element.136.refs_0_.refs_4_, f32[3,256,768]{2,1,0:T(8,128)} %bitcast.181, ...), custom_call_target="tpu_custom_call" | custom-call | flops 4529848320 | bytes 14155776 | tf_op jit(solution)/shard_map/mix_kernel/pallas_call | solution.py:380
  244.6 21.7 %feed_kernel.3 = (bf16[4,768,768]{2,1,0:T(8,128)(2,1)}, bf16[4,768,768]{2,1,0:T(8,128)(2,1)}, f32[768,768]{1,0:T(8,128)}, f32[768,768]{1,0:T(8,128)}) custom-call(s32[2]{0:T(128)} %pad_add_fusion.here_ref, bf16[768,768]{1,0:T(8,128)(2,1)} %get-tuple-element.137.refs_0_.refs_3_, f32[768,768]{1,0:T(8,128)} %get-tuple-element.138.refs_1_, ...), custom_call_target="tpu_custom_call" | custom-call | flops 10871635968 | bytes 23592960 | tf_op jit(solution)/shard_map/feed_kernel/pallas_call | solution.py:380
  266.3 4.4 broadcast_multiply_fusion
  270.7 29.6 %feed_back_kernel.2 = (bf16[4,4,96,768]{3,2,1,0:T(8,128)(2,1)}, bf16[4,4,96,768]{3,2,1,0:T(8,128)(2,1)}, bf16[4,4,96,768]{3,2,1,0:T(8,128)(2,1)}, bf16[4,4,96,76...) custom-call(s32[2]{0:T(128)} %pad_add_fusion.here_ref, ...), custom_call_target="tpu_custom_call" | custom-call | flops 14495514624 | bytes 29491200 | tf_op jit(solution)/shard_map/feed_back_kernel/pallas_call | solution.py:380
  300.8 24.6 %mix_back_kernel.2 = (f32[768,768]{1,0:T(8,128)}, bf16[4,768,768]{2,1,0:T(8,128)(2,1)}, f32[3,3,768]{2,1,0:T(4,128)}, f32[4,768]{1,0:T(4,128)}) custom-call(s32[2]{0:T(128)} %pad_add_fusion.here_ref, f32[768,768]{1,0:T(8,128)} %get-tuple-element.147.refs_0_, f32[768,768]{1,0:T(8,128)} %get-tuple-element.138.refs_1_, f32[768,768]{1,0:T(8,128)} %bitcast.195, ...), custom_call_target="tpu_custom_call" | custom-call | flops 9059696640 | bytes 23592960 | tf_op jit(solution)/shard_map/mix_back_kernel/pallas_call | solution.py:380
  326.9 6.2 round.8
  333.1 17.6 %qkv_back_kernel.2 = (bf16[4,4,96,768]{3,2,1,0:T(8,128)(2,1)}, bf16[4,4,96,768]{3,2,1,0:T(8,128)(2,1)}, f32[3,256,768]{2,1,0:T(8,128)}, f32[3,2,768]{2,1,0:T(2,128)}) custom-call(s32[2]{0:T(128)} %pad_add_fusion.here_ref, bf16[768,768]{1,0:T(8,128)(2,1)} %get-tuple-element.142.refs_0_, bf16[768,768]{1,0:T(8,128)(2,1)} %get-tuple-element.143.refs_1_, ...), custom_call_target="tpu_custom_call" | custom-call | flops 6341787648 | bytes 21233664 | tf_op jit(solution)/shard_map/qkv_back_kernel/pallas_call | solution.py:380
  354.4 29.7 %feed_back_kernel.3 = (bf16[4,4,96,768]{3,2,1,0:T(8,128)(2,1)}, bf16[4,4,96,768]{3,2,1,0:T(8,128)(2,1)}, bf16[4,4,96,768]{3,2,1,0:T(8,128)(2,1)}, bf16[4,4,96,76...) custom-call(s32[2]{0:T(128)} %pad_add_fusion.here_ref, ...), custom_call_target="tpu_custom_call" | custom-call | flops 14495514624 | bytes 29491200 | tf_op jit(solution)/shard_map/feed_back_kernel/pallas_call | solution.py:380
  386.8 6.1 round.9
  392.9 24.7 %mix_back_kernel.3 = (f32[768,768]{1,0:T(8,128)}, bf16[4,768,768]{2,1,0:T(8,128)(2,1)}, f32[3,3,768]{2,1,0:T(4,128)}, f32[4,768]{1,0:T(4,128)}) custom-call(s32[2]{0:T(128)} %pad_add_fusion.here_ref, f32[768,768]{1,0:T(8,128)} %get-tuple-element.162.refs_0_, f32[768,768]{1,0:T(8,128)} %get-tuple-element.134.refs_1_, f32[768,768]{1,0:T(8,128)} %bitcast.216, ...), custom_call_target="tpu_custom_call" | custom-call | flops 9059696640 | bytes 23592960 | tf_op jit(solution)/shard_map/mix_back_kernel/pallas_call | solution.py:380
  420.1 4.1 collective-permute-done.69
  424.2 3.4 collective-permute-start.75
  444.9 6.8 collective-permute-done.34.refs_1_
  453.0 8.1 %collective-permute-done.36.refs_5_ = bf16[4,96,768]{2,1,0:T(8,128)(2,1)} collective-permute-done((bf16[4,96,768]{2,1,0:T(8,128)(2,1)}, bf16[4,96,768]{2,1,0:T(8,128)(2,1)}, u32[]{:S(2)}, u32[]{:S(2)}) %collective-permute-start.36) | collective-permute-done | bytes 589856 | tf_op jit(solution)/shard_map/ppermute | solution.py:569
  461.1 8.1 %round.10 = (bf16[2,96,768]{2,1,0:T(8,128)(2,1)}, bf16[2,96,768]{2,1,0:T(8,128)(2,1)}, bf16[2,96,768]{2,1,0:T(8,128)(2,1)}, bf16[2,96,768]{2,1,0:T(8,128)(2,1)},...) custom-call(bf16[4,96,768]{2,1,0:T(8,128)(2,1)} %get-tuple-element.1, ...), custom_call_target="tpu_custom_call" | custom-call | tf_op jit(solution)/shard_map/round/pallas_call | solution.py:841
  469.3 17.6 %qkv_back_kernel.3 = (bf16[4,4,96,768]{3,2,1,0:T(8,128)(2,1)}, bf16[4,4,96,768]{3,2,1,0:T(8,128)(2,1)}, f32[3,256,768]{2,1,0:T(8,128)}, f32[3,2,768]{2,1,0:T(2,128)}) custom-call(s32[2]{0:T(128)} %pad_add_fusion.here_ref, bf16[768,768]{1,0:T(8,128)(2,1)} %get-tuple-element.140.refs_0_, bf16[768,768]{1,0:T(8,128)(2,1)} %get-tuple-element.141.refs_1_, ...), custom_call_target="tpu_custom_call" | custom-call | flops 6341787648 | bytes 21233664 | tf_op jit(solution)/shard_map/qkv_back_kernel/pallas_call | solution.py:380
  496.4 13.6 %collective-permute-done.41 = f32[2,6,4608]{2,1,0:T(8,128)S(1)} collective-permute-done((f32[2,6,4608]{2,1,0:T(8,128)S(1)}, f32[2,6,4608]{2,1,0:T(8,128)S(1)}, u32[]{:S(2)}, u32[]{:S(2)}) %collective-permute-start.41) | collective-permute-done | bytes 221216 | tf_op jit(solution)/shard_map/ppermute | solution.py:569
  527.0 4.6 collective-permute-done.45
  531.6 22.2 %collective-permute-done.55.refs_5_ = bf16[2,96,768]{2,1,0:T(8,128)(2,1)S(1)} collective-permute-done((bf16[2,96,768]{2,1,0:T(8,128)(2,1)S(1)}, bf16[2,96,768]{2,1,0:T(8,128)(2,1)S(1)}, u32[]{:S(2)}, u32[]{:S(2)}) %collective-permute-start.55) | collective-permute-done | bytes 294944 | tf_op jit(solution)/shard_map/ppermute | solution.py:569
  564.8 7.1 round.11
  579.2 6.9 collective-permute-done.61.refs_1_
  593.9 8.7 %collective-permute-done.66.refs_11_ = bf16[4,96,768]{2,1,0:T(8,128)(2,1)} collective-permute-done((bf16[4,96,768]{2,1,0:T(8,128)(2,1)}, bf16[4,96,768]{2,1,0:T(8,128)(2,1)}, u32[]{:S(2)}, u32[]{:S(2)}) %collective-permute-start.66) | collective-permute-done | bytes 589856 | tf_op jit(solution)/shard_map/ppermute | solution.py:569
  602.5 12.6 %collective-permute-done.67.refs_13_ = bf16[4,96,768]{2,1,0:T(8,128)(2,1)} collective-permute-done((bf16[4,96,768]{2,1,0:T(8,128)(2,1)}, bf16[4,96,768]{2,1,0:T(8,128)(2,1)}, u32[]{:S(2)}, u32[]{:S(2)}) %collective-permute-start.67) | collective-permute-done | bytes 589856 | tf_op jit(solution)/shard_map/ppermute | solution.py:569
  615.2 4.4 round.12
  623.8 4.3 collective-permute-done.70.refs_1_
  629.1 4.5 collective-permute-done.71.refs_3_
  633.6 4.8 collective-permute-done.72.refs_5_
  649.5 5.2 collective-permute-done.76.refs_1_
  668.0 5.2 collective-permute-done.81.refs_1_
  691.5 9.5 %collective-permute-done.83.refs_2_ = bf16[1,96,768]{2,1,0:T(8,128)(2,1)S(1)} collective-permute-done((bf16[1,96,768]{2,1,0:T(8,128)(2,1)S(1)}, bf16[1,96,768]{2,1,0:T(8,128)(2,1)S(1)}, u32[]{:S(2)}, u32[]{:S(2)}) %collective-permute-start.83) | collective-permute-done | bytes 147488 | tf_op jit(solution)/shard_map/ppermute | solution.py:569
  702.6 6.0 finish.1
  (527 shorter events, 197.7 us)
Async XLA Ops:
  7.2 217.2 %all-gather.2.cloned.1.call-start = ((), (), s32[]{:S(2)}) async-start(), calls=%async_computation | async-start | bytes 14598144 | tf_op jit(solution)/shard_map/all_gather | solution.py:999
  20.4 33.9 %collective-permute-start.17 = (bf16[1,2,96,768]{3,2,1,0:T(8,128)(2,1)}, bf16[1,2,96,768]{3,2,1,0:T(8,128)(2,1)}, u32[]{:S(2)}, u32[]{:S(2)}) collective-permute-start(bf16[1,2,96,768]{3,2,1,0:T(8,128)(2,1)} %fusion.4), channel_id=1, source_target_pairs={{0,4},{1,5},{2,6},{3,7},{4,0},{5,1},{6,2},{7,3},{8,12},{9,13},{10,... | collective-permute-start | bytes 884744 | tf_op jit(solution)/shard_map/ppermute | solution.py:569
  22.2 30.0 %collective-permute-start.7 = (bf16[1,1,96,768]{3,2,0,1:T(8,128)(2,1)}, bf16[1,1,96,768]{3,2,0,1:T(8,128)(2,1)}, u32[]{:S(2)}, u32[]{:S(2)}) collective-permute-start(bf16[1,1,96,768]{3,2,0,1:T(8,128)(2,1)} %dynamic-slice_bitcast_fusion), channel_id=1, source_target_pairs={{0,4},{1,5},{2,6},{3,7},{4,0},{5,1},{6,2},{7,3},{8,12},{9,13},{10,... | collective-permute-start | bytes 442376 | tf_op jit(solution)/shard_map/ppermute | solution.py:569
  25.1 96.5 %collective-permute-start.6 = (bf16[4,1,96,768]{3,2,0,1:T(8,128)(2,1)}, bf16[4,1,96,768]{3,2,0,1:T(8,128)(2,1)}, u32[]{:S(2)}, u32[]{:S(2)}) collective-permute-start(bf16[4,1,96,768]{3,2,0,1:T(8,128)(2,1)} %get-tuple-element.292), channel_id=1, source_target_pairs={{0,1},{1,0},{2,3},{3,2},{4,5},{5,4},{6,7},{7,6},{8,9},{9,8},{10,11... | collective-permute-start | bytes 1769480 | tf_op jit(solution)/shard_map/ppermute | solution.py:569
  47.6 30.2 %collective-permute-start.3 = (f32[4,3,2,4608]{3,2,1,0:T(2,128)S(1)}, f32[4,3,2,4608]{3,2,1,0:T(2,128)S(1)}, u32[]{:S(2)}, u32[]{:S(2)}) collective-permute-start(f32[4,3,2,4608]{3,2,1,0:T(2,128)S(1)} %bitcast.203), channel_id=1, source_target_pairs={{0,1},{1,0},{2,3},{3,2},{4,5},{5,4},{6,7},{7,6},{8,9},{9,8},{10,11... | collective-permute-start | bytes 1327112 | tf_op jit(solution)/shard_map/ppermute | solution.py:569
  53.3 20.2 %collective-permute-start.8 = (bf16[2,1,96,768]{3,2,0,1:T(8,128)(2,1)S(1)}, bf16[2,1,96,768]{3,2,0,1:T(8,128)(2,1)S(1)}, u32[]{:S(2)}, u32[]{:S(2)}) collective-permute-start(bf16[2,1,96,768]{3,2,0,1:T(8,128)(2,1)S(1)} %pad_maximum_fusion.12), channel_id=1, source_target_pairs={{0,2},{1,3},{2,0},{3,1},{4,6},{5,7},{6,4},{7,5},{8,10},{9,11},{10,... | collective-permute-start | bytes 884744 | tf_op jit(solution)/shard_map/ppermute | solution.py:569
  55.4 39.5 %collective-permute-start.18 = (bf16[2,2,96,768]{3,2,1,0:T(8,128)(2,1)S(1)}, bf16[2,2,96,768]{3,2,1,0:T(8,128)(2,1)S(1)}, u32[]{:S(2)}, u32[]{:S(2)}) collective-permute-start(bf16[2,2,96,768]{3,2,1,0:T(8,128)(2,1)S(1)} %pad_maximum_fusion.7), channel_id=1, source_target_pairs={{0,2},{1,3},{2,0},{3,1},{4,6},{5,7},{6,4},{7,5},{8,10},{9,11},{10,... | collective-permute-start | bytes 1769480 | tf_op jit(solution)/shard_map/ppermute | solution.py:569
  77.8 42.3 %collective-permute-start.28 = (bf16[1,8,3,768]{3,2,1,0:T(4,128)(2,1)S(1)}, bf16[1,8,3,768]{3,2,1,0:T(4,128)(2,1)S(1)}, u32[]{:S(2)}, u32[]{:S(2)}) collective-permute-start(bf16[1,8,3,768]{3,2,1,0:T(4,128)(2,1)S(1)} %copy-done.29), channel_id=1, source_target_pairs={{0,16},{8,24},{16,0},{24,8},{1,17},{9,25},{17,1},{25,9},{2,18},{10... | collective-permute-start | bytes 110600 | tf_op jit(solution)/shard_map/ppermute | solution.py:569
  79.5 18.0 %collective-permute-start.4 = (f32[2,3,2,4608]{3,2,1,0:T(2,128)S(1)}, f32[2,3,2,4608]{3,2,1,0:T(2,128)S(1)}, u32[]{:S(2)}, u32[]{:S(2)}) collective-permute-start(f32[2,3,2,4608]{3,2,1,0:T(2,128)S(1)} %slice.365), channel_id=1, source_target_pairs={{0,2},{1,3},{2,0},{3,1},{4,6},{5,7},{6,4},{7,5},{8,10},{9,11},{10,... | collective-permute-start | bytes 663560 | tf_op jit(solution)/shard_map/ppermute | solution.py:569
  81.1 48.9 %collective-permute-start.13 = (bf16[2,3,1,48,768]{4,3,1,2,0:T(8,128)(2,1)S(1)}, bf16[2,3,1,48,768]{4,3,1,2,0:T(8,128)(2,1)S(1)}, u32[]{:S(2)}, u32[]{:S(2)}) collective-permute-start(bf16[2,3,1,48,768]{4,3,1,2,0:T(8,128)(2,1)S(1)} %get-tuple-element.297), channel_id=1, source_target_pairs={{0,1},{1,0},{2,3},{3,2},{4,5},{5,4},{6,7},{7,6},{8,9},{9,8},{10,11... | collective-permute-start | bytes 1327112 | tf_op jit(solution)/shard_map/ppermute | solution.py:569
  97.5 19.2 %collective-permute-start.20 = (bf16[1,3,2,48,768]{4,3,2,1,0:T(8,128)(2,1)S(1)}, bf16[1,3,2,48,768]{4,3,2,1,0:T(8,128)(2,1)S(1)}, u32[]{:S(2)}, u32[]{:S(2)}) collective-permute-start(bf16[1,3,2,48,768]{4,3,2,1,0:T(8,128)(2,1)S(1)} %maximum_bitcast_fusion.4.refs_5_), channel_id=1, source_target_pairs={{0,16},{8,24},{16,0},{24,8},{1,17},{9,25},{17,1},{25,9},{2,18},{10... | collective-permute-start | bytes 1327112 | tf_op jit(solution)/shard_map/ppermute | solution.py:569
  103.4 31.7 %collective-permute-start.10 = (bf16[2,3,1,48,768]{4,3,1,2,0:T(8,128)(2,1)S(1)}, bf16[2,3,1,48,768]{4,3,1,2,0:T(8,128)(2,1)}, u32[]{:S(2)}, u32[]{:S(2)}) collective-permute-start(bf16[2,3,1,48,768]{4,3,1,2,0:T(8,128)(2,1)S(1)} %get-tuple-element.297), channel_id=1, source_target_pairs={{0,16},{8,24},{16,0},{24,8},{1,17},{9,25},{17,1},{25,9},{2,18},{10... | collective-permute-start | bytes 1327112 | tf_op jit(solution)/shard_map/ppermute | solution.py:569
  120.1 22.0 %collective-permute-start.12 = (bf16[2,3,1,48,768]{4,3,2,1,0:T(8,128)(2,1)}, bf16[2,3,1,48,768]{4,3,2,1,0:T(8,128)(2,1)}, u32[]{:S(2)}, u32[]{:S(2)}) collective-permute-start(bf16[2,3,1,48,768]{4,3,2,1,0:T(8,128)(2,1)} %pad_maximum_fusion.11.refs_2_), channel_id=1, source_target_pairs={{0,8},{8,0},{16,24},{24,16},{1,9},{9,1},{17,25},{25,17},{2,10},{10... | collective-permute-start | bytes 1327112 | tf_op jit(solution)/shard_map/ppermute | solution.py:569
  121.6 36.8 %collective-permute-start.23 = (bf16[2,3,2,48,768]{4,3,2,1,0:T(8,128)(2,1)}, bf16[2,3,2,48,768]{4,3,2,1,0:T(8,128)(2,1)}, u32[]{:S(2)}, u32[]{:S(2)}) collective-permute-start(bf16[2,3,2,48,768]{4,3,2,1,0:T(8,128)(2,1)} %pad_maximum_fusion.4.refs_6_.refs_2_), channel_id=1, source_target_pairs={{0,8},{8,0},{16,24},{24,16},{1,9},{9,1},{17,25},{25,17},{2,10},{10... | collective-permute-start | bytes 2654216 | tf_op jit(solution)/shard_map/ppermute | solution.py:569
  128.3 33.1 %collective-permute-start.22 = (bf16[2,3,2,48,768]{4,3,2,1,0:T(8,128)(2,1)}, bf16[2,3,2,48,768]{4,3,2,1,0:T(8,128)(2,1)}, u32[]{:S(2)}, u32[]{:S(2)}) collective-permute-start(bf16[2,3,2,48,768]{4,3,2,1,0:T(8,128)(2,1)} %pad_maximum_fusion.3.refs_5_.refs_0_), channel_id=1, source_target_pairs={{0,16},{8,24},{16,0},{24,8},{1,17},{9,25},{17,1},{25,9},{2,18},{10... | collective-permute-start | bytes 2654216 | tf_op jit(solution)/shard_map/ppermute | solution.py:569
  145.8 45.9 %collective-permute-start.21 = (bf16[4,2,96,768]{3,2,1,0:T(8,128)(2,1)S(1)}, bf16[4,2,96,768]{3,2,1,0:T(8,128)(2,1)}, u32[]{:S(2)}, u32[]{:S(2)}) collective-permute-start(bf16[4,2,96,768]{3,2,1,0:T(8,128)(2,1)S(1)} %pad_maximum_fusion.1.own_ref), channel_id=1, source_target_pairs={{0,1},{1,0},{2,3},{3,2},{4,5},{5,4},{6,7},{7,6},{8,9},{9,8},{10,11... | collective-permute-start | bytes 3538952 | tf_op jit(solution)/shard_map/ppermute | solution.py:569
  146.3 45.4 %collective-permute-start.26 = (bf16[2,3,2,48,768]{4,3,2,1,0:T(8,128)(2,1)}, bf16[2,3,2,48,768]{4,3,2,1,0:T(8,128)(2,1)}, u32[]{:S(2)}, u32[]{:S(2)}) collective-permute-start(bf16[2,3,2,48,768]{4,3,2,1,0:T(8,128)(2,1)} %pad_maximum_fusion.4.refs_6_.refs_2_), channel_id=1, source_target_pairs={{0,1},{1,0},{2,3},{3,2},{4,5},{5,4},{6,7},{7,6},{8,9},{9,8},{10,11... | collective-permute-start | bytes 2654216 | tf_op jit(solution)/shard_map/ppermute | solution.py:569
  146.4 45.3 %collective-permute-start.24 = (bf16[2,3,2,48,768]{4,3,2,1,0:T(8,128)(2,1)}, bf16[2,3,2,48,768]{4,3,2,1,0:T(8,128)(2,1)}, u32[]{:S(2)}, u32[]{:S(2)}) collective-permute-start(bf16[2,3,2,48,768]{4,3,2,1,0:T(8,128)(2,1)} %pad_maximum_fusion.3.refs_5_.refs_0_), channel_id=1, source_target_pairs={{0,1},{1,0},{2,3},{3,2},{4,5},{5,4},{6,7},{7,6},{8,9},{9,8},{10,11... | collective-permute-start | bytes 2654216 | tf_op jit(solution)/shard_map/ppermute | solution.py:569
  158.4 33.3 %collective-permute-start.27 = (bf16[2,3,2,48,768]{4,3,2,1,0:T(8,128)(2,1)}, bf16[2,3,2,48,768]{4,3,2,1,0:T(8,128)(2,1)}, u32[]{:S(2)}, u32[]{:S(2)}) collective-permute-start(bf16[2,3,2,48,768]{4,3,2,1,0:T(8,128)(2,1)} %collective-permute-done.23.refs_3_), channel_id=1, source_target_pairs={{0,1},{1,0},{2,3},{3,2},{4,5},{5,4},{6,7},{7,6},{8,9},{9,8},{10,11... | collective-permute-start | bytes 2654216 | tf_op jit(solution)/shard_map/ppermute | solution.py:569
  161.3 30.4 %collective-permute-start.25 = (bf16[2,3,2,48,768]{4,3,2,1,0:T(8,128)(2,1)}, bf16[2,3,2,48,768]{4,3,2,1,0:T(8,128)(2,1)}, u32[]{:S(2)}, u32[]{:S(2)}) collective-permute-start(bf16[2,3,2,48,768]{4,3,2,1,0:T(8,128)(2,1)} %collective-permute-done.22.refs_1_), channel_id=1, source_target_pairs={{0,1},{1,0},{2,3},{3,2},{4,5},{5,4},{6,7},{7,6},{8,9},{9,8},{10,11... | collective-permute-start | bytes 2654216 | tf_op jit(solution)/shard_map/ppermute | solution.py:569
  300.3 25.2 %collective-permute-start.29 = (bf16[16,96,768]{2,1,0:T(8,128)(2,1)}, bf16[16,96,768]{2,1,0:T(8,128)(2,1)S(1)}, u32[]{:S(2)}, u32[]{:S(2)}) collective-permute-start(bf16[16,96,768]{2,1,0:T(8,128)(2,1)} %bitcast.221), channel_id=1, source_target_pairs={{0,1},{1,0},{2,3},{3,2},{4,5},{5,4},{6,7},{7,6},{8,9},{9,8},{10,11... | collective-permute-start | bytes 7077896 | tf_op jit(solution)/shard_map/ppermute | solution.py:569
  300.5 25.0 %collective-permute-start.30 = (bf16[16,96,768]{2,1,0:T(8,128)(2,1)}, bf16[16,96,768]{2,1,0:T(8,128)(2,1)}, u32[]{:S(2)}, u32[]{:S(2)}) collective-permute-start(bf16[16,96,768]{2,1,0:T(8,128)(2,1)} %bitcast.219), channel_id=1, source_target_pairs={{0,1},{1,0},{2,3},{3,2},{4,5},{5,4},{6,7},{7,6},{8,9},{9,8},{10,11... | collective-permute-start | bytes 7077896 | tf_op jit(solution)/shard_map/ppermute | solution.py:569
  350.7 36.1 %collective-permute-start.33 = (bf16[16,96,768]{2,1,0:T(8,128)(2,1)}, bf16[16,96,768]{2,1,0:T(8,128)(2,1)}, u32[]{:S(2)}, u32[]{:S(2)}) collective-permute-start(bf16[16,96,768]{2,1,0:T(8,128)(2,1)} %bitcast.217), channel_id=1, source_target_pairs={{0,1},{1,0},{2,3},{3,2},{4,5},{5,4},{6,7},{7,6},{8,9},{9,8},{10,11... | collective-permute-start | bytes 7077896 | tf_op jit(solution)/shard_map/ppermute | solution.py:569
  351.0 35.8 %collective-permute-start.31 = (bf16[8,96,768]{2,1,0:T(8,128)(2,1)}, bf16[8,96,768]{2,1,0:T(8,128)(2,1)}, u32[]{:S(2)}, u32[]{:S(2)}) collective-permute-start(bf16[8,96,768]{2,1,0:T(8,128)(2,1)} %get-tuple-element.155.refs_7_), channel_id=1, source_target_pairs={{0,8},{8,0},{16,24},{24,16},{1,9},{9,1},{17,25},{25,17},{2,10},{10... | collective-permute-start | bytes 3538952 | tf_op jit(solution)/shard_map/ppermute | solution.py:569
  352.5 34.3 %collective-permute-start.32 = (bf16[8,96,768]{2,1,0:T(8,128)(2,1)S(1)}, bf16[8,96,768]{2,1,0:T(8,128)(2,1)}, u32[]{:S(2)}, u32[]{:S(2)}) collective-permute-start(bf16[8,96,768]{2,1,0:T(8,128)(2,1)S(1)} %copy-done.14), channel_id=1, source_target_pairs={{0,16},{8,24},{16,0},{24,8},{1,17},{9,25},{17,1},{25,9},{2,18},{10... | collective-permute-start | bytes 3538952 | tf_op jit(solution)/shard_map/ppermute | solution.py:569
  384.1 53.3 %collective-permute-start.38 = (bf16[16,96,768]{2,1,0:T(8,128)(2,1)}, bf16[16,96,768]{2,1,0:T(8,128)(2,1)}, u32[]{:S(2)}, u32[]{:S(2)}) collective-permute-start(bf16[16,96,768]{2,1,0:T(8,128)(2,1)} %bitcast.213), channel_id=1, source_target_pairs={{0,1},{1,0},{2,3},{3,2},{4,5},{5,4},{6,7},{7,6},{8,9},{9,8},{10,11... | collective-permute-start | bytes 7077896 | tf_op jit(solution)/shard_map/ppermute | solution.py:569
  386.3 58.6 %collective-permute-start.39 = (bf16[16,96,768]{2,1,0:T(8,128)(2,1)}, bf16[16,96,768]{2,1,0:T(8,128)(2,1)}, u32[]{:S(2)}, u32[]{:S(2)}) collective-permute-start(bf16[16,96,768]{2,1,0:T(8,128)(2,1)} %bitcast.210), channel_id=1, source_target_pairs={{0,1},{1,0},{2,3},{3,2},{4,5},{5,4},{6,7},{7,6},{8,9},{9,8},{10,11... | collective-permute-start | bytes 7077896 | tf_op jit(solution)/shard_map/ppermute | solution.py:569
  435.0 16.7 %collective-permute-start.34 = (bf16[4,96,768]{2,1,0:T(8,128)(2,1)}, bf16[4,96,768]{2,1,0:T(8,128)(2,1)S(1)}, u32[]{:S(2)}, u32[]{:S(2)}) collective-permute-start(bf16[4,96,768]{2,1,0:T(8,128)(2,1)} %get-tuple-element.169.refs_9_), channel_id=1, source_target_pairs={{0,16},{8,24},{16,0},{24,8},{1,17},{9,25},{17,1},{25,9},{2,18},{10... | collective-permute-start | bytes 1769480 | tf_op jit(solution)/shard_map/ppermute | solution.py:569
  436.4 16.5 %collective-permute-start.35 = (bf16[4,96,768]{2,1,0:T(8,128)(2,1)}, bf16[4,96,768]{2,1,0:T(8,128)(2,1)S(1)}, u32[]{:S(2)}, u32[]{:S(2)}) collective-permute-start(bf16[4,96,768]{2,1,0:T(8,128)(2,1)} %get-tuple-element.170.refs_10_), channel_id=1, source_target_pairs={{0,8},{8,0},{16,24},{24,16},{1,9},{9,1},{17,25},{25,17},{2,10},{10... | collective-permute-start | bytes 1769480 | tf_op jit(solution)/shard_map/ppermute | solution.py:569
  437.4 23.7 %collective-permute-start.36 = (bf16[4,96,768]{2,1,0:T(8,128)(2,1)}, bf16[4,96,768]{2,1,0:T(8,128)(2,1)}, u32[]{:S(2)}, u32[]{:S(2)}) collective-permute-start(bf16[4,96,768]{2,1,0:T(8,128)(2,1)} %get-tuple-element.171.refs_11_), channel_id=1, source_target_pairs={{0,8},{8,0},{16,24},{24,16},{1,9},{9,1},{17,25},{25,17},{2,10},{10... | collective-permute-start | bytes 1769480 | tf_op jit(solution)/shard_map/ppermute | solution.py:569
  439.1 22.0 %collective-permute-start.37 = (bf16[4,96,768]{2,1,0:T(8,128)(2,1)}, bf16[4,96,768]{2,1,0:T(8,128)(2,1)}, u32[]{:S(2)}, u32[]{:S(2)}) collective-permute-start(bf16[4,96,768]{2,1,0:T(8,128)(2,1)} %get-tuple-element.172.refs_12_), channel_id=1, source_target_pairs={{0,16},{8,24},{16,0},{24,8},{1,17},{9,25},{17,1},{25,9},{2,18},{10... | collective-permute-start | bytes 1769480 | tf_op jit(solution)/shard_map/ppermute | solution.py:569
  490.8 28.8 %collective-permute-start.53 = (bf16[2,96,768]{2,1,0:T(8,128)(2,1)}, bf16[2,96,768]{2,1,0:T(8,128)(2,1)}, u32[]{:S(2)}, u32[]{:S(2)}) collective-permute-start(bf16[2,96,768]{2,1,0:T(8,128)(2,1)} %get-tuple-element.187.refs_8_), channel_id=1, source_target_pairs={{0,2},{1,3},{2,0},{3,1},{4,6},{5,7},{6,4},{7,5},{8,10},{9,11},{10,... | collective-permute-start | bytes 884744 | tf_op jit(solution)/shard_map/ppermute | solution.py:569
  491.3 31.3 %collective-permute-start.54 = (bf16[2,96,768]{2,1,0:T(8,128)(2,1)}, bf16[2,96,768]{2,1,0:T(8,128)(2,1)}, u32[]{:S(2)}, u32[]{:S(2)}) collective-permute-start(bf16[2,96,768]{2,1,0:T(8,128)(2,1)} %get-tuple-element.188.refs_9_), channel_id=1, source_target_pairs={{0,2},{1,3},{2,0},{3,1},{4,6},{5,7},{6,4},{7,5},{8,10},{9,11},{10,... | collective-permute-start | bytes 884744 | tf_op jit(solution)/shard_map/ppermute | solution.py:569
  492.8 70.9 %collective-permute-start.57 = (bf16[8,96,768]{2,1,0:T(8,128)(2,1)}, bf16[8,96,768]{2,1,0:T(8,128)(2,1)}, u32[]{:S(2)}, u32[]{:S(2)}) collective-permute-start(bf16[8,96,768]{2,1,0:T(8,128)(2,1)} %get-tuple-element.191.refs_12_), channel_id=1, source_target_pairs={{0,8},{8,0},{16,24},{24,16},{1,9},{9,1},{17,25},{25,17},{2,10},{10... | collective-permute-start | bytes 3538952 | tf_op jit(solution)/shard_map/ppermute | solution.py:569
  494.3 69.5 %collective-permute-start.59 = (bf16[16,96,768]{2,1,0:T(8,128)(2,1)}, bf16[16,96,768]{2,1,0:T(8,128)(2,1)}, u32[]{:S(2)}, u32[]{:S(2)}) collective-permute-start(bf16[16,96,768]{2,1,0:T(8,128)(2,1)} %bitcast.212), channel_id=1, source_target_pairs={{0,1},{1,0},{2,3},{3,2},{4,5},{5,4},{6,7},{7,6},{8,9},{9,8},{10,11... | collective-permute-start | bytes 7077896 | tf_op jit(solution)/shard_map/ppermute | solution.py:569
  519.6 44.2 %collective-permute-start.58 = (bf16[8,96,768]{2,1,0:T(8,128)(2,1)S(1)}, bf16[8,96,768]{2,1,0:T(8,128)(2,1)S(1)}, u32[]{:S(2)}, u32[]{:S(2)}) collective-permute-start(bf16[8,96,768]{2,1,0:T(8,128)(2,1)S(1)} %copy-done.83), channel_id=1, source_target_pairs={{0,16},{8,24},{16,0},{24,8},{1,17},{9,25},{17,1},{25,9},{2,18},{10... | collective-permute-start | bytes 3538952 | tf_op jit(solution)/shard_map/ppermute | solution.py:569
  522.6 31.1 %collective-permute-start.55 = (bf16[2,96,768]{2,1,0:T(8,128)(2,1)S(1)}, bf16[2,96,768]{2,1,0:T(8,128)(2,1)S(1)}, u32[]{:S(2)}, u32[]{:S(2)}) collective-permute-start(bf16[2,96,768]{2,1,0:T(8,128)(2,1)S(1)} %copy-done.85), channel_id=1, source_target_pairs={{0,16},{8,24},{16,0},{24,8},{1,17},{9,25},{17,1},{25,9},{2,18},{10... | collective-permute-start | bytes 884744 | tf_op jit(solution)/shard_map/ppermute | solution.py:569
  531.6 23.6 %collective-permute-start.46 = (f32[3,96]{1,0:T(4,128)S(1)}, f32[3,96]{1,0:T(4,128)S(1)}, u32[]{:S(2)}, u32[]{:S(2)}) collective-permute-start(f32[3,96]{1,0:T(4,128)S(1)} %get-tuple-element.319), channel_id=1, source_target_pairs={{0,1},{1,0},{2,3},{3,2},{4,5},{5,4},{6,7},{7,6},{8,9},{9,8},{10,11... | collective-permute-start | bytes 3464 | tf_op jit(solution)/shard_map/ppermute | solution.py:569
  589.2 25.9 %collective-permute-start.67 = (bf16[4,96,768]{2,1,0:T(8,128)(2,1)}, bf16[4,96,768]{2,1,0:T(8,128)(2,1)}, u32[]{:S(2)}, u32[]{:S(2)}) collective-permute-start(bf16[4,96,768]{2,1,0:T(8,128)(2,1)} %get-tuple-element.221), channel_id=1, source_target_pairs={{0,8},{8,0},{16,24},{24,16},{1,9},{9,1},{17,25},{25,17},{2,10},{10... | collective-permute-start | bytes 1769480 | tf_op jit(solution)/shard_map/ppermute | solution.py:569
  591.1 24.1 %collective-permute-start.68 = (bf16[4,96,768]{2,1,0:T(8,128)(2,1)}, bf16[4,96,768]{2,1,0:T(8,128)(2,1)}, u32[]{:S(2)}, u32[]{:S(2)}) collective-permute-start(bf16[4,96,768]{2,1,0:T(8,128)(2,1)} %get-tuple-element.223), channel_id=1, source_target_pairs={{0,16},{8,24},{16,0},{24,8},{1,17},{9,25},{17,1},{25,9},{2,18},{10... | collective-permute-start | bytes 1769480 | tf_op jit(solution)/shard_map/ppermute | solution.py:569
  592.3 51.0 %collective-permute-start.52 = (bf16[2,8,6,4608]{3,1,2,0:T(8,128)(2,1)S(1)}, bf16[2,8,6,4608]{3,1,2,0:T(8,128)(2,1)S(1)}, u32[]{:S(2)}, u32[]{:S(2)}) collective-permute-start(bf16[2,8,6,4608]{3,1,2,0:T(8,128)(2,1)S(1)} %copy.73), channel_id=1, source_target_pairs={{0,8},{8,0},{16,24},{24,16},{1,9},{9,1},{17,25},{25,17},{2,10},{10... | collective-permute-start | bytes 2654216 | tf_op jit(solution)/shard_map/ppermute | solution.py:569
  644.3 31.7 %collective-permute-start.93 = (bf16[2,96,768]{2,1,0:T(8,128)(2,1)}, bf16[2,96,768]{2,1,0:T(8,128)(2,1)S(1)}, u32[]{:S(2)}, u32[]{:S(2)}) collective-permute-start(bf16[2,96,768]{2,1,0:T(8,128)(2,1)} %get-tuple-element.246.refs_12_), channel_id=1, source_target_pairs={{0,24},{8,16},{16,8},{24,0},{1,25},{9,17},{17,9},{25,1},{2,26},{10... | collective-permute-start | bytes 884744 | tf_op jit(solution)/shard_map/ppermute | solution.py:569
  645.9 31.6 %collective-permute-start.92 = (bf16[2,96,768]{2,1,0:T(8,128)(2,1)}, bf16[2,96,768]{2,1,0:T(8,128)(2,1)S(1)}, u32[]{:S(2)}, u32[]{:S(2)}) collective-permute-start(bf16[2,96,768]{2,1,0:T(8,128)(2,1)} %get-tuple-element.246.refs_12_), channel_id=1, source_target_pairs={{0,16},{8,24},{16,0},{24,8},{1,17},{9,25},{17,1},{25,9},{2,18},{10... | collective-permute-start | bytes 884744 | tf_op jit(solution)/shard_map/ppermute | solution.py:569
  659.4 20.5 %collective-permute-start.91 = (bf16[2,96,768]{2,1,0:T(8,128)(2,1)}, bf16[2,96,768]{2,1,0:T(8,128)(2,1)S(1)}, u32[]{:S(2)}, u32[]{:S(2)}) collective-permute-start(bf16[2,96,768]{2,1,0:T(8,128)(2,1)} %get-tuple-element.246.refs_12_), channel_id=1, source_target_pairs={{0,8},{8,0},{16,24},{24,16},{1,9},{9,1},{17,25},{25,17},{2,10},{10... | collective-permute-start | bytes 884744 | tf_op jit(solution)/shard_map/ppermute | solution.py:569
  679.9 21.1 %collective-permute-start.87 = (bf16[2,96,768]{2,1,0:T(8,128)(2,1)S(1)}, bf16[2,96,768]{2,1,0:T(8,128)(2,1)S(1)}, u32[]{:S(2)}, u32[]{:S(2)}) collective-permute-start(bf16[2,96,768]{2,1,0:T(8,128)(2,1)S(1)} %copy-done.42), channel_id=1, source_target_pairs={{0,24},{8,16},{16,8},{24,0},{1,25},{9,17},{17,9},{25,1},{2,26},{10... | collective-permute-start | bytes 884744 | tf_op jit(solution)/shard_map/ppermute | solution.py:569
  681.8 19.2 %collective-permute-start.86 = (bf16[2,96,768]{2,1,0:T(8,128)(2,1)S(1)}, bf16[2,96,768]{2,1,0:T(8,128)(2,1)S(1)}, u32[]{:S(2)}, u32[]{:S(2)}) collective-permute-start(bf16[2,96,768]{2,1,0:T(8,128)(2,1)S(1)} %copy-done.42), channel_id=1, source_target_pairs={{0,16},{8,24},{16,0},{24,8},{1,17},{9,25},{17,1},{25,9},{2,18},{10... | collective-permute-start | bytes 884744 | tf_op jit(solution)/shard_map/ppermute | solution.py:569
  682.5 18.6 %collective-permute-start.85 = (bf16[2,96,768]{2,1,0:T(8,128)(2,1)S(1)}, bf16[2,96,768]{2,1,0:T(8,128)(2,1)S(1)}, u32[]{:S(2)}, u32[]{:S(2)}) collective-permute-start(bf16[2,96,768]{2,1,0:T(8,128)(2,1)S(1)} %copy-done.42), channel_id=1, source_target_pairs={{0,8},{8,0},{16,24},{24,16},{1,9},{9,1},{17,25},{25,17},{2,10},{10... | collective-permute-start | bytes 884744 | tf_op jit(solution)/shard_map/ppermute | solution.py:569
  683.4 17.5 %collective-permute-start.83 = (bf16[1,96,768]{2,1,0:T(8,128)(2,1)S(1)}, bf16[1,96,768]{2,1,0:T(8,128)(2,1)S(1)}, u32[]{:S(2)}, u32[]{:S(2)}) collective-permute-start(bf16[1,96,768]{2,1,0:T(8,128)(2,1)S(1)} %copy-done.27), channel_id=1, source_target_pairs={{0,16},{8,24},{16,0},{24,8},{1,17},{9,25},{17,1},{25,9},{2,18},{10... | collective-permute-start | bytes 442376 | tf_op jit(solution)/shard_map/ppermute | solution.py:569
  (137 other events, 1678.3 us)
Sparse Core Ops, SparseCore 0:
  15.4 158.7 all-gather.1

commit v3 on v2

--- a/solution.py
+++ b/solution.py
@@ -584,22 +584,6 @@
                 stack = jnp.concatenate([stack, self.swap(stack, axis, step)])
         return stack
 
-    def gather_steps(self, values, axis):
-        stack = values[None]
-        for step in self.bits(axis)[::-1]:
-            got = self.swap(stack, axis, step)
-            yield [stack]
-            stack = jnp.concatenate([stack, got])
-        return stack
-
-    def total_steps(self, values):
-        for axis in ("shard", "replica"):
-            for step in self.bits(axis):
-                got = self.swap(values, axis, step)
-                yield [values]
-                values = values + got
-        return values
-
     def order(self, axis):
         found = [0]
         for step in self.bits(axis)[::-1]:
@@ -724,7 +708,7 @@
 
 
 class Fold:
-    def __init__(self, net, pairs):
+    def __init__(self, net, pairs, lazy):
         self.net = net
         near, places, rows, width = pairs[0][0].shape
         ahead = [("replica", step) for step in net.bits("replica")]
@@ -733,8 +717,10 @@
         flat = (near * places, rows, width)
         keeps = [keep.reshape(flat) for keep, _ in pairs]
         gives = [give.reshape(flat) for _, give in pairs]
-        self.gots = [net.swap(give, "shard", 1) for give in gives]
-        self.sent = gives
+        self.lazy = lazy
+        self.gives = gives
+        self.sent = [] if lazy else gives
+        self.gots = [None if lazy else net.swap(give, "shard", 1) for give in gives]
         labels = [(2 * t, q) for t in range(near) for q in range(places)]
         self.single = len(pairs) == 1
         if self.single:
@@ -744,23 +730,31 @@
                 Part((keeps[0], half), labels[half:], behind + shard_route[:-1]),
             ]
             self.last = shard_route[-1]
-            for part, start in zip(self.parts, (0, half)):
-                part.got = (self.gots[0], start)
+            starts = (0, half)
         else:
             self.parts = [
                 Part((keeps[0], 0), labels, ahead + shard_route),
                 Part((keeps[1], 0), labels, behind + shard_route),
             ]
-            for part, got in zip(self.parts, self.gots):
-                part.got = (got, 0)
+            starts = (0, 0)
+        self.starts = starts
         self.every = None
         self.merge = False
+        self.arm()
+
+    def arm(self):
+        gots = self.gots * 2 if self.single else self.gots
+        for part, got, start in zip(self.parts, gots, self.starts):
+            part.got = (got, start)
 
     def jobs(self):
         if self.every is not None:
             return [], []
         first = self.parts[0]
         rows, width = first.keep[0].shape[1:]
+        if self.lazy:
+            shapes = [give.shape for give in self.gives]
+            return [(give, None, i) for i, give in enumerate(self.gives)], shapes
         if self.merge or not first.route:
             if self.single and not self.merge:
                 a, b = self.parts
@@ -783,6 +777,11 @@
         if self.every is not None:
             return []
         net = self.net
+        if self.lazy:
+            self.lazy = False
+            self.gots = [net.swap(give, "shard", 1) for give in outs]
+            self.arm()
+            return list(outs)
         if self.merge or not self.parts[0].route:
             if self.single and not self.merge:
                 self.merge = True
@@ -805,9 +804,75 @@
         return sent
 
 
-def round_kernel(jobs, *refs):
+class Line:
+    def __init__(self, net, value, axes, sums=False, lower_at=None):
+        self.net = net
+        self.value = value
+        self.sums = sums
+        self.lower_at = lower_at
+        self.route = [(axis, step) for axis in axes for step in net.bits(axis)[::-1]]
+        self.count = 0
+        self.full = None
+        self.got = None
+        self.over = False
+        self.sent = self.send()
+
+    def send(self):
+        if not self.route:
+            self.over = True
+            return []
+        axis, step = self.route.pop(0)
+        self.got = self.net.swap(self.value, axis, step)
+        return [self.value]
+
+    def outs(self):
+        if self.over:
+            return []
+        dims = self.value.shape
+        if not self.sums:
+            dims = (2 * dims[0],) + dims[1:]
+        outs = [shape_of(dims, self.value.dtype)]
+        if self.count + 1 == self.lower_at:
+            outs.append(shape_of(dims, low_type))
+        return outs
+
+    def take(self, outs):
+        if self.over:
+            return []
+        self.count += 1
+        self.value = outs[0]
+        if self.count == self.lower_at:
+            self.full, self.value = outs
+        return self.send()
+
+    def end(self):
+        while not self.over:
+            if self.sums:
+                both = self.value + self.got
+            else:
+                both = jnp.concatenate([self.value, self.got])
+            self.take([both.astype(out.dtype) for out in self.outs()])
+        return self.value
+
+
+def line_kernel(sums, value_ref, got_ref, *out_refs):
+    count = value_ref.shape[0]
+    for out_ref in out_refs:
+        if sums:
+            out_ref[...] = value_ref[...] + got_ref[...]
+        else:
+            out_ref[:count] = value_ref[...].astype(out_ref.dtype)
+            out_ref[count:] = got_ref[...].astype(out_ref.dtype)
+
+
+def round_kernel(jobs, line_jobs, *refs):
+    for sums, value, got, outs in line_jobs:
+        line_kernel(sums, refs[value], refs[got], *[refs[out] for out in outs])
     place = [0] * 64
     for keep, got, blocks, keep_at, got_at, out in jobs:
+        if blocks is None:
+            refs[out][...] = refs[keep][...]
+            continue
         for block in blocks:
             refs[out][place[out]] = (
                 refs[keep][keep_at + block].astype(wide) + refs[got][got_at + block].astype(wide)
@@ -815,7 +880,7 @@
             place[out] += 1
 
 
-def run_round(folds, after=()):
+def run_round(folds, lines=(), after=()):
     arrays, jobs, shapes, counts = [], [], [], []
 
     def slot(array):
@@ -829,34 +894,51 @@
     for fold in folds:
         fold_jobs, outs = fold.jobs()
         for part, blocks, out in fold_jobs:
+            if blocks is None:
+                place = slot(part)
+                listed.append((place, place, None, 0, 0, len(shapes) + out))
+                continue
             keep, keep_at = part.keep
             got, got_at = part.got
             listed.append((slot(keep), slot(got), blocks, keep_at, got_at, len(shapes) + out))
         shapes += outs
         counts.append(len(outs))
+    shapes = [shape_of(dims, low_type) for dims in shapes]
+    line_listed = []
+    for line in lines:
+        outs = line.outs()
+        if outs:
+            places = range(len(shapes), len(shapes) + len(outs))
+            line_listed.append((line.sums, slot(line.value), slot(line.got), places))
+            shapes += outs
+        counts.append(len(outs))
     if not shapes:
         return []
     first_out = len(arrays) + len(after)
     jobs = [job[:5] + (first_out + job[5],) for job in listed]
+    line_jobs = [job[:3] + ([first_out + i for i in job[3]],) for job in line_listed]
     outs = pl.pallas_call(
-        functools.partial(round_kernel, jobs),
+        functools.partial(round_kernel, jobs, line_jobs),
         in_specs=[pl.BlockSpec(memory_space=pltpu.VMEM)] * len(arrays)
         + [pl.BlockSpec(memory_space=pl.ANY)] * len(after),
         out_specs=[pl.BlockSpec(memory_space=pltpu.VMEM)] * len(shapes),
-        out_shape=[shape_of(dims, low_type) for dims in shapes],
+        out_shape=shapes,
         compiler_params=pltpu.CompilerParams(vmem_limit_bytes=58 * 2**20),
         name="round",
     )(*arrays, *after)
     sent = []
-    for fold, count in zip(folds, counts):
+    for fold, count in zip(list(folds) + list(lines), counts):
         sent += fold.take(outs[:count])
         outs = outs[count:]
     return sent
 
 
-def finish_kernel(here_ref, *refs):
-    ins, (qkv_ref, proj_ref, up_ref, down_ref, at_ref, ff_ref) = refs[:-6], refs[-6:]
+def finish_kernel(steps, here_ref, *refs):
+    ins, (qkv_ref, proj_ref, up_ref, down_ref, back_ref, at_ref, ff_ref) = refs[:-7], refs[-7:]
     rows, width = proj_ref.shape[1:]
+    ins, parts = ins[: 2 * SLABS * LAYERS], ins[2 * SLABS * LAYERS :]
+    for step, part in zip(steps, parts):
+        back_ref[jnp.bitwise_xor(here_ref[0], step)] = part[...]
     for layer in range(LAYERS):
         at, ff = ins[:SLABS], ins[SLABS : 2 * SLABS]
         ins = ins[2 * SLABS :]
@@ -874,17 +956,18 @@
             down_ref[layer, place * rows : (place + 1) * rows] = ff_ref[place, 1].astype(wide)
 
 
-def finish(here, owned):
-    arrays = [part for at, ff in owned for part in (*at, *ff)]
+def finish(here, owned, back, steps):
+    arrays = [part for at, ff in owned for part in (*at, *ff)] + back
     rows, width = owned[0][0][0].shape[1:]
     outs = [
         shape_of((LAYERS, rows, 3 * width), wide),
         shape_of((LAYERS, rows, width), wide),
         shape_of((LAYERS, rows, SLABS * width), wide),
         shape_of((LAYERS, SLABS * rows, width), wide),
+        shape_of((len(back),) + back[0].shape, wide),
     ]
     return pl.pallas_call(
-        finish_kernel,
+        functools.partial(finish_kernel, steps),
         grid_spec=pltpu.PrefetchScalarGridSpec(
             num_scalar_prefetch=1,
             grid=(1,),
@@ -1077,8 +1160,7 @@
     packs = [pack(layer) for layer in range(LAYERS)]
     if fused:
         a0 = Steps(gather_steps(net, here, packs[0][0]))
-        f0 = Steps(gather_steps(net, here, jnp.concatenate(packs[0][1:], axis=1)))
-        later = gather_whole(net, here, jnp.concatenate(packs[1], axis=1))
+        later = gather_whole(net, here, jnp.concatenate(packs[1] + packs[0][1:], axis=1))
     else:
         wholes = [
             plain_slabs(net, gather_whole(net, here, jnp.concatenate(kinds, axis=1)), 2)
@@ -1095,8 +1177,8 @@
     spots = jnp.array([found.index(step) for step in range(shards)], jnp.int32)
     order = jnp.take(spots, jnp.bitwise_xor(jnp.arange(shards, dtype=jnp.int32), here[0]))
     bias_all = jnp.take(both_rel[:, latents_here:], order, axis=0)
-    cond_steps = Steps(net.gather_steps(cond_rel, "replica"))
     group = shards * latents_here
+    cond_line = Line(net, cond_rel.reshape(1, group, model_width), ["replica"])
     cond_rows = lax.dynamic_slice_in_dim(
         cond_rel.reshape(group, model_width), shard * rows, rows, axis=1
     )
@@ -1125,21 +1207,15 @@
         return (qkv_b[:, None], proj[None], up_b, down[None])
 
     def attn_first():
-        a0.go(2)
-        a0.go(), f0.go()
-        a0.go(), f0.go()
-        a0.go()
-        after = f0.go()
-        return (a0.end(), 0), after
-
-    def feed_first():
-        both = f0.end()
-        return (both, 0), (both, 1), cond_steps.go()
+        return (a0.end(), 0), []
 
     if fused:
         attn_calls = (attn_first, lambda: ((later, 0), []))
-        feed_calls = (feed_first, lambda: ((later, 1), (later, 2), cond_steps.go()))
-        slot_calls = (lambda: f0.go(), lambda: [])
+        feed_calls = (
+            lambda: ((later, 3), (later, 4), []),
+            lambda: ((later, 1), (later, 2), []),
+        )
+        slot_calls = [lambda: []] * LAYERS
     else:
         attn_calls = [lambda w=w: ((w, 0), []) for w in wholes]
         feed_calls = [lambda w=w: ((w, 1), (w, 2), []) for w in wholes]
@@ -1164,9 +1240,9 @@
     result = current * live_rows
     grad_now = out_grad * live_rows
 
-    def send(grads):
+    def send(grads, lazy):
         if fused:
-            return Fold(net, list(zip(grads[::2], grads[1::2])))
+            return Fold(net, list(zip(grads[::2], grads[1::2])), lazy)
         slabs = [grads[0].reshape(SLABS, shards, rows, model_width)]
         if len(grads) > 1:
             down = grads[1].reshape(shards, SLABS, rows, model_width)
@@ -1175,7 +1251,7 @@
         return Steps(reduce_steps(net, here, pairs))
 
     sends = {}
-    bias_steps = [None]
+    bias_line = [None]
 
     def bias_row(layer, sums, up_sums, down_sums):
         grads = (
@@ -1186,14 +1262,16 @@
         )
         bias_sums[layer] = jnp.concatenate([grad.reshape(shards, -1) for grad in grads], axis=1)
         if layer == 0:
-            bias_steps[0] = Steps(net.total_steps(jnp.stack(bias_sums)))
+            bias_line[0] = Line(net, jnp.stack(bias_sums), ["shard", "replica"], sums=True)
 
     def middle_slot(layer):
         def slot(ff_grads):
-            fold = sends["ff", layer] = send(ff_grads)
+            fold = sends["ff", layer] = send(ff_grads, layer == 0)
             if not fused:
                 return []
-            return fold.sent + (run_round([sends["ff", 1], sends["at", 1]]) if layer == 0 else [])
+            if layer == 1:
+                return fold.sent
+            return run_round([sends["ff", 1], sends["at", 1], fold])
 
         return slot
 
@@ -1203,9 +1281,8 @@
             if not fused:
                 return []
             if layer == 1:
-                return run_round([sends["ff", 1]])
-            sent = bias_steps[0].go()
-            return sent + run_round([sends["ff", 1], sends["at", 1], sends["ff", 0]])
+                return run_round([sends["ff", 1]], [cond_line])
+            return bias_line[0].sent + run_round([sends["ff", 1], sends["at", 1], sends["ff", 0]])
 
         return slot
 
@@ -1215,7 +1292,9 @@
     modul_grads = [None] * LAYERS
     bias_sums = [None] * LAYERS
     for layer in reversed(range(LAYERS)):
-        before = sends["at", 1].sent if layer == 0 and fused else []
+        before = []
+        if layer == 0 and fused:
+            before = run_round([sends["ff", 1], sends["at", 1]], [cond_line])
         grad_now, grad_modul, at_grads = backward_layer(
             here,
             fused,
@@ -1226,25 +1305,27 @@
             middle_slot(layer),
             late_slot(layer),
         )
-        sends["at", layer] = send(at_grads)
+        sends["at", layer] = send(at_grads, True)
         modul_grads[layer] = grad_modul
-    modul_steps = Steps(net.gather_steps(jnp.concatenate(modul_grads), "shard"))
-    bias_steps = bias_steps[0]
-    ring = [sends["ff", 1], sends["at", 1], sends["ff", 0], sends["at", 0]]
-    every_steps = None
-    for turn in range(8):
-        after = modul_steps.go() + bias_steps.go()
-        if modul_steps.over and every_steps is None:
-            modul_low = modul_steps.result.astype(low_type)
-            every_steps = Steps(net.gather_steps(modul_low, "replica"))
-        if every_steps is not None:
-            after += every_steps.go()
-        if fused:
-            run_round(ring, after)
-    modul = modul_steps.end()
-    modul_low = every_steps.end()
+    lines = [
+        bias_line[0],
+        cond_line,
+        Line(
+            net,
+            jnp.concatenate(modul_grads)[None],
+            ["shard", "replica"],
+            lower_at=len(net.bits("shard")),
+        ),
+    ]
+    if fused:
+        ring = [sends["ff", 1], sends["at", 1], sends["ff", 0], sends["at", 0]]
+        while any(fold.every is None for fold in ring) or not all(line.over for line in lines):
+            run_round(ring, lines)
+    bias_total, cond_all, modul_low = [line.end() for line in lines]
+    modul = lines[2].full
+    modul_low = modul_low.reshape((replicas, shards) + modul_low.shape[1:])
     cond_every = lax.dynamic_slice_in_dim(
-        cond_steps.end().reshape(replicas * group, model_width), shard * rows, rows, axis=1
+        cond_all.reshape(replicas * group, model_width), shard * rows, rows, axis=1
     )
     per_layer = lambda w, layer: w[..., layer * latents_here : (layer + 1) * latents_here, :]
     for layer in range(LAYERS):
@@ -1255,22 +1336,21 @@
     own_mod = lax.dynamic_slice_in_dim(modul_low, shard * ada_part, ada_part, axis=3).astype(wide)
     own_mod = own_mod.reshape(replicas * shards, LAYERS, latents_here, ada_part)
     ada_bias_out = jnp.sum(own_mod, axis=(0, 2))
-    bias_total = bias_steps.end()
     bias_mine = lax.dynamic_index_in_dim(bias_total, shard, 1, keepdims=False)
     bias_out = [bias_mine[:, start : start + width] for start, width in zip(starts, widths)]
 
+    parts = grad_cond.reshape(shards, latents_here, rows)
+    back = [parts[0]]
+    back += [net.swap(parts[i], "shard", found[i]) for i in range(1, shards)]
     if fused:
         owned = [(sends["at", layer].every, sends["ff", layer].every) for layer in range(LAYERS)]
-        weight_outs = finish(here, owned)
+        *weight_outs, back = finish(here, owned, back, found)
     else:
         owned = [
             (sends["at", layer].end(), sends["ff", layer].end()) for layer in range(LAYERS)
         ]
         weight_outs = finish_plain(here, owned, replicas)
-    parts = grad_cond.reshape(shards, latents_here, rows)
-    back = [parts[0]]
-    back += [net.swap(parts[i], "shard", found[i]) for i in range(1, shards)]
-    back = jnp.take(jnp.stack(back), order, axis=0)
+        back = jnp.take(jnp.stack(back), order, axis=0)
     cond_back = back.transpose(1, 0, 2).reshape(latents_here, model_width)
     grad_condition = jax.vjp(jax.nn.silu, condition)[1](cond_back)[0]
     return (

time: 720 us -> 693 us (0.963); the launches traced: 716 us -> 681 us
  waiting for transfers between devices: 238 us -> 185 us
  local copies, waits for them, and re-layouts: 42.8 us -> 62.3 us
  Pallas kernels: 292 us -> 304 us
    ppermute x95 -> x84, waiting for transfers between devices: 238 us -> 125 us  [swap(): return lax.ppermute(values, axis, [(i, i ^ step) for i in range(count)])]
    all_gather x1, waiting for transfers between devices: 0.02 us -> 60.1 us  [gather_whole(): whole = lax.all_gather(flat, ('replica', 'shard'), axis=0, tiled=True)]
    pallas_call x9 -> x11, Pallas kernels: 44.7 us -> 58.7 us  [the longest x10 52.7 us: run_round(): pl.pallas_call(functools.partial(round_kernel, jobs, line_jobs), in_specs...]
    pallas_call x2 -> x1, Pallas kernels: 19.1 us -> 8.18 us  [place_weights(): pl.pallas_call(place_kernel, grid_spec=pltpu.PrefetchScalarGridSpec(num_s...]
    pallas_call x12, Pallas kernels: 228 us -> 237 us  [call(): return lambda *arrays: run(here, *arrays, *after)]
    ppermute x95 -> x84, starting transfers between devices: 88.3 us -> 81.5 us  [swap(): return lax.ppermute(values, axis, [(i, i ^ step) for i in range(count)])]
    unnamed x190 -> x234, local copies, waits for them, and re-layouts: 10.2 us -> 16 us
  transfers between devices with their start and end apart: 96 -> 85, of which waited for: 44 -> 26; matrix products, arithmetic and copies ran while one was open for 9% -> 9% of each run, Pallas kernels for 23% -> 24%
where the time goes in v3:
time: 693 us; the launch traced here: 681 us
  Pallas kernels  304 us (44%)
  waiting for transfers between devices  185 us (27%)
  starting transfers between devices  81.6 us (12%)
  local copies, waits for them, and re-layouts  62.3 us (9%)
  other arithmetic  27 us (4%)
  between operations  15.9 us (2%)
    pallas_call x12, Pallas kernels, call(): return lambda *arrays: run(here, *arrays, *after)  237 us
    ppermute x84, waiting for transfers between devices, swap(): return lax.ppermute(values, axis, [(i, i ^ step) for i in range(count)])  125 us
    ppermute x84, starting transfers between devices, swap(): return lax.ppermute(values, axis, [(i, i ^ step) for i in range(count)])  81.5 us
    all_gather x1, waiting for transfers between devices, gather_whole(): whole = lax.all_gather(flat, ('replica', 'shard'), axis=0, tiled=True)  60.1 us
    pallas_call x10, Pallas kernels, run_round(): pl.pallas_call(functools.partial(round_kernel, jobs, line_jobs), in_specs...  52.7 us
    unnamed x234, local copies, waits for them, and re-layouts  16 us
  transfers between devices with their start and end apart: 85, of which 26 were waited for; matrix products, arithmetic and copies ran while one was open for 9% of the time, Pallas kernels for 24%

profile of v3, /device:TPU:0, one launch (start us, length us, event | category | flops | bytes accessed | tf_op | source)
XLA Modules:
  0.0 681.0 jit_solution(8014118040366057131)
XLA Ops:
  17.4 4.0 collective-permute-start
  25.7 2.5 collective-permute-done.1
  42.6 12.4 %collective-permute-done.8 = bf16[2,1,96,768]{3,2,0,1:T(8,128)(2,1)S(1)} collective-permute-done((bf16[2,1,96,768]{3,2,0,1:T(8,128)(2,1)S(1)}, bf16[2,1,96,768]{3,2,0,1:T(8,128)(2,1)S(1)}, u32[]{:S(2)}, u32[]{:S(2)}) %collective-permute-start.8) | collective-permute-done | bytes 294944 | tf_op jit(solution)/shard_map/ppermute | solution.py:569
  61.0 4.8 collective-permute-done.9
  70.5 9.3 %collective-permute-done.4 = f32[2,3,2,4608]{3,2,1,0:T(2,128)S(1)} collective-permute-done((f32[2,3,2,4608]{3,2,1,0:T(2,128)S(1)}, f32[2,3,2,4608]{3,2,1,0:T(2,128)S(1)}, u32[]{:S(2)}, u32[]{:S(2)}) %collective-permute-start.4) | collective-permute-done | bytes 221216 | tf_op jit(solution)/shard_map/ppermute | solution.py:569
  85.3 3.4 collective-permute-done.5
  93.4 8.2 %place_weights.1.refs_2_.refs_3_.refs_6_ = bf16[4,8,1,96,768]{4,3,2,1,0:T(8,128)(2,1)} custom-call(s32[2]{0:T(128)} %pad_add_fusion.here_ref, bf16[4,1,96,768]{3,2,1,0:T(8,128)(2,1)} %copy-done.3, bf16[4,1,96,768]{3,2,1,0:T(8,128)(2,1)} %copy-done.17, bf16[2,3,1,48,768]{4,3,2,1,0:T(8,128)(2,1)} %get-tuple-element.329.refs_0_, ...), custom_call_target="tpu_custom_call" | custom-call | tf_op jit(solution)/shard_map/place_weights/pallas_call | solution.py:1040
  101.5 8.4 %qkv_kernel.2 = (bf16[768,768]{1,0:T(8,128)(2,1)}, bf16[3,768,768]{2,1,0:T(8,128)(2,1)}) custom-call(s32[2]{0:T(128)} %pad_add_fusion.here_ref, f32[3,256,768]{2,1,0:T(8,128)} %refs_4_.1, f32[3,6,768]{2,1,0:T(8,128)} %reshape_squeeze.12.refs_1_.refs_2_.refs_5_.refs_6_, bf16[4,8,1,96,768]{4,3,2,1,0:T(8,128)(2,1)} %place_weights.1.refs_2_.refs_3_.refs_6_, ...), custom_call_target="tpu_custom_call" | custom-call | flops 2717908992 | bytes 10616832 | tf_op jit(solution)/shard_map/qkv_kernel/pallas_call | solution.py:380
  109.9 12.8 %mix_kernel.2 = (bf16[768,768]{1,0:T(8,128)(2,1)}, f32[768,768]{1,0:T(8,128)}, f32[768,768]{1,0:T(8,128)}, bf16[768,768]{1,0:T(8,128)(2,1)}) custom-call(s32[2]{0:T(128)} %pad_add_fusion.here_ref, bf16[3,768,768]{2,1,0:T(8,128)(2,1)} %get-tuple-element.150.refs_0_.refs_4_, f32[3,256,768]{2,1,0:T(8,128)} %refs_4_.1, ...), custom_call_target="tpu_custom_call" | custom-call | flops 4529848320 | bytes 14155776 | tf_op jit(solution)/shard_map/mix_kernel/pallas_call | solution.py:380
  122.7 60.1 %all-gather.2.cloned.1.call-done = bf16[15360,768]{1,0:T(8,128)(2,1)} async-done(((bf16[480,768]{1,0:T(8,128)(2,1)}), bf16[15360,768]{1,0:T(8,128)(2,1)}) %all-gather.2.cloned.1.call-update) | async-done | bytes 23592976 | tf_op jit(solution)/shard_map/all_gather | solution.py:1082
  182.8 21.8 %feed_kernel.2 = (bf16[4,768,768]{2,1,0:T(8,128)(2,1)}, bf16[4,768,768]{2,1,0:T(8,128)(2,1)}, f32[768,768]{1,0:T(8,128)}, f32[768,768]{1,0:T(8,128)}) custom-call(s32[2]{0:T(128)} %pad_add_fusion.here_ref, bf16[768,768]{1,0:T(8,128)(2,1)} %get-tuple-element.151.refs_0_.refs_3_, f32[768,768]{1,0:T(8,128)} %get-tuple-element.152.refs_1_, ...), custom_call_target="tpu_custom_call" | custom-call | flops 10871635968 | bytes 23592960 | tf_op jit(solution)/shard_map/feed_kernel/pallas_call | solution.py:380
  204.6 8.4 %qkv_kernel.3 = (bf16[768,768]{1,0:T(8,128)(2,1)}, bf16[3,768,768]{2,1,0:T(8,128)(2,1)}) custom-call(s32[2]{0:T(128)} %pad_add_fusion.here_ref, f32[3,256,768]{2,1,0:T(8,128)} %bitcast.154, f32[3,6,768]{2,1,0:T(8,128)} %reshape_squeeze.13.refs_1_.refs_2_.refs_5_.refs_6_, bf16[4,8,5,96,768]{4,3,2,1,0:T(8,128)(2,1)} %bitcast.144, ...), custom_call_target="tpu_custom_call" | custom-call | flops 2717908992 | bytes 10616832 | tf_op jit(solution)/shard_map/qkv_kernel/pallas_call | solution.py:380
  213.0 11.8 %mix_kernel.3 = (bf16[768,768]{1,0:T(8,128)(2,1)}, f32[768,768]{1,0:T(8,128)}, f32[768,768]{1,0:T(8,128)}, bf16[768,768]{1,0:T(8,128)(2,1)}) custom-call(s32[2]{0:T(128)} %pad_add_fusion.here_ref, bf16[3,768,768]{2,1,0:T(8,128)(2,1)} %get-tuple-element.154.refs_0_.refs_4_, f32[3,256,768]{2,1,0:T(8,128)} %bitcast.155, ...), custom_call_target="tpu_custom_call" | custom-call | flops 4529848320 | bytes 14155776 | tf_op jit(solution)/shard_map/mix_kernel/pallas_call | solution.py:380
  224.8 21.7 %feed_kernel.3 = (bf16[4,768,768]{2,1,0:T(8,128)(2,1)}, bf16[4,768,768]{2,1,0:T(8,128)(2,1)}, f32[768,768]{1,0:T(8,128)}, f32[768,768]{1,0:T(8,128)}) custom-call(s32[2]{0:T(128)} %pad_add_fusion.here_ref, bf16[768,768]{1,0:T(8,128)(2,1)} %get-tuple-element.155.refs_0_.refs_3_, f32[768,768]{1,0:T(8,128)} %get-tuple-element.156.refs_1_, ...), custom_call_target="tpu_custom_call" | custom-call | flops 10871635968 | bytes 23592960 | tf_op jit(solution)/shard_map/feed_kernel/pallas_call | solution.py:380
  246.5 4.4 broadcast_multiply_fusion
  250.8 29.5 %feed_back_kernel.2 = (bf16[4,4,96,768]{3,2,1,0:T(8,128)(2,1)}, bf16[4,4,96,768]{3,2,1,0:T(8,128)(2,1)}, bf16[4,4,96,768]{3,2,1,0:T(8,128)(2,1)}, bf16[4,4,96,76...) custom-call(s32[2]{0:T(128)} %pad_add_fusion.here_ref, ...), custom_call_target="tpu_custom_call" | custom-call | flops 14495514624 | bytes 29491200 | tf_op jit(solution)/shard_map/feed_back_kernel/pallas_call | solution.py:380
  282.5 2.5 collective-permute-done.19.refs_5_
  286.0 2.7 collective-permute-done.18.refs_3_
  288.7 6.2 round.10
  296.9 33.3 %mix_back_kernel.2 = (f32[768,768]{1,0:T(8,128)}, bf16[4,768,768]{2,1,0:T(8,128)(2,1)}, f32[3,3,768]{2,1,0:T(4,128)}, f32[4,768]{1,0:T(4,128)}) custom-call(s32[2]{0:T(128)} %pad_add_fusion.here_ref, f32[768,768]{1,0:T(8,128)} %get-tuple-element.165.refs_0_, f32[768,768]{1,0:T(8,128)} %get-tuple-element.156.refs_1_, f32[768,768]{1,0:T(8,128)} %bitcast.158, ...), custom_call_target="tpu_custom_call" | custom-call | flops 9059696640 | bytes 23592960 | tf_op jit(solution)/shard_map/mix_back_kernel/pallas_call | solution.py:380
  331.8 17.5 %qkv_back_kernel.2 = (bf16[4,4,96,768]{3,2,1,0:T(8,128)(2,1)}, bf16[4,4,96,768]{3,2,1,0:T(8,128)(2,1)}, f32[3,256,768]{2,1,0:T(8,128)}, f32[3,2,768]{2,1,0:T(2,128)}) custom-call(s32[2]{0:T(128)} %pad_add_fusion.here_ref, bf16[768,768]{1,0:T(8,128)(2,1)} %get-tuple-element.160.refs_0_, bf16[768,768]{1,0:T(8,128)(2,1)} %get-tuple-element.161.refs_1_, ...), custom_call_target="tpu_custom_call" | custom-call | flops 6341787648 | bytes 21233664 | tf_op jit(solution)/shard_map/qkv_back_kernel/pallas_call | solution.py:380
  350.8 5.6 round.11
  358.4 29.6 %feed_back_kernel.3 = (bf16[4,4,96,768]{3,2,1,0:T(8,128)(2,1)}, bf16[4,4,96,768]{3,2,1,0:T(8,128)(2,1)}, bf16[4,4,96,768]{3,2,1,0:T(8,128)(2,1)}, bf16[4,4,96,76...) custom-call(s32[2]{0:T(128)} %pad_add_fusion.here_ref, ...), custom_call_target="tpu_custom_call" | custom-call | flops 14495514624 | bytes 29491200 | tf_op jit(solution)/shard_map/feed_back_kernel/pallas_call | solution.py:380
  389.9 7.9 %round.12 = (bf16[2,96,768]{2,1,0:T(8,128)(2,1)}, bf16[2,96,768]{2,1,0:T(8,128)(2,1)}, bf16[2,96,768]{2,1,0:T(8,128)(2,1)}, bf16[2,96,768]{2,1,0:T(8,128)(2,1)},...) custom-call(bf16[4,96,768]{2,1,0:T(8,128)(2,1)} %get-tuple-element.1, ...), custom_call_target="tpu_custom_call" | custom-call | tf_op jit(solution)/shard_map/round/pallas_call | solution.py:920
  403.1 24.6 %mix_back_kernel.3 = (f32[768,768]{1,0:T(8,128)}, bf16[4,768,768]{2,1,0:T(8,128)(2,1)}, f32[3,3,768]{2,1,0:T(4,128)}, f32[4,768]{1,0:T(4,128)}) custom-call(s32[2]{0:T(128)} %pad_add_fusion.here_ref, f32[768,768]{1,0:T(8,128)} %get-tuple-element.186.refs_0_, f32[768,768]{1,0:T(8,128)} %get-tuple-element.152.refs_1_, f32[768,768]{1,0:T(8,128)} %bitcast.163, ...), custom_call_target="tpu_custom_call" | custom-call | flops 9059696640 | bytes 23592960 | tf_op jit(solution)/shard_map/mix_back_kernel/pallas_call | solution.py:380
  441.1 7.7 %round.13 = (bf16[1,96,768]{2,1,0:T(8,128)(2,1)}, bf16[1,96,768]{2,1,0:T(8,128)(2,1)}, bf16[1,96,768]{2,1,0:T(8,128)(2,1)}, bf16[1,96,768]{2,1,0:T(8,128)(2,1)},...) custom-call(bf16[2,96,768]{2,1,0:T(8,128)(2,1)} %get-tuple-element.2, ...), custom_call_target="tpu_custom_call" | custom-call | tf_op jit(solution)/shard_map/round/pallas_call | solution.py:920
  450.8 17.7 %qkv_back_kernel.3 = (bf16[4,4,96,768]{3,2,1,0:T(8,128)(2,1)}, bf16[4,4,96,768]{3,2,1,0:T(8,128)(2,1)}, f32[3,256,768]{2,1,0:T(8,128)}, f32[3,2,768]{2,1,0:T(2,128)}) custom-call(s32[2]{0:T(128)} %pad_add_fusion.here_ref, bf16[768,768]{1,0:T(8,128)(2,1)} %get-tuple-element.158.refs_0_, bf16[768,768]{1,0:T(8,128)(2,1)} %get-tuple-element.159.refs_1_, ...), custom_call_target="tpu_custom_call" | custom-call | flops 6341787648 | bytes 21233664 | tf_op jit(solution)/shard_map/qkv_back_kernel/pallas_call | solution.py:380
  474.0 9.5 %collective-permute-done.38.refs_14_ = f32[2,8,768]{2,1,0:T(8,128)S(1)} collective-permute-done((f32[2,8,768]{2,1,0:T(8,128)S(1)}, f32[2,8,768]{2,1,0:T(8,128)S(1)}, u32[]{:S(2)}, u32[]{:S(2)}) %collective-permute-start.38) | collective-permute-done | bytes 49184 | tf_op jit(solution)/shard_map/ppermute | solution.py:569
  486.1 8.1 %collective-permute-done.33.refs_3_ = bf16[1,96,768]{2,1,0:T(8,128)(2,1)S(1)} collective-permute-done((bf16[1,96,768]{2,1,0:T(8,128)(2,1)S(1)}, bf16[1,96,768]{2,1,0:T(8,128)(2,1)S(1)}, u32[]{:S(2)}, u32[]{:S(2)}) %collective-permute-start.33) | collective-permute-done | bytes 147488 | tf_op jit(solution)/shard_map/ppermute | solution.py:569
  495.9 6.5 round.14
  506.7 4.9 collective-permute-done.45.refs_11_
  513.6 9.3 %collective-permute-done.41.refs_3_ = bf16[1,96,768]{2,1,0:T(8,128)(2,1)S(1)} collective-permute-done((bf16[1,96,768]{2,1,0:T(8,128)(2,1)}, bf16[1,96,768]{2,1,0:T(8,128)(2,1)S(1)}, u32[]{:S(2)}, u32[]{:S(2)}) %collective-permute-start.41) | collective-permute-done | bytes 147488 | tf_op jit(solution)/shard_map/ppermute | solution.py:569
  524.8 5.6 round.15
  535.9 2.4 collective-permute-start.47
  539.3 11.9 %collective-permute-done.47.refs_1_ = bf16[1,96,768]{2,1,0:T(8,128)(2,1)S(1)} collective-permute-done((bf16[1,96,768]{2,1,0:T(8,128)(2,1)}, bf16[1,96,768]{2,1,0:T(8,128)(2,1)S(1)}, u32[]{:S(2)}, u32[]{:S(2)}) %collective-permute-start.47) | collective-permute-done | bytes 147488 | tf_op jit(solution)/shard_map/ppermute | solution.py:569
  554.1 4.5 round.16
  565.5 7.4 %collective-permute-done.59 = bf16[8,6,4608]{2,0,1:T(8,128)(2,1)S(1)} collective-permute-done((bf16[8,6,4608]{2,0,1:T(8,128)(2,1)S(1)}, bf16[8,6,4608]{2,0,1:T(8,128)(2,1)S(1)}, u32[]{:S(2)}, u32[]{:S(2)}) %collective-permute-start.59) | collective-permute-done | bytes 442400 | tf_op jit(solution)/shard_map/ppermute | solution.py:569
  574.5 4.5 collective-permute-done.58.refs_9_
  580.6 3.4 round.17
  584.0 2.4 copy.54
  593.6 13.8 %collective-permute-done.63 = bf16[16,6,4608]{2,0,1:T(8,128)(2,1)} collective-permute-done((bf16[16,6,4608]{2,0,1:T(8,128)(2,1)}, bf16[16,6,4608]{2,0,1:T(8,128)(2,1)}, u32[]{:S(2)}, u32[]{:S(2)}) %collective-permute-start.63) | collective-permute-done | bytes 884768 | tf_op jit(solution)/shard_map/ppermute | solution.py:569
  608.8 2.7 copy.55.refs_7_
  615.9 3.7 round.18
  619.6 3.4 fusion.23
  644.3 4.6 collective-permute-done.64.refs_1_
  660.0 2.7 collective-permute-done.65.refs_1_
  662.8 3.0 collective-permute-done.66.refs_2_
  666.5 6.0 finish.1
  (519 shorter events, 166.2 us)
Async XLA Ops:
  7.2 175.6 %all-gather.2.cloned.1.call-start = ((), (), s32[]{:S(2)}) async-start(), calls=%async_computation | async-start | bytes 24330240 | tf_op jit(solution)/shard_map/all_gather | solution.py:1082
  21.6 71.0 %collective-permute-start.6 = (bf16[4,1,96,768]{3,2,1,0:T(8,128)(2,1)S(1)}, bf16[4,1,96,768]{3,2,1,0:T(8,128)(2,1)S(1)}, u32[]{:S(2)}, u32[]{:S(2)}) collective-permute-start(bf16[4,1,96,768]{3,2,1,0:T(8,128)(2,1)S(1)} %get-tuple-element.324.own_ref), channel_id=1, source_target_pairs={{0,1},{1,0},{2,3},{3,2},{4,5},{5,4},{6,7},{7,6},{8,9},{9,8},{10,11... | collective-permute-start | bytes 1769480 | tf_op jit(solution)/shard_map/ppermute | solution.py:569
  22.4 14.5 %collective-permute-start.7 = (bf16[1,1,96,768]{3,2,0,1:T(8,128)(2,1)}, bf16[1,1,96,768]{3,2,0,1:T(8,128)(2,1)}, u32[]{:S(2)}, u32[]{:S(2)}) collective-permute-start(bf16[1,1,96,768]{3,2,0,1:T(8,128)(2,1)} %dynamic-slice_bitcast_fusion), channel_id=1, source_target_pairs={{0,4},{1,5},{2,6},{3,7},{4,0},{5,1},{6,2},{7,3},{8,12},{9,13},{10,... | collective-permute-start | bytes 442376 | tf_op jit(solution)/shard_map/ppermute | solution.py:569
  34.3 26.3 %collective-permute-start.3 = (f32[4,3,2,4608]{3,2,1,0:T(2,128)S(1)}, f32[4,3,2,4608]{3,2,1,0:T(2,128)S(1)}, u32[]{:S(2)}, u32[]{:S(2)}) collective-permute-start(f32[4,3,2,4608]{3,2,1,0:T(2,128)S(1)} %bitcast.182), channel_id=1, source_target_pairs={{0,1},{1,0},{2,3},{3,2},{4,5},{5,4},{6,7},{7,6},{8,9},{9,8},{10,11... | collective-permute-start | bytes 1327112 | tf_op jit(solution)/shard_map/ppermute | solution.py:569
  38.0 17.0 %collective-permute-start.8 = (bf16[2,1,96,768]{3,2,0,1:T(8,128)(2,1)S(1)}, bf16[2,1,96,768]{3,2,0,1:T(8,128)(2,1)S(1)}, u32[]{:S(2)}, u32[]{:S(2)}) collective-permute-start(bf16[2,1,96,768]{3,2,0,1:T(8,128)(2,1)S(1)} %pad_maximum_fusion.4), channel_id=1, source_target_pairs={{0,2},{1,3},{2,0},{3,1},{4,6},{5,7},{6,4},{7,5},{8,10},{9,11},{10,... | collective-permute-start | bytes 884744 | tf_op jit(solution)/shard_map/ppermute | solution.py:569
  60.9 18.9 %collective-permute-start.4 = (f32[2,3,2,4608]{3,2,1,0:T(2,128)S(1)}, f32[2,3,2,4608]{3,2,1,0:T(2,128)S(1)}, u32[]{:S(2)}, u32[]{:S(2)}) collective-permute-start(f32[2,3,2,4608]{3,2,1,0:T(2,128)S(1)} %slice.344), channel_id=1, source_target_pairs={{0,2},{1,3},{2,0},{3,1},{4,6},{5,7},{6,4},{7,5},{8,10},{9,11},{10,... | collective-permute-start | bytes 663560 | tf_op jit(solution)/shard_map/ppermute | solution.py:569
  66.6 22.2 %collective-permute-start.10 = (bf16[2,3,1,48,768]{4,3,1,2,0:T(8,128)(2,1)S(1)}, bf16[2,3,1,48,768]{4,3,1,2,0:T(8,128)(2,1)S(1)}, u32[]{:S(2)}, u32[]{:S(2)}) collective-permute-start(bf16[2,3,1,48,768]{4,3,1,2,0:T(8,128)(2,1)S(1)} %get-tuple-element.328), channel_id=1, source_target_pairs={{0,16},{8,24},{16,0},{24,8},{1,17},{9,25},{17,1},{25,9},{2,18},{10... | collective-permute-start | bytes 1327112 | tf_op jit(solution)/shard_map/ppermute | solution.py:569
  69.2 21.6 %collective-permute-start.12 = (bf16[2,3,1,48,768]{4,3,2,1,0:T(8,128)(2,1)S(1)}, bf16[2,3,1,48,768]{4,3,2,1,0:T(8,128)(2,1)S(1)}, u32[]{:S(2)}, u32[]{:S(2)}) collective-permute-start(bf16[2,3,1,48,768]{4,3,2,1,0:T(8,128)(2,1)S(1)} %pad_maximum_fusion.3.refs_2_), channel_id=1, source_target_pairs={{0,8},{8,0},{16,24},{24,16},{1,9},{9,1},{17,25},{25,17},{2,10},{10... | collective-permute-start | bytes 1327112 | tf_op jit(solution)/shard_map/ppermute | solution.py:569
  294.9 54.4 %collective-permute-start.20 = (bf16[8,96,768]{2,1,0:T(8,128)(2,1)}, bf16[8,96,768]{2,1,0:T(8,128)(2,1)S(1)}, u32[]{:S(2)}, u32[]{:S(2)}) collective-permute-start(bf16[8,96,768]{2,1,0:T(8,128)(2,1)} %get-tuple-element.173.refs_7_), channel_id=1, source_target_pairs={{0,8},{8,0},{16,24},{24,16},{1,9},{9,1},{17,25},{25,17},{2,10},{10... | collective-permute-start | bytes 3538952 | tf_op jit(solution)/shard_map/ppermute | solution.py:569
  296.3 53.0 %collective-permute-start.21 = (bf16[8,96,768]{2,1,0:T(8,128)(2,1)}, bf16[8,96,768]{2,1,0:T(8,128)(2,1)S(1)}, u32[]{:S(2)}, u32[]{:S(2)}) collective-permute-start(bf16[8,96,768]{2,1,0:T(8,128)(2,1)} %get-tuple-element.174.refs_8_), channel_id=1, source_target_pairs={{0,16},{8,24},{16,0},{24,8},{1,17},{9,25},{17,1},{25,9},{2,18},{10... | collective-permute-start | bytes 3538952 | tf_op jit(solution)/shard_map/ppermute | solution.py:569
  330.3 19.0 %collective-permute-start.22 = (bf16[2,24,768]{2,1,0:T(8,128)(2,1)S(1)}, bf16[2,24,768]{2,1,0:T(8,128)(2,1)S(1)}, u32[]{:S(2)}, u32[]{:S(2)}) collective-permute-start(bf16[2,24,768]{2,1,0:T(8,128)(2,1)S(1)} %copy-done.36), channel_id=1, source_target_pairs={{0,8},{8,0},{16,24},{24,16},{1,9},{9,1},{17,25},{25,17},{2,10},{10... | collective-permute-start | bytes 221192 | tf_op jit(solution)/shard_map/ppermute | solution.py:569
  356.3 31.7 %collective-permute-start.25 = (bf16[16,96,768]{2,1,0:T(8,128)(2,1)}, bf16[16,96,768]{2,1,0:T(8,128)(2,1)S(1)}, u32[]{:S(2)}, u32[]{:S(2)}) collective-permute-start(bf16[16,96,768]{2,1,0:T(8,128)(2,1)} %get-tuple-element.185.refs_10_), channel_id=1, source_target_pairs={{0,1},{1,0},{2,3},{3,2},{4,5},{5,4},{6,7},{7,6},{8,9},{9,8},{10,11... | collective-permute-start | bytes 7077896 | tf_op jit(solution)/shard_map/ppermute | solution.py:569
  356.3 31.7 %collective-permute-start.23 = (bf16[4,96,768]{2,1,0:T(8,128)(2,1)}, bf16[4,96,768]{2,1,0:T(8,128)(2,1)S(1)}, u32[]{:S(2)}, u32[]{:S(2)}) collective-permute-start(bf16[4,96,768]{2,1,0:T(8,128)(2,1)} %get-tuple-element.183.refs_8_), channel_id=1, source_target_pairs={{0,16},{8,24},{16,0},{24,8},{1,17},{9,25},{17,1},{25,9},{2,18},{10... | collective-permute-start | bytes 1769480 | tf_op jit(solution)/shard_map/ppermute | solution.py:569
  357.0 31.0 %collective-permute-start.24 = (bf16[4,96,768]{2,1,0:T(8,128)(2,1)}, bf16[4,96,768]{2,1,0:T(8,128)(2,1)S(1)}, u32[]{:S(2)}, u32[]{:S(2)}) collective-permute-start(bf16[4,96,768]{2,1,0:T(8,128)(2,1)} %get-tuple-element.184.refs_9_), channel_id=1, source_target_pairs={{0,8},{8,0},{16,24},{24,16},{1,9},{9,1},{17,25},{25,17},{2,10},{10... | collective-permute-start | bytes 1769480 | tf_op jit(solution)/shard_map/ppermute | solution.py:569
  397.7 41.6 %collective-permute-start.30 = (bf16[16,96,768]{2,1,0:T(8,128)(2,1)}, bf16[16,96,768]{2,1,0:T(8,128)(2,1)S(1)}, u32[]{:S(2)}, u32[]{:S(2)}) collective-permute-start(bf16[16,96,768]{2,1,0:T(8,128)(2,1)} %get-tuple-element.197.refs_11_), channel_id=1, source_target_pairs={{0,1},{1,0},{2,3},{3,2},{4,5},{5,4},{6,7},{7,6},{8,9},{9,8},{10,11... | collective-permute-start | bytes 7077896 | tf_op jit(solution)/shard_map/ppermute | solution.py:569
  397.8 41.6 %collective-permute-start.31 = (bf16[16,96,768]{2,1,0:T(8,128)(2,1)}, bf16[16,96,768]{2,1,0:T(8,128)(2,1)}, u32[]{:S(2)}, u32[]{:S(2)}) collective-permute-start(bf16[16,96,768]{2,1,0:T(8,128)(2,1)} %get-tuple-element.198.refs_12_), channel_id=1, source_target_pairs={{0,1},{1,0},{2,3},{3,2},{4,5},{5,4},{6,7},{7,6},{8,9},{9,8},{10,11... | collective-permute-start | bytes 7077896 | tf_op jit(solution)/shard_map/ppermute | solution.py:569
  400.9 29.5 %collective-permute-start.26 = (bf16[2,96,768]{2,1,0:T(8,128)(2,1)}, bf16[2,96,768]{2,1,0:T(8,128)(2,1)}, u32[]{:S(2)}, u32[]{:S(2)}) collective-permute-start(bf16[2,96,768]{2,1,0:T(8,128)(2,1)} %get-tuple-element.193.refs_7_), channel_id=1, source_target_pairs={{0,2},{1,3},{2,0},{3,1},{4,6},{5,7},{6,4},{7,5},{8,10},{9,11},{10,... | collective-permute-start | bytes 884744 | tf_op jit(solution)/shard_map/ppermute | solution.py:569
  400.9 38.4 %collective-permute-start.28 = (bf16[4,96,768]{2,1,0:T(8,128)(2,1)}, bf16[4,96,768]{2,1,0:T(8,128)(2,1)S(1)}, u32[]{:S(2)}, u32[]{:S(2)}) collective-permute-start(bf16[4,96,768]{2,1,0:T(8,128)(2,1)} %get-tuple-element.195.refs_9_), channel_id=1, source_target_pairs={{0,8},{8,0},{16,24},{24,16},{1,9},{9,1},{17,25},{25,17},{2,10},{10... | collective-permute-start | bytes 1769480 | tf_op jit(solution)/shard_map/ppermute | solution.py:569
  401.7 37.6 %collective-permute-start.29 = (bf16[4,96,768]{2,1,0:T(8,128)(2,1)}, bf16[4,96,768]{2,1,0:T(8,128)(2,1)S(1)}, u32[]{:S(2)}, u32[]{:S(2)}) collective-permute-start(bf16[4,96,768]{2,1,0:T(8,128)(2,1)} %get-tuple-element.196.refs_10_), channel_id=1, source_target_pairs={{0,16},{8,24},{16,0},{24,8},{1,17},{9,25},{17,1},{25,9},{2,18},{10... | collective-permute-start | bytes 1769480 | tf_op jit(solution)/shard_map/ppermute | solution.py:569
  448.8 45.5 %collective-permute-start.36 = (bf16[8,96,768]{2,1,0:T(8,128)(2,1)}, bf16[8,96,768]{2,1,0:T(8,128)(2,1)S(1)}, u32[]{:S(2)}, u32[]{:S(2)}) collective-permute-start(bf16[8,96,768]{2,1,0:T(8,128)(2,1)} %get-tuple-element.217.refs_12_), channel_id=1, source_target_pairs={{0,8},{8,0},{16,24},{24,16},{1,9},{9,1},{17,25},{25,17},{2,10},{10... | collective-permute-start | bytes 3538952 | tf_op jit(solution)/shard_map/ppermute | solution.py:569
  449.4 45.0 %collective-permute-start.37 = (bf16[8,96,768]{2,1,0:T(8,128)(2,1)}, bf16[8,96,768]{2,1,0:T(8,128)(2,1)S(1)}, u32[]{:S(2)}, u32[]{:S(2)}) collective-permute-start(bf16[8,96,768]{2,1,0:T(8,128)(2,1)} %get-tuple-element.218.refs_13_), channel_id=1, source_target_pairs={{0,16},{8,24},{16,0},{24,8},{1,17},{9,25},{17,1},{25,9},{2,18},{10... | collective-permute-start | bytes 3538952 | tf_op jit(solution)/shard_map/ppermute | solution.py:569
  469.4 14.7 %collective-permute-start.39 = (f32[1,6,4608]{2,1,0:T(8,128)S(1)}, f32[1,6,4608]{2,1,0:T(8,128)S(1)}, u32[]{:S(2)}, u32[]{:S(2)}) collective-permute-start(f32[1,6,4608]{2,1,0:T(8,128)S(1)} %maximum_bitcast_fusion.5.refs_15_), channel_id=1, source_target_pairs={{0,4},{1,5},{2,6},{3,7},{4,0},{5,1},{6,2},{7,3},{8,12},{9,13},{10,... | collective-permute-start | bytes 331784 | tf_op jit(solution)/shard_map/ppermute | solution.py:569
  472.4 13.7 %collective-permute-start.32 = (bf16[1,96,768]{2,1,0:T(8,128)(2,1)S(1)}, bf16[1,96,768]{2,1,0:T(8,128)(2,1)S(1)}, u32[]{:S(2)}, u32[]{:S(2)}) collective-permute-start(bf16[1,96,768]{2,1,0:T(8,128)(2,1)S(1)} %copy-done.111), channel_id=1, source_target_pairs={{0,4},{1,5},{2,6},{3,7},{4,0},{5,1},{6,2},{7,3},{8,12},{9,13},{10,... | collective-permute-start | bytes 442376 | tf_op jit(solution)/shard_map/ppermute | solution.py:569
  502.4 20.5 %collective-permute-start.44 = (bf16[16,96,768]{2,1,0:T(8,128)(2,1)}, bf16[16,96,768]{2,1,0:T(8,128)(2,1)S(1)}, u32[]{:S(2)}, u32[]{:S(2)}) collective-permute-start(bf16[16,96,768]{2,1,0:T(8,128)(2,1)} %get-tuple-element.242), channel_id=1, source_target_pairs={{0,1},{1,0},{2,3},{3,2},{4,5},{5,4},{6,7},{7,6},{8,9},{9,8},{10,11... | collective-permute-start | bytes 7077896 | tf_op jit(solution)/shard_map/ppermute | solution.py:569
  502.5 20.4 %collective-permute-start.42 = (bf16[4,96,768]{2,1,0:T(8,128)(2,1)}, bf16[4,96,768]{2,1,0:T(8,128)(2,1)S(1)}, u32[]{:S(2)}, u32[]{:S(2)}) collective-permute-start(bf16[4,96,768]{2,1,0:T(8,128)(2,1)} %get-tuple-element.238), channel_id=1, source_target_pairs={{0,16},{8,24},{16,0},{24,8},{1,17},{9,25},{17,1},{25,9},{2,18},{10... | collective-permute-start | bytes 1769480 | tf_op jit(solution)/shard_map/ppermute | solution.py:569
  503.2 19.7 %collective-permute-start.43 = (bf16[4,96,768]{2,1,0:T(8,128)(2,1)}, bf16[4,96,768]{2,1,0:T(8,128)(2,1)S(1)}, u32[]{:S(2)}, u32[]{:S(2)}) collective-permute-start(bf16[4,96,768]{2,1,0:T(8,128)(2,1)} %get-tuple-element.240), channel_id=1, source_target_pairs={{0,8},{8,0},{16,24},{24,16},{1,9},{9,1},{17,25},{25,17},{2,10},{10... | collective-permute-start | bytes 1769480 | tf_op jit(solution)/shard_map/ppermute | solution.py:569
  531.8 21.2 %collective-permute-start.50 = (bf16[4,96,768]{2,1,0:T(8,128)(2,1)}, bf16[4,96,768]{2,1,0:T(8,128)(2,1)S(1)}, u32[]{:S(2)}, u32[]{:S(2)}) collective-permute-start(bf16[4,96,768]{2,1,0:T(8,128)(2,1)} %get-tuple-element.252), channel_id=1, source_target_pairs={{0,8},{8,0},{16,24},{24,16},{1,9},{9,1},{17,25},{25,17},{2,10},{10... | collective-permute-start | bytes 1769480 | tf_op jit(solution)/shard_map/ppermute | solution.py:569
  532.5 20.5 %collective-permute-start.51 = (bf16[4,96,768]{2,1,0:T(8,128)(2,1)}, bf16[4,96,768]{2,1,0:T(8,128)(2,1)S(1)}, u32[]{:S(2)}, u32[]{:S(2)}) collective-permute-start(bf16[4,96,768]{2,1,0:T(8,128)(2,1)} %get-tuple-element.254), channel_id=1, source_target_pairs={{0,16},{8,24},{16,0},{24,8},{1,17},{9,25},{17,1},{25,9},{2,18},{10... | collective-permute-start | bytes 1769480 | tf_op jit(solution)/shard_map/ppermute | solution.py:569
  533.9 17.3 %collective-permute-start.48 = (bf16[2,96,768]{2,1,0:T(8,128)(2,1)}, bf16[2,96,768]{2,1,0:T(8,128)(2,1)S(1)}, u32[]{:S(2)}, u32[]{:S(2)}) collective-permute-start(bf16[2,96,768]{2,1,0:T(8,128)(2,1)} %get-tuple-element.248), channel_id=1, source_target_pairs={{0,2},{1,3},{2,0},{3,1},{4,6},{5,7},{6,4},{7,5},{8,10},{9,11},{10,... | collective-permute-start | bytes 884744 | tf_op jit(solution)/shard_map/ppermute | solution.py:569
  535.3 17.7 %collective-permute-start.49 = (bf16[2,96,768]{2,1,0:T(8,128)(2,1)}, bf16[2,96,768]{2,1,0:T(8,128)(2,1)S(1)}, u32[]{:S(2)}, u32[]{:S(2)}) collective-permute-start(bf16[2,96,768]{2,1,0:T(8,128)(2,1)} %get-tuple-element.250), channel_id=1, source_target_pairs={{0,2},{1,3},{2,0},{3,1},{4,6},{5,7},{6,4},{7,5},{8,10},{9,11},{10,... | collective-permute-start | bytes 884744 | tf_op jit(solution)/shard_map/ppermute | solution.py:569
  535.9 15.3 %collective-permute-start.47 = (bf16[1,96,768]{2,1,0:T(8,128)(2,1)}, bf16[1,96,768]{2,1,0:T(8,128)(2,1)S(1)}, u32[]{:S(2)}, u32[]{:S(2)}) collective-permute-start(bf16[1,96,768]{2,1,0:T(8,128)(2,1)} %get-tuple-element.246), channel_id=1, source_target_pairs={{0,4},{1,5},{2,6},{3,7},{4,0},{5,1},{6,2},{7,3},{8,12},{9,13},{10,... | collective-permute-start | bytes 442376 | tf_op jit(solution)/shard_map/ppermute | solution.py:569
  560.5 19.2 %collective-permute-start.56 = (bf16[2,96,768]{2,1,0:T(8,128)(2,1)}, bf16[2,96,768]{2,1,0:T(8,128)(2,1)S(1)}, u32[]{:S(2)}, u32[]{:S(2)}) collective-permute-start(bf16[2,96,768]{2,1,0:T(8,128)(2,1)} %get-tuple-element.262), channel_id=1, source_target_pairs={{0,16},{8,24},{16,0},{24,8},{1,17},{9,25},{17,1},{25,9},{2,18},{10... | collective-permute-start | bytes 884744 | tf_op jit(solution)/shard_map/ppermute | solution.py:569
  561.9 17.9 %collective-permute-start.57 = (bf16[2,96,768]{2,1,0:T(8,128)(2,1)}, bf16[2,96,768]{2,1,0:T(8,128)(2,1)S(1)}, u32[]{:S(2)}, u32[]{:S(2)}) collective-permute-start(bf16[2,96,768]{2,1,0:T(8,128)(2,1)} %get-tuple-element.264), channel_id=1, source_target_pairs={{0,8},{8,0},{16,24},{24,16},{1,9},{9,1},{17,25},{25,17},{2,10},{10... | collective-permute-start | bytes 884744 | tf_op jit(solution)/shard_map/ppermute | solution.py:569
  562.6 17.2 %collective-permute-start.54 = (bf16[1,96,768]{2,1,0:T(8,128)(2,1)}, bf16[1,96,768]{2,1,0:T(8,128)(2,1)S(1)}, u32[]{:S(2)}, u32[]{:S(2)}) collective-permute-start(bf16[1,96,768]{2,1,0:T(8,128)(2,1)} %get-tuple-element.258), channel_id=1, source_target_pairs={{0,4},{1,5},{2,6},{3,7},{4,0},{5,1},{6,2},{7,3},{8,12},{9,13},{10,... | collective-permute-start | bytes 442376 | tf_op jit(solution)/shard_map/ppermute | solution.py:569
  564.2 15.5 %collective-permute-start.55 = (bf16[1,96,768]{2,1,0:T(8,128)(2,1)}, bf16[1,96,768]{2,1,0:T(8,128)(2,1)S(1)}, u32[]{:S(2)}, u32[]{:S(2)}) collective-permute-start(bf16[1,96,768]{2,1,0:T(8,128)(2,1)} %get-tuple-element.260), channel_id=1, source_target_pairs={{0,4},{1,5},{2,6},{3,7},{4,0},{5,1},{6,2},{7,3},{8,12},{9,13},{10,... | collective-permute-start | bytes 442376 | tf_op jit(solution)/shard_map/ppermute | solution.py:569
  579.0 49.0 %collective-permute-start.74 = (bf16[2,96,768]{2,1,0:T(8,128)(2,1)}, bf16[2,96,768]{2,1,0:T(8,128)(2,1)}, u32[]{:S(2)}, u32[]{:S(2)}) collective-permute-start(bf16[2,96,768]{2,1,0:T(8,128)(2,1)} %get-tuple-element.277.refs_12_), channel_id=1, source_target_pairs={{0,8},{8,0},{16,24},{24,16},{1,9},{9,1},{17,25},{25,17},{2,10},{10... | collective-permute-start | bytes 884744 | tf_op jit(solution)/shard_map/ppermute | solution.py:569
  586.5 21.0 %collective-permute-start.63 = (bf16[16,6,4608]{2,0,1:T(8,128)(2,1)}, bf16[16,6,4608]{2,0,1:T(8,128)(2,1)}, u32[]{:S(2)}, u32[]{:S(2)}) collective-permute-start(bf16[16,6,4608]{2,0,1:T(8,128)(2,1)} %copy.54), channel_id=1, source_target_pairs={{0,8},{8,0},{16,24},{24,16},{1,9},{9,1},{17,25},{25,17},{2,10},{10... | collective-permute-start | bytes 2654216 | tf_op jit(solution)/shard_map/ppermute | solution.py:569
  590.2 22.8 %collective-permute-start.60 = (bf16[1,96,768]{2,1,0:T(8,128)(2,1)}, bf16[1,96,768]{2,1,0:T(8,128)(2,1)S(1)}, u32[]{:S(2)}, u32[]{:S(2)}) collective-permute-start(bf16[1,96,768]{2,1,0:T(8,128)(2,1)} %get-tuple-element.268), channel_id=1, source_target_pairs={{0,2},{1,3},{2,0},{3,1},{4,6},{5,7},{6,4},{7,5},{8,10},{9,11},{10,... | collective-permute-start | bytes 442376 | tf_op jit(solution)/shard_map/ppermute | solution.py:569
  591.9 22.6 %collective-permute-start.61 = (bf16[1,96,768]{2,1,0:T(8,128)(2,1)}, bf16[1,96,768]{2,1,0:T(8,128)(2,1)S(1)}, u32[]{:S(2)}, u32[]{:S(2)}) collective-permute-start(bf16[1,96,768]{2,1,0:T(8,128)(2,1)} %get-tuple-element.270), channel_id=1, source_target_pairs={{0,2},{1,3},{2,0},{3,1},{4,6},{5,7},{6,4},{7,5},{8,10},{9,11},{10,... | collective-permute-start | bytes 442376 | tf_op jit(solution)/shard_map/ppermute | solution.py:569
  592.3 19.3 %collective-permute-start.62 = (f32[2,8,768]{2,1,0:T(8,128)}, f32[2,8,768]{2,1,0:T(8,128)S(1)}, u32[]{:S(2)}, u32[]{:S(2)}) collective-permute-start(f32[2,8,768]{2,1,0:T(8,128)} %get-tuple-element.271.refs_4_), channel_id=1, source_target_pairs={{0,8},{8,0},{16,24},{24,16},{1,9},{9,1},{17,25},{25,17},{2,10},{10... | collective-permute-start | bytes 147464 | tf_op jit(solution)/shard_map/ppermute | solution.py:569
  607.4 22.4 %collective-permute-start.75 = (bf16[2,96,768]{2,1,0:T(8,128)(2,1)}, bf16[2,96,768]{2,1,0:T(8,128)(2,1)S(1)}, u32[]{:S(2)}, u32[]{:S(2)}) collective-permute-start(bf16[2,96,768]{2,1,0:T(8,128)(2,1)} %get-tuple-element.277.refs_12_), channel_id=1, source_target_pairs={{0,16},{8,24},{16,0},{24,8},{1,17},{9,25},{17,1},{25,9},{2,18},{10... | collective-permute-start | bytes 884744 | tf_op jit(solution)/shard_map/ppermute | solution.py:569
  611.5 18.3 %collective-permute-start.76 = (bf16[2,96,768]{2,1,0:T(8,128)(2,1)}, bf16[2,96,768]{2,1,0:T(8,128)(2,1)}, u32[]{:S(2)}, u32[]{:S(2)}) collective-permute-start(bf16[2,96,768]{2,1,0:T(8,128)(2,1)} %get-tuple-element.277.refs_12_), channel_id=1, source_target_pairs={{0,24},{8,16},{16,8},{24,0},{1,25},{9,17},{17,9},{25,1},{2,26},{10... | collective-permute-start | bytes 884744 | tf_op jit(solution)/shard_map/ppermute | solution.py:569
  612.9 17.4 %collective-permute-start.77 = (f32[3,96]{1,0:T(4,128)}, f32[3,96]{1,0:T(4,128)S(1)}, u32[]{:S(2)}, u32[]{:S(2)}) collective-permute-start(f32[3,96]{1,0:T(4,128)} %get-tuple-element.349), channel_id=1, source_target_pairs={{0,4},{1,5},{2,6},{3,7},{4,0},{5,1},{6,2},{7,3},{8,12},{9,13},{10,... | collective-permute-start | bytes 3464 | tf_op jit(solution)/shard_map/ppermute | solution.py:569
  614.6 17.7 %collective-permute-start.78 = (f32[3,96]{1,0:T(4,128)}, f32[3,96]{1,0:T(4,128)S(1)}, u32[]{:S(2)}, u32[]{:S(2)}) collective-permute-start(f32[3,96]{1,0:T(4,128)} %get-tuple-element.348), channel_id=1, source_target_pairs={{0,2},{1,3},{2,0},{3,1},{4,6},{5,7},{6,4},{7,5},{8,10},{9,11},{10,... | collective-permute-start | bytes 3464 | tf_op jit(solution)/shard_map/ppermute | solution.py:569
  636.6 19.3 %collective-permute-start.72 = (bf16[1,96,768]{2,1,0:T(8,128)(2,1)S(1)}, bf16[1,96,768]{2,1,0:T(8,128)(2,1)}, u32[]{:S(2)}, u32[]{:S(2)}) collective-permute-start(bf16[1,96,768]{2,1,0:T(8,128)(2,1)S(1)} %copy-done.66), channel_id=1, source_target_pairs={{0,16},{8,24},{16,0},{24,8},{1,17},{9,25},{17,1},{25,9},{2,18},{10... | collective-permute-start | bytes 442376 | tf_op jit(solution)/shard_map/ppermute | solution.py:569
  638.0 19.3 %collective-permute-start.73 = (bf16[1,96,768]{2,1,0:T(8,128)(2,1)S(1)}, bf16[1,96,768]{2,1,0:T(8,128)(2,1)}, u32[]{:S(2)}, u32[]{:S(2)}) collective-permute-start(bf16[1,96,768]{2,1,0:T(8,128)(2,1)S(1)} %copy-done.66), channel_id=1, source_target_pairs={{0,24},{8,16},{16,8},{24,0},{1,25},{9,17},{17,9},{25,1},{2,26},{10... | collective-permute-start | bytes 442376 | tf_op jit(solution)/shard_map/ppermute | solution.py:569
  639.9 18.0 %collective-permute-start.68 = (bf16[2,96,768]{2,1,0:T(8,128)(2,1)S(1)}, bf16[2,96,768]{2,1,0:T(8,128)(2,1)S(1)}, u32[]{:S(2)}, u32[]{:S(2)}) collective-permute-start(bf16[2,96,768]{2,1,0:T(8,128)(2,1)S(1)} %copy-done.45), channel_id=1, source_target_pairs={{0,8},{8,0},{16,24},{24,16},{1,9},{9,1},{17,25},{25,17},{2,10},{10... | collective-permute-start | bytes 884744 | tf_op jit(solution)/shard_map/ppermute | solution.py:569
  642.9 17.1 %collective-permute-start.69 = (bf16[2,96,768]{2,1,0:T(8,128)(2,1)S(1)}, bf16[2,96,768]{2,1,0:T(8,128)(2,1)S(1)}, u32[]{:S(2)}, u32[]{:S(2)}) collective-permute-start(bf16[2,96,768]{2,1,0:T(8,128)(2,1)S(1)} %copy-done.45), channel_id=1, source_target_pairs={{0,16},{8,24},{16,0},{24,8},{1,17},{9,25},{17,1},{25,9},{2,18},{10... | collective-permute-start | bytes 884744 | tf_op jit(solution)/shard_map/ppermute | solution.py:569
  (152 other events, 1139.3 us)
Sparse Core Ops, SparseCore 0:
  17.3 165.3 all-gather.1

commit v4 on v3

--- a/solution.py
+++ b/solution.py
@@ -1159,8 +1159,8 @@
 
     packs = [pack(layer) for layer in range(LAYERS)]
     if fused:
-        a0 = Steps(gather_steps(net, here, packs[0][0]))
-        later = gather_whole(net, here, jnp.concatenate(packs[1] + packs[0][1:], axis=1))
+        a0, a1 = [Steps(gather_steps(net, here, kinds[0])) for kinds in packs]
+        later = gather_whole(net, here, jnp.concatenate(packs[0][1:] + packs[1][1:], axis=1))
     else:
         wholes = [
             plain_slabs(net, gather_whole(net, here, jnp.concatenate(kinds, axis=1)), 2)
@@ -1210,10 +1210,10 @@
         return (a0.end(), 0), []
 
     if fused:
-        attn_calls = (attn_first, lambda: ((later, 0), []))
+        attn_calls = (attn_first, lambda: ((a1.end(), 0), []))
         feed_calls = (
-            lambda: ((later, 3), (later, 4), []),
-            lambda: ((later, 1), (later, 2), []),
+            lambda: ((later, 0), (later, 1), [a1.end()]),
+            lambda: ((later, 2), (later, 3), []),
         )
         slot_calls = [lambda: []] * LAYERS
     else:
@@ -1305,7 +1305,7 @@
             middle_slot(layer),
             late_slot(layer),
         )
-        sends["at", layer] = send(at_grads, True)
+        sends["at", layer] = send(at_grads, layer == 1)
         modul_grads[layer] = grad_modul
     lines = [
         bias_line[0],

time: 693 us -> 668 us (0.964); the launches traced: 681 us -> 664 us
  waiting for transfers between devices: 185 us -> 163 us
  starting transfers between devices: 81.6 us -> 96.5 us
  local copies, waits for them, and re-layouts: 62.3 us -> 50.6 us
    all_gather x1, waiting for transfers between devices: 60.1 us -> 1.76 us  [gather_whole(): whole = lax.all_gather(flat, ('replica', 'shard'), axis=0, tiled=True)]
    ppermute x84 -> x95, waiting for transfers between devices: 125 us -> 161 us  [swap(): return lax.ppermute(values, axis, [(i, i ^ step) for i in range(count)])]
    ppermute x84 -> x95, starting transfers between devices: 81.5 us -> 96.5 us  [swap(): return lax.ppermute(values, axis, [(i, i ^ step) for i in range(count)])]
    pallas_call x12, Pallas kernels: 237 us -> 228 us  [call(): return lambda *arrays: run(here, *arrays, *after)]
    pallas_call x1 -> x2, Pallas kernels: 8.18 us -> 16.3 us  [place_weights(): pl.pallas_call(place_kernel, grid_spec=pltpu.PrefetchScalarGridSpec(num_s...]
    pallas_call x10 -> x9, Pallas kernels: 52.7 us -> 49.3 us  [run_round(): pl.pallas_call(functools.partial(round_kernel, jobs, line_jobs), in_specs...]
    unnamed x234 -> x191, local copies, waits for them, and re-layouts: 16 us -> 13.2 us
  transfers between devices with their start and end apart: 85 -> 96, of which waited for: 26 -> 32; matrix products, arithmetic and copies ran while one was open for 9% -> 10% of each run, Pallas kernels for 24% -> 21%
where the time goes in v4:
time: 668 us; the launch traced here: 664 us
  Pallas kernels  299 us (45%)
  waiting for transfers between devices  163 us (24%)
  starting transfers between devices  96.5 us (14%)
  local copies, waits for them, and re-layouts  50.6 us (8%)
  other arithmetic  32.7 us (5%)
  between operations  15.8 us (2%)
    pallas_call x12, Pallas kernels, call(): return lambda *arrays: run(here, *arrays, *after)  228 us
    ppermute x95, waiting for transfers between devices, swap(): return lax.ppermute(values, axis, [(i, i ^ step) for i in range(count)])  161 us
    ppermute x95, starting transfers between devices, swap(): return lax.ppermute(values, axis, [(i, i ^ step) for i in range(count)])  96.5 us
    pallas_call x9, Pallas kernels, run_round(): pl.pallas_call(functools.partial(round_kernel, jobs, line_jobs), in_specs...  49.3 us
    pallas_call x2, Pallas kernels, place_weights(): pl.pallas_call(place_kernel, grid_spec=pltpu.PrefetchScalarGridSpec(num_s...  16.3 us
  transfers between devices with their start and end apart: 96, of which 32 were waited for; matrix products, arithmetic and copies ran while one was open for 10% of the time, Pallas kernels for 21%

profile of v4, /device:TPU:0, one launch (start us, length us, event | category | flops | bytes accessed | tf_op | source)
XLA Modules:
  0.0 663.8 jit_solution(7562485690183368577)
XLA Ops:
  13.2 4.0 collective-permute-start
  25.6 3.7 collective-permute-done.1
  43.3 3.9 collective-permute-done.18
  47.3 6.2 collective-permute-done.8
  56.7 15.8 %collective-permute-done.19 = bf16[2,1,96,768]{3,2,0,1:T(8,128)(2,1)S(1)} collective-permute-done((bf16[2,1,96,768]{3,2,0,1:T(8,128)(2,1)S(1)}, bf16[2,1,96,768]{3,2,0,1:T(8,128)(2,1)S(1)}, u32[]{:S(2)}, u32[]{:S(2)}) %collective-permute-start.19) | collective-permute-done | bytes 294944 | tf_op jit(solution)/shard_map/ppermute | solution.py:569
  85.4 7.3 %collective-permute-start.23 = (bf16[2,3,1,48,768]{4,3,2,1,0:T(8,128)(2,1)S(1)}, bf16[2,3,1,48,768]{4,3,2,1,0:T(8,128)(2,1)}, u32[]{:S(2)}, u32[]{:S(2)}) collective-permute-start(bf16[2,3,1,48,768]{4,3,2,1,0:T(8,128)(2,1)S(1)} %pad_maximum_fusion.6.refs_2_), channel_id=1, source_target_pairs={{0,8},{8,0},{16,24},{24,16},{1,9},{9,1},{17,25},{25,17},{2,10},{10... | collective-permute-start | bytes 1327112 | tf_op jit(solution)/shard_map/ppermute | solution.py:569
  93.1 5.5 collective-permute-done.5
  107.2 13.4 %collective-permute-done.12.refs_3_ = bf16[2,3,1,48,768]{4,3,2,1,0:T(8,128)(2,1)S(1)} collective-permute-done((bf16[2,3,1,48,768]{4,3,2,1,0:T(8,128)(2,1)S(1)}, bf16[2,3,1,48,768]{4,3,2,1,0:T(8,128)(2,1)S(1)}, u32[]{:S(2)}, u32[]{:S(2)}) %collective-permute-start.12) | collective-permute-done | bytes 442400 | tf_op jit(solution)/shard_map/ppermute | solution.py:569
  125.1 8.2 %place_weights.3.refs_7_.refs_2_.refs_3_.refs_6_ = bf16[4,8,1,96,768]{4,3,2,1,0:T(8,128)(2,1)} custom-call(s32[2]{0:T(128)} %pad_add_fusion.here_ref, bf16[4,1,96,768]{3,2,1,0:T(8,128)(2,1)} %copy-done.1, bf16[4,1,96,768]{3,2,1,0:T(8,128)(2,1)} %collective-permute-done.17.own_far_ref, bf16[2,3,1,48,768]{4,3,2,1,0:T(8,128)(2,1)} %get-tuple-element.329.refs_0_, ...), custom_call_target="tpu_custom_call" | custom-call | tf_op jit(solution)/shard_map/place_weights/pallas_call | solution.py:1040
  134.2 8.1 %place_weights.2.refs_2_.refs_3_.refs_6_ = bf16[4,8,1,96,768]{4,3,2,1,0:T(8,128)(2,1)} custom-call(s32[2]{0:T(128)} %pad_add_fusion.here_ref, bf16[4,1,96,768]{3,2,1,0:T(8,128)(2,1)} %get-tuple-element.327.own_ref, bf16[4,1,96,768]{3,2,1,0:T(8,128)(2,1)} %bitcast.179, bf16[2,3,1,48,768]{4,3,2,1,0:T(8,128)(2,1)} %get-tuple-element.334.refs_0_, ...), custom_call_target="tpu_custom_call" | custom-call | tf_op jit(solution)/shard_map/place_weights/pallas_call | solution.py:1040
  142.3 8.4 %qkv_kernel.2 = (bf16[768,768]{1,0:T(8,128)(2,1)}, bf16[3,768,768]{2,1,0:T(8,128)(2,1)}) custom-call(s32[2]{0:T(128)} %pad_add_fusion.here_ref, f32[3,256,768]{2,1,0:T(8,128)} %refs_4_.1, f32[3,6,768]{2,1,0:T(8,128)} %reshape_squeeze.12.refs_1_.refs_2_.refs_5_.refs_6_, bf16[4,8,1,96,768]{4,3,2,1,0:T(8,128)(2,1)} %place_weights.2.refs_2_.refs_3_.refs_6_, ...), custom_call_target="tpu_custom_call" | custom-call | flops 2717908992 | bytes 10616832 | tf_op jit(solution)/shard_map/qkv_kernel/pallas_call | solution.py:380
  150.7 12.0 %mix_kernel.2 = (bf16[768,768]{1,0:T(8,128)(2,1)}, f32[768,768]{1,0:T(8,128)}, f32[768,768]{1,0:T(8,128)}, bf16[768,768]{1,0:T(8,128)(2,1)}) custom-call(s32[2]{0:T(128)} %pad_add_fusion.here_ref, bf16[3,768,768]{2,1,0:T(8,128)(2,1)} %get-tuple-element.150.refs_0_.refs_4_, f32[3,256,768]{2,1,0:T(8,128)} %refs_4_.1, ...), custom_call_target="tpu_custom_call" | custom-call | flops 4529848320 | bytes 14155776 | tf_op jit(solution)/shard_map/mix_kernel/pallas_call | solution.py:380
  164.5 22.0 %feed_kernel.2 = (bf16[4,768,768]{2,1,0:T(8,128)(2,1)}, bf16[4,768,768]{2,1,0:T(8,128)(2,1)}, f32[768,768]{1,0:T(8,128)}, f32[768,768]{1,0:T(8,128)}) custom-call(s32[2]{0:T(128)} %pad_add_fusion.here_ref, bf16[768,768]{1,0:T(8,128)(2,1)} %get-tuple-element.151.refs_0_.refs_3_, f32[768,768]{1,0:T(8,128)} %get-tuple-element.152.refs_1_, ...), custom_call_target="tpu_custom_call" | custom-call | flops 10871635968 | bytes 23592960 | tf_op jit(solution)/shard_map/feed_kernel/pallas_call | solution.py:380
  186.5 8.4 %qkv_kernel.3 = (bf16[768,768]{1,0:T(8,128)(2,1)}, bf16[3,768,768]{2,1,0:T(8,128)(2,1)}) custom-call(s32[2]{0:T(128)} %pad_add_fusion.here_ref, f32[3,256,768]{2,1,0:T(8,128)} %bitcast.191, f32[3,6,768]{2,1,0:T(8,128)} %reshape_squeeze.13.refs_1_.refs_2_.refs_5_.refs_6_, bf16[4,8,1,96,768]{4,3,2,1,0:T(8,128)(2,1)} %place_weights.3.refs_7_.refs_2_.refs_3_.refs_6_, ...), custom_call_target="tpu_custom_call" | custom-call | flops 2717908992 | bytes 10616832 | tf_op jit(solution)/shard_map/qkv_kernel/pallas_call | solution.py:380
  194.8 11.8 %mix_kernel.3 = (bf16[768,768]{1,0:T(8,128)(2,1)}, f32[768,768]{1,0:T(8,128)}, f32[768,768]{1,0:T(8,128)}, bf16[768,768]{1,0:T(8,128)(2,1)}) custom-call(s32[2]{0:T(128)} %pad_add_fusion.here_ref, bf16[3,768,768]{2,1,0:T(8,128)(2,1)} %get-tuple-element.154.refs_0_.refs_4_, f32[3,256,768]{2,1,0:T(8,128)} %bitcast.192, ...), custom_call_target="tpu_custom_call" | custom-call | flops 4529848320 | bytes 14155776 | tf_op jit(solution)/shard_map/mix_kernel/pallas_call | solution.py:380
  206.7 21.7 %feed_kernel.3 = (bf16[4,768,768]{2,1,0:T(8,128)(2,1)}, bf16[4,768,768]{2,1,0:T(8,128)(2,1)}, f32[768,768]{1,0:T(8,128)}, f32[768,768]{1,0:T(8,128)}) custom-call(s32[2]{0:T(128)} %pad_add_fusion.here_ref, bf16[768,768]{1,0:T(8,128)(2,1)} %get-tuple-element.155.refs_0_.refs_3_, f32[768,768]{1,0:T(8,128)} %get-tuple-element.156.refs_1_, ...), custom_call_target="tpu_custom_call" | custom-call | flops 10871635968 | bytes 23592960 | tf_op jit(solution)/shard_map/feed_kernel/pallas_call | solution.py:380
  228.3 4.4 broadcast_multiply_fusion
  232.7 29.4 %feed_back_kernel.2 = (bf16[4,4,96,768]{3,2,1,0:T(8,128)(2,1)}, bf16[4,4,96,768]{3,2,1,0:T(8,128)(2,1)}, bf16[4,4,96,768]{3,2,1,0:T(8,128)(2,1)}, bf16[4,4,96,76...) custom-call(s32[2]{0:T(128)} %pad_add_fusion.here_ref, ...), custom_call_target="tpu_custom_call" | custom-call | flops 14495514624 | bytes 29491200 | tf_op jit(solution)/shard_map/feed_back_kernel/pallas_call | solution.py:380
  263.6 3.2 collective-permute-done.30.refs_5_
  267.0 3.4 collective-permute-done.29.refs_3_
  270.4 6.3 round.9
  278.1 24.6 %mix_back_kernel.2 = (f32[768,768]{1,0:T(8,128)}, bf16[4,768,768]{2,1,0:T(8,128)(2,1)}, f32[3,3,768]{2,1,0:T(4,128)}, f32[4,768]{1,0:T(4,128)}) custom-call(s32[2]{0:T(128)} %pad_add_fusion.here_ref, f32[768,768]{1,0:T(8,128)} %get-tuple-element.165.refs_0_, f32[768,768]{1,0:T(8,128)} %get-tuple-element.156.refs_1_, f32[768,768]{1,0:T(8,128)} %bitcast.168, ...), custom_call_target="tpu_custom_call" | custom-call | flops 9059696640 | bytes 23592960 | tf_op jit(solution)/shard_map/mix_back_kernel/pallas_call | solution.py:380
  304.2 17.4 %qkv_back_kernel.2 = (bf16[4,4,96,768]{3,2,1,0:T(8,128)(2,1)}, bf16[4,4,96,768]{3,2,1,0:T(8,128)(2,1)}, f32[3,256,768]{2,1,0:T(8,128)}, f32[3,2,768]{2,1,0:T(2,128)}) custom-call(s32[2]{0:T(128)} %pad_add_fusion.here_ref, bf16[768,768]{1,0:T(8,128)(2,1)} %get-tuple-element.160.refs_0_, bf16[768,768]{1,0:T(8,128)(2,1)} %get-tuple-element.161.refs_1_, ...), custom_call_target="tpu_custom_call" | custom-call | flops 6341787648 | bytes 21233664 | tf_op jit(solution)/shard_map/qkv_back_kernel/pallas_call | solution.py:380
  323.2 5.5 round.10
  331.4 29.7 %feed_back_kernel.3 = (bf16[4,4,96,768]{3,2,1,0:T(8,128)(2,1)}, bf16[4,4,96,768]{3,2,1,0:T(8,128)(2,1)}, bf16[4,4,96,768]{3,2,1,0:T(8,128)(2,1)}, bf16[4,4,96,76...) custom-call(s32[2]{0:T(128)} %pad_add_fusion.here_ref, ...), custom_call_target="tpu_custom_call" | custom-call | flops 14495514624 | bytes 29491200 | tf_op jit(solution)/shard_map/feed_back_kernel/pallas_call | solution.py:380
  363.0 7.8 %round.11 = (bf16[2,96,768]{2,1,0:T(8,128)(2,1)}, bf16[2,96,768]{2,1,0:T(8,128)(2,1)}, bf16[2,96,768]{2,1,0:T(8,128)(2,1)}, bf16[2,96,768]{2,1,0:T(8,128)(2,1)},...) custom-call(bf16[4,96,768]{2,1,0:T(8,128)(2,1)} %get-tuple-element.1, ...), custom_call_target="tpu_custom_call" | custom-call | tf_op jit(solution)/shard_map/round/pallas_call | solution.py:920
  377.5 24.7 %mix_back_kernel.3 = (f32[768,768]{1,0:T(8,128)}, bf16[4,768,768]{2,1,0:T(8,128)(2,1)}, f32[3,3,768]{2,1,0:T(4,128)}, f32[4,768]{1,0:T(4,128)}) custom-call(s32[2]{0:T(128)} %pad_add_fusion.here_ref, f32[768,768]{1,0:T(8,128)} %get-tuple-element.186.refs_0_, f32[768,768]{1,0:T(8,128)} %get-tuple-element.152.refs_1_, f32[768,768]{1,0:T(8,128)} %bitcast.177, ...), custom_call_target="tpu_custom_call" | custom-call | flops 9059696640 | bytes 23592960 | tf_op jit(solution)/shard_map/mix_back_kernel/pallas_call | solution.py:380
  411.9 7.6 %round.12 = (bf16[1,96,768]{2,1,0:T(8,128)(2,1)}, bf16[1,96,768]{2,1,0:T(8,128)(2,1)}, bf16[1,96,768]{2,1,0:T(8,128)(2,1)}, bf16[1,96,768]{2,1,0:T(8,128)(2,1)},...) custom-call(bf16[2,96,768]{2,1,0:T(8,128)(2,1)} %get-tuple-element.2, ...), custom_call_target="tpu_custom_call" | custom-call | tf_op jit(solution)/shard_map/round/pallas_call | solution.py:920
  419.6 17.7 %qkv_back_kernel.3 = (bf16[4,4,96,768]{3,2,1,0:T(8,128)(2,1)}, bf16[4,4,96,768]{3,2,1,0:T(8,128)(2,1)}, f32[3,256,768]{2,1,0:T(8,128)}, f32[3,2,768]{2,1,0:T(2,128)}) custom-call(s32[2]{0:T(128)} %pad_add_fusion.here_ref, bf16[768,768]{1,0:T(8,128)(2,1)} %get-tuple-element.158.refs_0_, bf16[768,768]{1,0:T(8,128)(2,1)} %get-tuple-element.159.refs_1_, ...), custom_call_target="tpu_custom_call" | custom-call | flops 6341787648 | bytes 21233664 | tf_op jit(solution)/shard_map/qkv_back_kernel/pallas_call | solution.py:380
  443.6 9.1 %collective-permute-done.50.refs_15_ = f32[2,8,768]{2,1,0:T(8,128)} collective-permute-done((f32[2,8,768]{2,1,0:T(8,128)S(1)}, f32[2,8,768]{2,1,0:T(8,128)}, u32[]{:S(2)}, u32[]{:S(2)}) %collective-permute-start.50) | collective-permute-done | bytes 49184 | tf_op jit(solution)/shard_map/ppermute | solution.py:569
  455.7 7.9 %collective-permute-done.43.refs_1_ = bf16[1,96,768]{2,1,0:T(8,128)(2,1)S(1)} collective-permute-done((bf16[1,96,768]{2,1,0:T(8,128)(2,1)S(1)}, bf16[1,96,768]{2,1,0:T(8,128)(2,1)S(1)}, u32[]{:S(2)}, u32[]{:S(2)}) %collective-permute-start.43) | collective-permute-done | bytes 147488 | tf_op jit(solution)/shard_map/ppermute | solution.py:569
  468.3 4.7 collective-permute-done.45.refs_5_
  478.2 7.1 %round.13 = (bf16[2,96,768]{2,1,0:T(8,128)(2,1)}, bf16[1,96,768]{2,1,0:T(8,128)(2,1)}, bf16[1,96,768]{2,1,0:T(8,128)(2,1)}, bf16[1,96,768]{2,1,0:T(8,128)(2,1)},...) custom-call(bf16[1,96,768]{2,1,0:T(8,128)(2,1)} %get-tuple-element.2, ...), custom_call_target="tpu_custom_call" | custom-call | tf_op jit(solution)/shard_map/round/pallas_call | solution.py:920
  489.4 4.3 collective-permute-done.58.refs_13_
  493.7 6.2 collective-permute-done.52.refs_1_
  500.0 6.9 %collective-permute-done.53.refs_3_ = bf16[1,96,768]{2,1,0:T(8,128)(2,1)S(1)} collective-permute-done((bf16[1,96,768]{2,1,0:T(8,128)(2,1)}, bf16[1,96,768]{2,1,0:T(8,128)(2,1)S(1)}, u32[]{:S(2)}, u32[]{:S(2)}) %collective-permute-start.53) | collective-permute-done | bytes 147488 | tf_op jit(solution)/shard_map/ppermute | solution.py:569
  506.9 6.9 %collective-permute-done.59.refs_15_ = f32[2,6,4608]{2,1,0:T(8,128)S(1)} collective-permute-done((f32[2,6,4608]{2,1,0:T(8,128)}, f32[2,6,4608]{2,1,0:T(8,128)S(1)}, u32[]{:S(2)}, u32[]{:S(2)}) %collective-permute-start.59) | collective-permute-done | bytes 221216 | tf_op jit(solution)/shard_map/ppermute | solution.py:569
  515.3 4.6 round.14
  528.4 10.0 %collective-permute-done.60.refs_1_ = bf16[1,96,768]{2,1,0:T(8,128)(2,1)S(1)} collective-permute-done((bf16[1,96,768]{2,1,0:T(8,128)(2,1)}, bf16[1,96,768]{2,1,0:T(8,128)(2,1)S(1)}, u32[]{:S(2)}, u32[]{:S(2)}) %collective-permute-start.60) | collective-permute-done | bytes 147488 | tf_op jit(solution)/shard_map/ppermute | solution.py:569
  541.4 3.9 round.15
  552.2 5.7 collective-permute-done.72
  564.9 3.1 round.16
  577.1 13.2 %collective-permute-done.75 = bf16[16,6,4608]{2,0,1:T(8,128)(2,1)} collective-permute-done((bf16[16,6,4608]{2,0,1:T(8,128)(2,1)}, bf16[16,6,4608]{2,0,1:T(8,128)(2,1)}, u32[]{:S(2)}, u32[]{:S(2)}) %collective-permute-start.75) | collective-permute-done | bytes 884768 | tf_op jit(solution)/shard_map/ppermute | solution.py:569
  599.9 3.5 round.17
  603.4 3.4 fusion.26
  636.3 6.6 collective-permute-done.80.refs_6_
  643.6 5.0 collective-permute-done.77.refs_2_
  649.3 6.0 finish.1
  (505 shorter events, 188.0 us)
Async XLA Ops:
  7.2 157.3 %all-gather.2.cloned.1.call-start = ((), (), s32[]{:S(2)}) async-start(), calls=%async_computation | async-start | bytes 19464192 | tf_op jit(solution)/shard_map/all_gather | solution.py:1082
  18.8 21.9 %collective-permute-start.7 = (bf16[1,1,96,768]{3,2,0,1:T(8,128)(2,1)S(1)}, bf16[1,1,96,768]{3,2,0,1:T(8,128)(2,1)S(1)}, u32[]{:S(2)}, u32[]{:S(2)}) collective-permute-start(bf16[1,1,96,768]{3,2,0,1:T(8,128)(2,1)S(1)} %dynamic-slice_bitcast_fusion.1), channel_id=1, source_target_pairs={{0,4},{1,5},{2,6},{3,7},{4,0},{5,1},{6,2},{7,3},{8,12},{9,13},{10,... | collective-permute-start | bytes 442376 | tf_op jit(solution)/shard_map/ppermute | solution.py:569
  19.0 74.0 %collective-permute-start.17 = (bf16[4,1,96,768]{3,2,1,0:T(8,128)(2,1)S(1)}, bf16[4,1,96,768]{3,2,1,0:T(8,128)(2,1)}, u32[]{:S(2)}, u32[]{:S(2)}) collective-permute-start(bf16[4,1,96,768]{3,2,1,0:T(8,128)(2,1)S(1)} %get-tuple-element.316.own_ref), channel_id=1, source_target_pairs={{0,1},{1,0},{2,3},{3,2},{4,5},{5,4},{6,7},{7,6},{8,9},{9,8},{10,11... | collective-permute-start | bytes 1769480 | tf_op jit(solution)/shard_map/ppermute | solution.py:569
  19.1 28.1 %collective-permute-start.18 = (bf16[1,1,96,768]{3,2,0,1:T(8,128)(2,1)S(1)}, bf16[1,1,96,768]{3,2,0,1:T(8,128)(2,1)S(1)}, u32[]{:S(2)}, u32[]{:S(2)}) collective-permute-start(bf16[1,1,96,768]{3,2,0,1:T(8,128)(2,1)S(1)} %dynamic-slice_bitcast_fusion), channel_id=1, source_target_pairs={{0,4},{1,5},{2,6},{3,7},{4,0},{5,1},{6,2},{7,3},{8,12},{9,13},{10,... | collective-permute-start | bytes 442376 | tf_op jit(solution)/shard_map/ppermute | solution.py:569
  37.5 36.5 %collective-permute-start.3 = (f32[4,3,2,4608]{3,2,1,0:T(2,128)}, f32[4,3,2,4608]{3,2,1,0:T(2,128)}, u32[]{:S(2)}, u32[]{:S(2)}) collective-permute-start(f32[4,3,2,4608]{3,2,1,0:T(2,128)} %bitcast.8), channel_id=1, source_target_pairs={{0,1},{1,0},{2,3},{3,2},{4,5},{5,4},{6,7},{7,6},{8,9},{9,8},{10,11... | collective-permute-start | bytes 1327112 | tf_op jit(solution)/shard_map/ppermute | solution.py:569
  47.2 25.2 %collective-permute-start.19 = (bf16[2,1,96,768]{3,2,0,1:T(8,128)(2,1)S(1)}, bf16[2,1,96,768]{3,2,0,1:T(8,128)(2,1)S(1)}, u32[]{:S(2)}, u32[]{:S(2)}) collective-permute-start(bf16[2,1,96,768]{3,2,0,1:T(8,128)(2,1)S(1)} %pad_maximum_fusion.8), channel_id=1, source_target_pairs={{0,2},{1,3},{2,0},{3,1},{4,6},{5,7},{6,4},{7,5},{8,10},{9,11},{10,... | collective-permute-start | bytes 884744 | tf_op jit(solution)/shard_map/ppermute | solution.py:569
  53.6 23.5 %collective-permute-start.9 = (bf16[1,3,1,48,768]{4,3,1,2,0:T(8,128)(2,1)S(1)}, bf16[1,3,1,48,768]{4,3,1,2,0:T(8,128)(2,1)S(1)}, u32[]{:S(2)}, u32[]{:S(2)}) collective-permute-start(bf16[1,3,1,48,768]{4,3,1,2,0:T(8,128)(2,1)S(1)} %maximum_bitcast_fusion.2), channel_id=1, source_target_pairs={{0,8},{8,0},{16,24},{24,16},{1,9},{9,1},{17,25},{25,17},{2,10},{10... | collective-permute-start | bytes 663560 | tf_op jit(solution)/shard_map/ppermute | solution.py:569
  55.1 37.7 %collective-permute-start.11 = (bf16[1,3,1,48,768]{4,3,2,1,0:T(8,128)(2,1)S(1)}, bf16[1,3,1,48,768]{4,3,2,1,0:T(8,128)(2,1)S(1)}, u32[]{:S(2)}, u32[]{:S(2)}) collective-permute-start(bf16[1,3,1,48,768]{4,3,2,1,0:T(8,128)(2,1)S(1)} %maximum_bitcast_fusion.3), channel_id=1, source_target_pairs={{0,16},{8,24},{16,0},{24,8},{1,17},{9,25},{17,1},{25,9},{2,18},{10... | collective-permute-start | bytes 663560 | tf_op jit(solution)/shard_map/ppermute | solution.py:569
  80.5 18.1 %collective-permute-start.10 = (bf16[2,3,1,48,768]{4,3,1,2,0:T(8,128)(2,1)S(1)}, bf16[2,3,1,48,768]{4,3,1,2,0:T(8,128)(2,1)S(1)}, u32[]{:S(2)}, u32[]{:S(2)}) collective-permute-start(bf16[2,3,1,48,768]{4,3,1,2,0:T(8,128)(2,1)S(1)} %get-tuple-element.333), channel_id=1, source_target_pairs={{0,16},{8,24},{16,0},{24,8},{1,17},{9,25},{17,1},{25,9},{2,18},{10... | collective-permute-start | bytes 1327112 | tf_op jit(solution)/shard_map/ppermute | solution.py:569
  82.9 18.4 %collective-permute-start.21 = (bf16[2,3,1,48,768]{4,3,1,2,0:T(8,128)(2,1)}, bf16[2,3,1,48,768]{4,3,1,2,0:T(8,128)(2,1)}, u32[]{:S(2)}, u32[]{:S(2)}) collective-permute-start(bf16[2,3,1,48,768]{4,3,1,2,0:T(8,128)(2,1)} %get-tuple-element.328), channel_id=1, source_target_pairs={{0,16},{8,24},{16,0},{24,8},{1,17},{9,25},{17,1},{25,9},{2,18},{10... | collective-permute-start | bytes 1327112 | tf_op jit(solution)/shard_map/ppermute | solution.py:569
  93.0 28.4 %collective-permute-start.24 = (bf16[2,3,1,48,768]{4,3,1,2,0:T(8,128)(2,1)}, bf16[2,3,1,48,768]{4,3,1,2,0:T(8,128)(2,1)}, u32[]{:S(2)}, u32[]{:S(2)}) collective-permute-start(bf16[2,3,1,48,768]{4,3,1,2,0:T(8,128)(2,1)} %get-tuple-element.328), channel_id=1, source_target_pairs={{0,1},{1,0},{2,3},{3,2},{4,5},{5,4},{6,7},{7,6},{8,9},{9,8},{10,11... | collective-permute-start | bytes 1327112 | tf_op jit(solution)/shard_map/ppermute | solution.py:569
  98.5 23.4 %collective-permute-start.26 = (bf16[2,3,1,48,768]{4,3,2,1,0:T(8,128)(2,1)S(1)}, bf16[2,3,1,48,768]{4,3,2,1,0:T(8,128)(2,1)}, u32[]{:S(2)}, u32[]{:S(2)}) collective-permute-start(bf16[2,3,1,48,768]{4,3,2,1,0:T(8,128)(2,1)S(1)} %pad_maximum_fusion.6.refs_2_), channel_id=1, source_target_pairs={{0,1},{1,0},{2,3},{3,2},{4,5},{5,4},{6,7},{7,6},{8,9},{9,8},{10,11... | collective-permute-start | bytes 1327112 | tf_op jit(solution)/shard_map/ppermute | solution.py:569
  98.6 22.1 %collective-permute-start.12 = (bf16[2,3,1,48,768]{4,3,2,1,0:T(8,128)(2,1)S(1)}, bf16[2,3,1,48,768]{4,3,2,1,0:T(8,128)(2,1)S(1)}, u32[]{:S(2)}, u32[]{:S(2)}) collective-permute-start(bf16[2,3,1,48,768]{4,3,2,1,0:T(8,128)(2,1)S(1)} %pad_maximum_fusion.4.refs_2_), channel_id=1, source_target_pairs={{0,8},{8,0},{16,24},{24,16},{1,9},{9,1},{17,25},{25,17},{2,10},{10... | collective-permute-start | bytes 1327112 | tf_op jit(solution)/shard_map/ppermute | solution.py:569
  101.3 20.6 %collective-permute-start.25 = (bf16[2,3,1,48,768]{4,3,1,2,0:T(8,128)(2,1)}, bf16[2,3,1,48,768]{4,3,1,2,0:T(8,128)(2,1)}, u32[]{:S(2)}, u32[]{:S(2)}) collective-permute-start(bf16[2,3,1,48,768]{4,3,1,2,0:T(8,128)(2,1)} %collective-permute-done.21), channel_id=1, source_target_pairs={{0,1},{1,0},{2,3},{3,2},{4,5},{5,4},{6,7},{7,6},{8,9},{9,8},{10,11... | collective-permute-start | bytes 1327112 | tf_op jit(solution)/shard_map/ppermute | solution.py:569
  101.3 21.1 %collective-permute-start.27 = (bf16[2,3,1,48,768]{4,3,2,1,0:T(8,128)(2,1)}, bf16[2,3,1,48,768]{4,3,2,1,0:T(8,128)(2,1)}, u32[]{:S(2)}, u32[]{:S(2)}) collective-permute-start(bf16[2,3,1,48,768]{4,3,2,1,0:T(8,128)(2,1)} %collective-permute-done.23.refs_3_), channel_id=1, source_target_pairs={{0,1},{1,0},{2,3},{3,2},{4,5},{5,4},{6,7},{7,6},{8,9},{9,8},{10,11... | collective-permute-start | bytes 1327112 | tf_op jit(solution)/shard_map/ppermute | solution.py:569
  276.7 45.0 %collective-permute-start.31 = (bf16[8,96,768]{2,1,0:T(8,128)(2,1)}, bf16[8,96,768]{2,1,0:T(8,128)(2,1)S(1)}, u32[]{:S(2)}, u32[]{:S(2)}) collective-permute-start(bf16[8,96,768]{2,1,0:T(8,128)(2,1)} %get-tuple-element.173.refs_7_), channel_id=1, source_target_pairs={{0,8},{8,0},{16,24},{24,16},{1,9},{9,1},{17,25},{25,17},{2,10},{10... | collective-permute-start | bytes 3538952 | tf_op jit(solution)/shard_map/ppermute | solution.py:569
  278.1 43.6 %collective-permute-start.32 = (bf16[8,96,768]{2,1,0:T(8,128)(2,1)}, bf16[8,96,768]{2,1,0:T(8,128)(2,1)S(1)}, u32[]{:S(2)}, u32[]{:S(2)}) collective-permute-start(bf16[8,96,768]{2,1,0:T(8,128)(2,1)} %get-tuple-element.174.refs_8_), channel_id=1, source_target_pairs={{0,16},{8,24},{16,0},{24,8},{1,17},{9,25},{17,1},{25,9},{2,18},{10... | collective-permute-start | bytes 3538952 | tf_op jit(solution)/shard_map/ppermute | solution.py:569
  302.7 19.0 %collective-permute-start.33 = (bf16[2,24,768]{2,1,0:T(8,128)(2,1)S(1)}, bf16[2,24,768]{2,1,0:T(8,128)(2,1)S(1)}, u32[]{:S(2)}, u32[]{:S(2)}) collective-permute-start(bf16[2,24,768]{2,1,0:T(8,128)(2,1)S(1)} %copy-done.61), channel_id=1, source_target_pairs={{0,8},{8,0},{16,24},{24,16},{1,9},{9,1},{17,25},{25,17},{2,10},{10... | collective-permute-start | bytes 221192 | tf_op jit(solution)/shard_map/ppermute | solution.py:569
  328.8 32.4 %collective-permute-start.36 = (bf16[16,96,768]{2,1,0:T(8,128)(2,1)}, bf16[16,96,768]{2,1,0:T(8,128)(2,1)S(1)}, u32[]{:S(2)}, u32[]{:S(2)}) collective-permute-start(bf16[16,96,768]{2,1,0:T(8,128)(2,1)} %get-tuple-element.185.refs_10_), channel_id=1, source_target_pairs={{0,1},{1,0},{2,3},{3,2},{4,5},{5,4},{6,7},{7,6},{8,9},{9,8},{10,11... | collective-permute-start | bytes 7077896 | tf_op jit(solution)/shard_map/ppermute | solution.py:569
  328.8 32.4 %collective-permute-start.34 = (bf16[4,96,768]{2,1,0:T(8,128)(2,1)}, bf16[4,96,768]{2,1,0:T(8,128)(2,1)S(1)}, u32[]{:S(2)}, u32[]{:S(2)}) collective-permute-start(bf16[4,96,768]{2,1,0:T(8,128)(2,1)} %get-tuple-element.183.refs_8_), channel_id=1, source_target_pairs={{0,16},{8,24},{16,0},{24,8},{1,17},{9,25},{17,1},{25,9},{2,18},{10... | collective-permute-start | bytes 1769480 | tf_op jit(solution)/shard_map/ppermute | solution.py:569
  330.1 31.1 %collective-permute-start.35 = (bf16[4,96,768]{2,1,0:T(8,128)(2,1)}, bf16[4,96,768]{2,1,0:T(8,128)(2,1)S(1)}, u32[]{:S(2)}, u32[]{:S(2)}) collective-permute-start(bf16[4,96,768]{2,1,0:T(8,128)(2,1)} %get-tuple-element.184.refs_9_), channel_id=1, source_target_pairs={{0,8},{8,0},{16,24},{24,16},{1,9},{9,1},{17,25},{25,17},{2,10},{10... | collective-permute-start | bytes 1769480 | tf_op jit(solution)/shard_map/ppermute | solution.py:569
  370.8 40.1 %collective-permute-start.41 = (bf16[16,96,768]{2,1,0:T(8,128)(2,1)}, bf16[16,96,768]{2,1,0:T(8,128)(2,1)}, u32[]{:S(2)}, u32[]{:S(2)}) collective-permute-start(bf16[16,96,768]{2,1,0:T(8,128)(2,1)} %get-tuple-element.197.refs_11_), channel_id=1, source_target_pairs={{0,1},{1,0},{2,3},{3,2},{4,5},{5,4},{6,7},{7,6},{8,9},{9,8},{10,11... | collective-permute-start | bytes 7077896 | tf_op jit(solution)/shard_map/ppermute | solution.py:569
  370.8 40.1 %collective-permute-start.42 = (bf16[16,96,768]{2,1,0:T(8,128)(2,1)}, bf16[16,96,768]{2,1,0:T(8,128)(2,1)}, u32[]{:S(2)}, u32[]{:S(2)}) collective-permute-start(bf16[16,96,768]{2,1,0:T(8,128)(2,1)} %get-tuple-element.198.refs_12_), channel_id=1, source_target_pairs={{0,1},{1,0},{2,3},{3,2},{4,5},{5,4},{6,7},{7,6},{8,9},{9,8},{10,11... | collective-permute-start | bytes 7077896 | tf_op jit(solution)/shard_map/ppermute | solution.py:569
  373.2 29.0 %collective-permute-start.37 = (bf16[2,96,768]{2,1,0:T(8,128)(2,1)}, bf16[2,96,768]{2,1,0:T(8,128)(2,1)S(1)}, u32[]{:S(2)}, u32[]{:S(2)}) collective-permute-start(bf16[2,96,768]{2,1,0:T(8,128)(2,1)} %get-tuple-element.193.refs_7_), channel_id=1, source_target_pairs={{0,2},{1,3},{2,0},{3,1},{4,6},{5,7},{6,4},{7,5},{8,10},{9,11},{10,... | collective-permute-start | bytes 884744 | tf_op jit(solution)/shard_map/ppermute | solution.py:569
  375.7 35.1 %collective-permute-start.39 = (bf16[4,96,768]{2,1,0:T(8,128)(2,1)}, bf16[4,96,768]{2,1,0:T(8,128)(2,1)S(1)}, u32[]{:S(2)}, u32[]{:S(2)}) collective-permute-start(bf16[4,96,768]{2,1,0:T(8,128)(2,1)} %get-tuple-element.195.refs_9_), channel_id=1, source_target_pairs={{0,8},{8,0},{16,24},{24,16},{1,9},{9,1},{17,25},{25,17},{2,10},{10... | collective-permute-start | bytes 1769480 | tf_op jit(solution)/shard_map/ppermute | solution.py:569
  377.4 33.4 %collective-permute-start.40 = (bf16[4,96,768]{2,1,0:T(8,128)(2,1)}, bf16[4,96,768]{2,1,0:T(8,128)(2,1)S(1)}, u32[]{:S(2)}, u32[]{:S(2)}) collective-permute-start(bf16[4,96,768]{2,1,0:T(8,128)(2,1)} %get-tuple-element.196.refs_10_), channel_id=1, source_target_pairs={{0,16},{8,24},{16,0},{24,8},{1,17},{9,25},{17,1},{25,9},{2,18},{10... | collective-permute-start | bytes 1769480 | tf_op jit(solution)/shard_map/ppermute | solution.py:569
  437.4 38.4 %collective-permute-start.49 = (bf16[16,96,768]{2,1,0:T(8,128)(2,1)}, bf16[16,96,768]{2,1,0:T(8,128)(2,1)S(1)}, u32[]{:S(2)}, u32[]{:S(2)}) collective-permute-start(bf16[16,96,768]{2,1,0:T(8,128)(2,1)} %bitcast.194), channel_id=1, source_target_pairs={{0,1},{1,0},{2,3},{3,2},{4,5},{5,4},{6,7},{7,6},{8,9},{9,8},{10,11... | collective-permute-start | bytes 7077896 | tf_op jit(solution)/shard_map/ppermute | solution.py:569
  437.6 38.1 %collective-permute-start.47 = (bf16[8,96,768]{2,1,0:T(8,128)(2,1)}, bf16[8,96,768]{2,1,0:T(8,128)(2,1)S(1)}, u32[]{:S(2)}, u32[]{:S(2)}) collective-permute-start(bf16[8,96,768]{2,1,0:T(8,128)(2,1)} %get-tuple-element.217.refs_12_), channel_id=1, source_target_pairs={{0,8},{8,0},{16,24},{24,16},{1,9},{9,1},{17,25},{25,17},{2,10},{10... | collective-permute-start | bytes 3538952 | tf_op jit(solution)/shard_map/ppermute | solution.py:569
  438.4 37.4 %collective-permute-start.48 = (bf16[8,96,768]{2,1,0:T(8,128)(2,1)}, bf16[8,96,768]{2,1,0:T(8,128)(2,1)S(1)}, u32[]{:S(2)}, u32[]{:S(2)}) collective-permute-start(bf16[8,96,768]{2,1,0:T(8,128)(2,1)} %get-tuple-element.218.refs_13_), channel_id=1, source_target_pairs={{0,16},{8,24},{16,0},{24,8},{1,17},{9,25},{17,1},{25,9},{2,18},{10... | collective-permute-start | bytes 3538952 | tf_op jit(solution)/shard_map/ppermute | solution.py:569
  485.3 28.5 %collective-permute-start.54 = (bf16[4,96,768]{2,1,0:T(8,128)(2,1)}, bf16[4,96,768]{2,1,0:T(8,128)(2,1)S(1)}, u32[]{:S(2)}, u32[]{:S(2)}) collective-permute-start(bf16[4,96,768]{2,1,0:T(8,128)(2,1)} %get-tuple-element.239), channel_id=1, source_target_pairs={{0,16},{8,24},{16,0},{24,8},{1,17},{9,25},{17,1},{25,9},{2,18},{10... | collective-permute-start | bytes 1769480 | tf_op jit(solution)/shard_map/ppermute | solution.py:569
  486.0 27.9 %collective-permute-start.55 = (bf16[4,96,768]{2,1,0:T(8,128)(2,1)}, bf16[4,96,768]{2,1,0:T(8,128)(2,1)S(1)}, u32[]{:S(2)}, u32[]{:S(2)}) collective-permute-start(bf16[4,96,768]{2,1,0:T(8,128)(2,1)} %get-tuple-element.241), channel_id=1, source_target_pairs={{0,8},{8,0},{16,24},{24,16},{1,9},{9,1},{17,25},{25,17},{2,10},{10... | collective-permute-start | bytes 1769480 | tf_op jit(solution)/shard_map/ppermute | solution.py:569
  487.3 26.6 %collective-permute-start.56 = (bf16[4,96,768]{2,1,0:T(8,128)(2,1)}, bf16[4,96,768]{2,1,0:T(8,128)(2,1)S(1)}, u32[]{:S(2)}, u32[]{:S(2)}) collective-permute-start(bf16[4,96,768]{2,1,0:T(8,128)(2,1)} %get-tuple-element.243), channel_id=1, source_target_pairs={{0,8},{8,0},{16,24},{24,16},{1,9},{9,1},{17,25},{25,17},{2,10},{10... | collective-permute-start | bytes 1769480 | tf_op jit(solution)/shard_map/ppermute | solution.py:569
  488.0 25.9 %collective-permute-start.57 = (bf16[4,96,768]{2,1,0:T(8,128)(2,1)}, bf16[4,96,768]{2,1,0:T(8,128)(2,1)S(1)}, u32[]{:S(2)}, u32[]{:S(2)}) collective-permute-start(bf16[4,96,768]{2,1,0:T(8,128)(2,1)} %get-tuple-element.245), channel_id=1, source_target_pairs={{0,16},{8,24},{16,0},{24,8},{1,17},{9,25},{17,1},{25,9},{2,18},{10... | collective-permute-start | bytes 1769480 | tf_op jit(solution)/shard_map/ppermute | solution.py:569
  521.8 16.6 %collective-permute-start.61 = (bf16[2,96,768]{2,1,0:T(8,128)(2,1)}, bf16[2,96,768]{2,1,0:T(8,128)(2,1)S(1)}, u32[]{:S(2)}, u32[]{:S(2)}) collective-permute-start(bf16[2,96,768]{2,1,0:T(8,128)(2,1)} %get-tuple-element.251), channel_id=1, source_target_pairs={{0,2},{1,3},{2,0},{3,1},{4,6},{5,7},{6,4},{7,5},{8,10},{9,11},{10,... | collective-permute-start | bytes 884744 | tf_op jit(solution)/shard_map/ppermute | solution.py:569
  521.8 18.7 %collective-permute-start.62 = (bf16[2,96,768]{2,1,0:T(8,128)(2,1)}, bf16[2,96,768]{2,1,0:T(8,128)(2,1)S(1)}, u32[]{:S(2)}, u32[]{:S(2)}) collective-permute-start(bf16[2,96,768]{2,1,0:T(8,128)(2,1)} %get-tuple-element.253), channel_id=1, source_target_pairs={{0,2},{1,3},{2,0},{3,1},{4,6},{5,7},{6,4},{7,5},{8,10},{9,11},{10,... | collective-permute-start | bytes 884744 | tf_op jit(solution)/shard_map/ppermute | solution.py:569
  523.8 16.7 %collective-permute-start.63 = (bf16[2,96,768]{2,1,0:T(8,128)(2,1)}, bf16[2,96,768]{2,1,0:T(8,128)(2,1)S(1)}, u32[]{:S(2)}, u32[]{:S(2)}) collective-permute-start(bf16[2,96,768]{2,1,0:T(8,128)(2,1)} %get-tuple-element.255), channel_id=1, source_target_pairs={{0,16},{8,24},{16,0},{24,8},{1,17},{9,25},{17,1},{25,9},{2,18},{10... | collective-permute-start | bytes 884744 | tf_op jit(solution)/shard_map/ppermute | solution.py:569
  524.5 16.1 %collective-permute-start.64 = (bf16[2,96,768]{2,1,0:T(8,128)(2,1)}, bf16[2,96,768]{2,1,0:T(8,128)(2,1)S(1)}, u32[]{:S(2)}, u32[]{:S(2)}) collective-permute-start(bf16[2,96,768]{2,1,0:T(8,128)(2,1)} %get-tuple-element.257), channel_id=1, source_target_pairs={{0,8},{8,0},{16,24},{24,16},{1,9},{9,1},{17,25},{25,17},{2,10},{10... | collective-permute-start | bytes 884744 | tf_op jit(solution)/shard_map/ppermute | solution.py:569
  547.2 16.7 %collective-permute-start.67 = (bf16[1,96,768]{2,1,0:T(8,128)(2,1)}, bf16[1,96,768]{2,1,0:T(8,128)(2,1)S(1)}, u32[]{:S(2)}, u32[]{:S(2)}) collective-permute-start(bf16[1,96,768]{2,1,0:T(8,128)(2,1)} %get-tuple-element.261), channel_id=1, source_target_pairs={{0,4},{1,5},{2,6},{3,7},{4,0},{5,1},{6,2},{7,3},{8,12},{9,13},{10,... | collective-permute-start | bytes 442376 | tf_op jit(solution)/shard_map/ppermute | solution.py:569
  562.2 49.7 %collective-permute-start.85 = (bf16[2,96,768]{2,1,0:T(8,128)(2,1)}, bf16[2,96,768]{2,1,0:T(8,128)(2,1)}, u32[]{:S(2)}, u32[]{:S(2)}) collective-permute-start(bf16[2,96,768]{2,1,0:T(8,128)(2,1)} %get-tuple-element.277.refs_12_), channel_id=1, source_target_pairs={{0,8},{8,0},{16,24},{24,16},{1,9},{9,1},{17,25},{25,17},{2,10},{10... | collective-permute-start | bytes 884744 | tf_op jit(solution)/shard_map/ppermute | solution.py:569
  563.9 49.1 %collective-permute-start.86 = (bf16[2,96,768]{2,1,0:T(8,128)(2,1)}, bf16[2,96,768]{2,1,0:T(8,128)(2,1)}, u32[]{:S(2)}, u32[]{:S(2)}) collective-permute-start(bf16[2,96,768]{2,1,0:T(8,128)(2,1)} %get-tuple-element.277.refs_12_), channel_id=1, source_target_pairs={{0,16},{8,24},{16,0},{24,8},{1,17},{9,25},{17,1},{25,9},{2,18},{10... | collective-permute-start | bytes 884744 | tf_op jit(solution)/shard_map/ppermute | solution.py:569
  570.4 19.9 %collective-permute-start.75 = (bf16[16,6,4608]{2,0,1:T(8,128)(2,1)}, bf16[16,6,4608]{2,0,1:T(8,128)(2,1)}, u32[]{:S(2)}, u32[]{:S(2)}) collective-permute-start(bf16[16,6,4608]{2,0,1:T(8,128)(2,1)} %copy.72), channel_id=1, source_target_pairs={{0,8},{8,0},{16,24},{24,16},{1,9},{9,1},{17,25},{25,17},{2,10},{10... | collective-permute-start | bytes 2654216 | tf_op jit(solution)/shard_map/ppermute | solution.py:569
  573.4 24.1 %collective-permute-start.73 = (bf16[1,96,768]{2,1,0:T(8,128)(2,1)}, bf16[1,96,768]{2,1,0:T(8,128)(2,1)S(1)}, u32[]{:S(2)}, u32[]{:S(2)}) collective-permute-start(bf16[1,96,768]{2,1,0:T(8,128)(2,1)} %get-tuple-element.271), channel_id=1, source_target_pairs={{0,4},{1,5},{2,6},{3,7},{4,0},{5,1},{6,2},{7,3},{8,12},{9,13},{10,... | collective-permute-start | bytes 442376 | tf_op jit(solution)/shard_map/ppermute | solution.py:569
  575.1 20.7 %collective-permute-start.74 = (f32[2,8,768]{2,1,0:T(8,128)}, f32[2,8,768]{2,1,0:T(8,128)S(1)}, u32[]{:S(2)}, u32[]{:S(2)}) collective-permute-start(f32[2,8,768]{2,1,0:T(8,128)} %get-tuple-element.272.refs_2_), channel_id=1, source_target_pairs={{0,8},{8,0},{16,24},{24,16},{1,9},{9,1},{17,25},{25,17},{2,10},{10... | collective-permute-start | bytes 147464 | tf_op jit(solution)/shard_map/ppermute | solution.py:569
  590.3 22.7 %collective-permute-start.87 = (bf16[2,96,768]{2,1,0:T(8,128)(2,1)}, bf16[2,96,768]{2,1,0:T(8,128)(2,1)S(1)}, u32[]{:S(2)}, u32[]{:S(2)}) collective-permute-start(bf16[2,96,768]{2,1,0:T(8,128)(2,1)} %get-tuple-element.277.refs_12_), channel_id=1, source_target_pairs={{0,24},{8,16},{16,8},{24,0},{1,25},{9,17},{17,9},{25,1},{2,26},{10... | collective-permute-start | bytes 884744 | tf_op jit(solution)/shard_map/ppermute | solution.py:569
  595.8 18.4 %collective-permute-start.88 = (f32[3,96]{1,0:T(4,128)}, f32[3,96]{1,0:T(4,128)S(1)}, u32[]{:S(2)}, u32[]{:S(2)}) collective-permute-start(f32[3,96]{1,0:T(4,128)} %get-tuple-element.358), channel_id=1, source_target_pairs={{0,4},{1,5},{2,6},{3,7},{4,0},{5,1},{6,2},{7,3},{8,12},{9,13},{10,... | collective-permute-start | bytes 3464 | tf_op jit(solution)/shard_map/ppermute | solution.py:569
  597.5 20.4 %collective-permute-start.89 = (f32[3,96]{1,0:T(4,128)}, f32[3,96]{1,0:T(4,128)S(1)}, u32[]{:S(2)}, u32[]{:S(2)}) collective-permute-start(f32[3,96]{1,0:T(4,128)} %get-tuple-element.357), channel_id=1, source_target_pairs={{0,2},{1,3},{2,0},{3,1},{4,6},{5,7},{6,4},{7,5},{8,10},{9,11},{10,... | collective-permute-start | bytes 3464 | tf_op jit(solution)/shard_map/ppermute | solution.py:569
  626.4 16.5 %collective-permute-start.80 = (bf16[2,96,768]{2,1,0:T(8,128)(2,1)S(1)}, bf16[2,96,768]{2,1,0:T(8,128)(2,1)S(1)}, u32[]{:S(2)}, u32[]{:S(2)}) collective-permute-start(bf16[2,96,768]{2,1,0:T(8,128)(2,1)S(1)} %copy-done.33), channel_id=1, source_target_pairs={{0,16},{8,24},{16,0},{24,8},{1,17},{9,25},{17,1},{25,9},{2,18},{10... | collective-permute-start | bytes 884744 | tf_op jit(solution)/shard_map/ppermute | solution.py:569
  626.8 16.2 %collective-permute-start.81 = (bf16[2,96,768]{2,1,0:T(8,128)(2,1)S(1)}, bf16[2,96,768]{2,1,0:T(8,128)(2,1)S(1)}, u32[]{:S(2)}, u32[]{:S(2)}) collective-permute-start(bf16[2,96,768]{2,1,0:T(8,128)(2,1)S(1)} %copy-done.33), channel_id=1, source_target_pairs={{0,24},{8,16},{16,8},{24,0},{1,25},{9,17},{17,9},{25,1},{2,26},{10... | collective-permute-start | bytes 884744 | tf_op jit(solution)/shard_map/ppermute | solution.py:569
  (142 other events, 1310.5 us)
Sparse Core Ops, SparseCore 0:
  11.6 152.8 all-gather.1
